TPU v7x, 512 devices: a whole 4x4x16 slice. The times are simulated.
512 devices in a mesh: wide: 32 (over x, z_hi, core), narrow: 16 (over z_lo, y).
Axes of the slice: x: 4, y: 4, z: 16 (z_hi: 4, z_lo: 4; z = z_hi * 4 + z_lo), core: 2. Of those that a mesh axis runs over, the one named last changes fastest.
Arguments:
- chaos_field: float32 [64, 4, 256, 455], P('wide', None, 'narrow'), may hold values from -2.4 to 2.4
- mean_conductivity: float32 [64, 4, 256], P('wide', None, 'narrow'), may hold values from 0.5 to 2
- kl_fields: float32 [12, 64, 4, 256], P(None, 'wide', None, 'narrow'), may hold values from -1.5 to 1.5
- pairs: int32 [12, 91, 3], replicated, may hold values from 0 to 454, as said below
Outputs:
- applied: float32 [64, 4, 256, 455], P('wide', None, 'narrow')
Inputs may be any that keep to these rules, and one draw needn't show every extreme that they name: `pairs`: the first two entries of each row are mode numbers; each random variable's rows name each mode of total degree below 3 once as lower and the mode raised by one in that variable as raised; the third entry is that degree, 1 to 3. The modes are numbered in an order drawn from the seed.
All inputs are finite; a program needn't handle non-finite values.
Results may differ from a plain program's by a relative error of at most 0.0001.
Values sent between devices are 32-bit elements; how exact they have to be, the bound alone decides.
No kernel may reach another device: no remote copies, remote signals or barrier semaphores. Data moves between devices by JAX's collectives and lax.ppermute only.
A program may use at most 64 MiB of HBM per device.

v0:
```python
import jax
import jax.numpy as jnp
from jax import lax
from jax.sharding import PartitionSpec as P


def from_behind(block, axis, distance):
    devices = range(lax.axis_size(axis))
    route = [(i - distance, i) for i in devices if i - distance in devices]
    return lax.ppermute(block, axis, route)


def build_tables(pairs, modes_total):
    lower_index = pairs[:, :, 0].reshape(-1)
    upper_index = pairs[:, :, 1].reshape(-1)
    scaling = jnp.sqrt(pairs[:, :, 2].reshape(-1).astype(jnp.float32))
    numbers = jnp.arange(modes_total, dtype=jnp.int32)[:, None]
    upper_hot = (numbers == upper_index[None, :]).astype(jnp.float32)
    lower_hot = (numbers == lower_index[None, :]).astype(jnp.float32)
    pick = jnp.concatenate([upper_hot, lower_hot], axis=1)
    place = jnp.concatenate([lower_hot, upper_hot], axis=1).T
    return (pick, place, scaling)


def gather_pairs(pieces, pick):
    modes_total = pick.shape[0]
    width = pick.shape[1]
    flat = jnp.concatenate([piece.reshape(-1, modes_total) for piece in pieces], axis=0)
    product = jnp.dot(
        flat, pick, precision=lax.Precision.HIGHEST, preferred_element_type=jnp.float32
    )
    results = []
    offset = 0
    for piece in pieces:
        count = piece.size // modes_total
        results.append(product[offset : offset + count].reshape(piece.shape[:-1] + (width,)))
        offset = offset + count
    return results


def couple_weights(kl_face, scaling):
    kl_last = jnp.moveaxis(kl_face, 0, -1)
    variables = kl_last.shape[-1]
    weights = jnp.repeat(kl_last, scaling.shape[0] // variables, axis=-1) * scaling
    return jnp.concatenate([weights, weights], axis=-1)


def ahead(values, direction, incoming):
    size = values.shape[direction]
    kept = lax.slice_in_dim(values, 1, size, axis=direction)
    return jnp.concatenate([kept, incoming], axis=direction)


def per_device(chaos_field, mean_conductivity, kl_fields, pairs):
    modes_total = chaos_field.shape[3]
    pick, place, scaling = build_tables(pairs, modes_total)
    coefficients = jnp.concatenate([mean_conductivity[None], kl_fields], axis=0)
    zero_z = jnp.zeros_like(chaos_field[:, 0:1])
    extra = []
    row_field, coef_row = from_behind((chaos_field[0:1], coefficients[:, 0:1]), "wide", -1)
    plane_field, coef_plane = from_behind(
        (chaos_field[:, :, 0:1], coefficients[:, :, :, 0:1]), "narrow", -1
    )
    differences = (
        chaos_field - ahead(chaos_field, 0, row_field),
        chaos_field - ahead(chaos_field, 1, zero_z),
        chaos_field - ahead(chaos_field, 2, plane_field),
    )
    gathered_all = gather_pairs([chaos_field, row_field, plane_field] + extra, pick)
    own = gathered_all[0]
    coupled_diffs = (
        own - ahead(own, 0, gathered_all[1]),
        own - ahead(own, 1, jnp.zeros_like(own[:, 0:1])),
        own - ahead(own, 2, gathered_all[2]),
    )
    faces = (
        0.5 * (coefficients + ahead(coefficients, 1, coef_row)),
        0.5 * (coefficients + ahead(coefficients, 2, jnp.zeros_like(coefficients[:, :, 0:1]))),
        0.5 * (coefficients + ahead(coefficients, 3, coef_plane)),
    )
    center_sum = jnp.zeros_like(chaos_field)
    coupled_sum = jnp.zeros(chaos_field.shape[:-1] + (pick.shape[1],), jnp.float32)
    for direction in range(3):
        face_coef = faces[direction]
        center_flux = face_coef[0][..., None] * differences[direction]
        coupled = coupled_diffs[direction] * couple_weights(face_coef[1:], scaling)
        if direction == 0:
            in_center, in_coupled = from_behind((center_flux[-1:], coupled[-1:]), "wide", 1)
            prev_center = jnp.concatenate([in_center, center_flux[:-1]], axis=0)
            prev_coupled = jnp.concatenate([in_coupled, coupled[:-1]], axis=0)
        elif direction == 1:
            prev_center = jnp.concatenate(
                [jnp.zeros_like(center_flux[:, 0:1]), center_flux[:, :-1]], axis=1
            )
            prev_coupled = jnp.concatenate(
                [jnp.zeros_like(coupled[:, 0:1]), coupled[:, :-1]], axis=1
            )
        else:
            in_center, in_coupled = from_behind(
                (center_flux[:, :, -1:], coupled[:, :, -1:]), "narrow", 1
            )
            prev_center = jnp.concatenate([in_center, center_flux[:, :, :-1]], axis=2)
            prev_coupled = jnp.concatenate([in_coupled, coupled[:, :, :-1]], axis=2)
        center_sum = center_sum + center_flux - prev_center
        coupled_sum = coupled_sum + coupled - prev_coupled
    spread = jnp.dot(
        coupled_sum.reshape(-1, pick.shape[1]),
        place,
        precision=lax.Precision.HIGHEST,
        preferred_element_type=jnp.float32,
    )
    return center_sum + spread.reshape(chaos_field.shape)


def solution(mesh):
    placed = (
        P("wide", None, "narrow", None),
        P("wide", None, "narrow"),
        P(None, "wide", None, "narrow"),
        P(),
    )
    return jax.shard_map(
        per_device,
        mesh=mesh,
        in_specs=placed,
        out_specs=P("wide", None, "narrow", None),
        check_vma=False,
    )
```

profile of v0, /device:TPU:62, one launch (start us, length us, event | category | flops | bytes accessed | tf_op | source)
XLA Modules:
  0.0 108.9 jit_solution(5106576367192599257)
XLA Ops:
  0.0 0.8 fusion.39
  0.8 11.5 %collective-permute-start = (f32[13,1,4,16]{3,2,1,0:T(4,128)S(1)}, f32[13,1,4,16]{3,2,1,0:T(4,128)S(1)}, u32[]{:S(2)}, u32[]{:S(2)}) collective-permute-start(f32[13,1,4,16]{3,2,1,0:T(4,128)S(1)} %get-tuple-element.25), channel_id=1, source_target_pairs={{16,0},{32,16},{48,32},{64,48},{80,64},{96,80},{112,96},{128,112},... | collective-permute-start | bytes 9992 | tf_op jit(solution)/shard_map/ppermute | solution.py:10
  12.3 0.8 fusion.36
  13.2 2.7 %collective-permute-start.3 = (f32[13,2,4,1]{3,2,1,0:T(4,128)S(1)}, f32[13,2,4,1]{3,2,1,0:T(4,128)S(1)}, u32[]{:S(2)}, u32[]{:S(2)}) collective-permute-start(f32[13,2,4,1]{3,2,1,0:T(4,128)S(1)} %fusion.36), channel_id=1, source_target_pairs={{1,0},{2,1},{3,2},{4,3},{5,4},{6,5},{7,6},{8,7},{9,8},{10,9},{11,1... | collective-permute-start | bytes 1256 | tf_op jit(solution)/shard_map/ppermute | solution.py:10
  15.8 1.7 %fusion.49 = (f32[1,4,16,455]{3,2,1,0:T(8,128)}, f32[1,4,16,455]{3,2,1,0:T(8,128)}) fusion(f32[2,4,16,455]{3,2,1,0:T(8,128)} %param.4), kind=kLoop, calls=%fused_computation.80 | loop fusion | bytes 465920 | tf_op jit(solution)/shard_map/slice | solution.py:50
  17.5 2.3 %collective-permute-start.1 = (f32[1,4,16,455]{3,2,1,0:T(8,128)}, f32[1,4,16,455]{3,2,1,0:T(8,128)S(1)}, u32[]{:S(2)}, u32[]{:S(2)}) collective-permute-start(f32[1,4,16,455]{3,2,1,0:T(8,128)} %get-tuple-element.20), channel_id=1, source_target_pairs={{16,0},{32,16},{48,32},{64,48},{80,64},{96,80},{112,96},{128,112},... | collective-permute-start | bytes 349448 | tf_op jit(solution)/shard_map/ppermute | solution.py:10
  19.8 1.5 %slice.124 = f32[2,4,1,455]{3,2,1,0:T(1,128)} slice(f32[2,4,16,455]{3,2,1,0:T(8,128)} %param.4), slice={[0:2], [0:4], [0:1], [0:455]} | slice | bytes 29120 | tf_op jit(solution)/shard_map/slice | solution.py:62
  21.3 2.3 %collective-permute-start.4 = (f32[2,4,1,455]{3,2,1,0:T(1,128)}, f32[2,4,1,455]{3,2,1,0:T(1,128)}, u32[]{:S(2)}, u32[]{:S(2)}) collective-permute-start(f32[2,4,1,455]{3,2,1,0:T(1,128)} %slice.124), channel_id=1, source_target_pairs={{1,0},{2,1},{3,2},{4,3},{5,4},{6,5},{7,6},{8,7},{9,8},{10,9},{11,1... | collective-permute-start | bytes 43688 | tf_op jit(solution)/shard_map/ppermute | solution.py:10
  23.7 0.8 fusion.34
  24.5 0.8 sqrt_reduce_fusion
  25.3 0.9 slice_reduce_fusion
  26.2 0.1 eq.31
  26.2 0.1 eq.35
  26.3 0.0 copy-start.2
  26.3 0.0 copy-start.8
  26.4 0.0 copy-start.1
  26.4 1.6 %fusion.7 = (f32[455,1092]{1,0:T(8,128)S(1)}, f32[455,1092]{1,0:T(8,128)}) fusion(s32[1092]{0:T(1024)S(1)} %eq.31, s32[1092]{0:T(1024)S(1)} %eq.35), kind=kLoop, calls=%fused_computation.10 | loop fusion | flops 1987440 | bytes 3983616 | tf_op jit(solution)/shard_map/convert_element_type | solution.py:18
  28.0 0.1 fusion.35
  28.1 0.7 slice.123
  28.8 0.7 slice.118
  29.5 0.1 sqrt.11
  29.6 0.0 collective-permute-done.3
  29.6 0.0 collective-permute-done
  29.6 0.7 fusion.37
  30.3 0.6 slice_bitcast_fusion
  30.9 0.6 slice_bitcast_fusion.3
  31.5 0.8 copy.10
  32.3 1.2 %broadcast_in_dim.19 = f32[2,4,16,12,91]{4,3,2,1,0:T(8,128)S(1)} broadcast(f32[2,4,16,12]{3,2,1,0:T(8,128)} %copy.10), dimensions={0,1,2,3} | broadcast | bytes 565248 | tf_op jit(solution)/shard_map/broadcast_in_dim | solution.py:44
  33.4 1.2 %reshape.51 = f32[2,4,16,1092]{3,2,1,0:T(8,128)} reshape(f32[2,4,16,12,91]{4,3,2,1,0:T(8,128)S(1)} %broadcast_in_dim.19) | data formatting | bytes 1118208 | tf_op jit(solution)/shard_map/reshape | solution.py:44
  34.6 1.5 %copy.12 = f32[2,4,16,12]{3,2,1,0:T(8,128)} copy(f32[2,4,16,12]{2,1,0,3:T(4,128)} %get-tuple-element.29) | data formatting | bytes 12288 | tf_op jit(solution)/shard_map/transpose | solution.py:42
  36.2 1.2 %broadcast_in_dim.20 = f32[2,4,16,12,91]{4,3,2,1,0:T(8,128)S(1)} broadcast(f32[2,4,16,12]{3,2,1,0:T(8,128)} %copy.12), dimensions={0,1,2,3} | broadcast | bytes 565248 | tf_op jit(solution)/shard_map/broadcast_in_dim | solution.py:44
  37.3 1.2 %reshape.53 = f32[2,4,16,1092]{3,2,1,0:T(8,128)} reshape(f32[2,4,16,12,91]{4,3,2,1,0:T(8,128)S(1)} %broadcast_in_dim.20) | data formatting | bytes 1118208 | tf_op jit(solution)/shard_map/reshape | solution.py:44
  38.5 0.8 slice_bitcast_fusion.2
  39.3 0.8 copy.9
  40.1 1.2 %broadcast_in_dim.18 = f32[2,4,16,12,91]{4,3,2,1,0:T(8,128)S(1)} broadcast(f32[2,4,16,12]{3,2,1,0:T(8,128)} %copy.9), dimensions={0,1,2,3} | broadcast | bytes 565248 | tf_op jit(solution)/shard_map/broadcast_in_dim | solution.py:44
  41.3 1.2 %reshape.50 = f32[2,4,16,1092]{3,2,1,0:T(8,128)} reshape(f32[2,4,16,12,91]{4,3,2,1,0:T(8,128)S(1)} %broadcast_in_dim.18) | data formatting | bytes 1118208 | tf_op jit(solution)/shard_map/reshape | solution.py:44
  42.5 2.7 %broadcast_multiply_fusion.2 = (f32[2,4,16,1092]{3,2,1,0:T(8,128)}, f32[2,4,16,1092]{3,2,1,0:T(8,128)}, f32[2,4,16,1092]{3,2,1,0:T(8,128)}) fusion(f32[2,4,16,1092]{3,2,1,0:T(8,128)} %reshape.50, f32[1092]{0:T(1024)S(1)} %sqrt.11, f32[2,4,16,1092]{3,2,1,0:T(8,128)} %reshape.51, f32[2,4,16,1092]{3,2,1,0:T(8,128)} %reshape.53), kind=kLoop, calls=%fused_computation.35 | loop fusion | flops 419328 | bytes 3358992 | tf_op jit(solution)/shard_map/mul | solution.py:44
  45.2 0.7 slice_bitcast_fusion.5
  45.9 0.0 collective-permute-done.4
  45.9 0.8 reduce
  46.6 0.0 collective-permute-done.1
  46.7 0.6 copy-done.5
  47.3 5.1 %fusion = f32[200,2184]{1,0:T(8,128)S(1)} fusion(f32[455,1092]{1,0:T(8,128)} %get-tuple-element.34, f32[455,1092]{1,0:T(8,128)S(1)} %get-tuple-element.33, f32[8,455]{1,0:T(8,128)S(1)} %reshape.47, f32[64,455]{1,0:T(8,128)S(1)} %bitcast.35, f32[128,455]{1,0:T(8,128)S(1)} %bitcast.31), kind=kOutput, calls=%fused_computation | convolution fusion | flops 2386103808 | bytes 6086080 | tf_op jit(solution)/shard_map/dot_general | solution.py:29
  52.4 0.1 slice.163
  52.5 1.1 %slice.172 = f32[2,4,15,2184]{3,2,1,0:T(8,128)} slice(f32[2,4,16,2184]{3,2,1,0:T(8,128)S(1)} %bitcast.27), slice={[0:2], [0:4], [1:16], [0:2184]} | slice | bytes 2096640 | tf_op jit(solution)/shard_map/slice | solution.py:50
  53.6 1.0 slice.169
  54.6 1.1 %fusion.46 = (f32[64,2184]{1,0:T(8,128)}, f32[64,2184]{1,0:T(8,128)}) fusion(f32[200,2184]{1,0:T(8,128)S(1)} %fusion), kind=kLoop, calls=%fused_computation.77 | loop fusion | bytes 2236416 | tf_op jit(solution)/shard_map/slice | solution.py:50
  55.7 0.6 slice.173
  56.4 1.6 %reshape.55 = f32[2,4,1,2184]{3,2,1,0:T(1,128)} reshape(f32[8,2184]{1,0:T(8,128)} %slice.173) | data formatting | bytes 139776 | tf_op jit(solution)/shard_map/reshape | solution.py:36
  58.0 3.8 %fusion.9 = (f32[2,4,16,2184]{3,2,1,0:T(8,128)S(1)}, f32[2,4,16,2184]{3,2,1,0:T(8,128)S(1)}, f32[2,4,16,2184]{3,2,1,0:T(8,128)S(1)}) fusion(f32[2,4,16,2184]{3,2,1,0:T(8,128)S(1)} %bitcast.29, f32[1,4,16,2184]{3,2,1,0:T(8,128)} %bitcast.34, f32[1,4,16,2184]{3,2,1,0:T(8,128)} %bitcast.33, f32[2,4,16,1092]{3,2,1,0:T(8,128)} %get-tuple-element.26, ...), kind=kLoop, calls=%fused_computation.13 | loop fusion | flops 3075072 | bytes 9225216 | tf_op jit(solution)/shard_map/mul | solution.py:86
  61.8 0.0 copy-start.3
  61.8 0.1 fusion.47
  61.9 2.1 %collective-permute-start.6 = (f32[1,4,16,2184]{3,2,1,0:T(8,128)S(1)}, f32[1,4,16,2184]{3,2,1,0:T(8,128)S(1)}, u32[]{:S(2)}, u32[]{:S(2)}) collective-permute-start(f32[1,4,16,2184]{3,2,1,0:T(8,128)S(1)} %get-tuple-element.9), channel_id=1, source_target_pairs={{0,16},{16,32},{32,48},{48,64},{64,80},{80,96},{96,112},{112,128},... | collective-permute-start | bytes 1677320 | tf_op jit(solution)/shard_map/ppermute | solution.py:10
  64.0 0.9 fusion.27
  64.9 2.1 %collective-permute-start.2 = (f32[1,4,16,455]{3,2,1,0:T(8,128)S(1)}, f32[1,4,16,455]{3,2,1,0:T(8,128)S(1)}, u32[]{:S(2)}, u32[]{:S(2)}) collective-permute-start(f32[1,4,16,455]{3,2,1,0:T(8,128)S(1)} %get-tuple-element.14), channel_id=1, source_target_pairs={{0,16},{16,32},{32,48},{48,64},{64,80},{80,96},{96,112},{112,128},... | collective-permute-start | bytes 349448 | tf_op jit(solution)/shard_map/ppermute | solution.py:10
  67.0 0.1 slice.175
  67.1 5.6 %collective-permute-start.7 = (f32[2,4,1,2184]{3,2,1,0:T(1,128)S(1)}, f32[2,4,1,2184]{3,2,1,0:T(1,128)S(1)}, u32[]{:S(2)}, u32[]{:S(2)}) collective-permute-start(f32[2,4,1,2184]{3,2,1,0:T(1,128)S(1)} %slice.175), channel_id=1, source_target_pairs={{0,1},{1,2},{2,3},{3,4},{4,5},{5,6},{6,7},{7,8},{8,9},{9,10},{10,1... | collective-permute-start | bytes 209672 | tf_op jit(solution)/shard_map/ppermute | solution.py:10
  72.7 3.4 %collective-permute-start.5 = (f32[2,4,1,455]{3,2,1,0:T(1,128)S(1)}, f32[2,4,1,455]{3,2,1,0:T(1,128)S(1)}, u32[]{:S(2)}, u32[]{:S(2)}) collective-permute-start(f32[2,4,1,455]{3,2,1,0:T(1,128)S(1)} %slice.161), channel_id=1, source_target_pairs={{0,1},{1,2},{2,3},{3,4},{4,5},{5,6},{6,7},{7,8},{8,9},{9,10},{10,1... | collective-permute-start | bytes 43688 | tf_op jit(solution)/shard_map/ppermute | solution.py:10
  76.1 0.1 slice.171
  76.2 2.2 %collective-permute-done.5 = f32[2,4,1,455]{3,2,1,0:T(1,128)S(1)} collective-permute-done((f32[2,4,1,455]{3,2,1,0:T(1,128)S(1)}, f32[2,4,1,455]{3,2,1,0:T(1,128)S(1)}, u32[]{:S(2)}, u32[]{:S(2)}) %collective-permute-start.5) | collective-permute-done | bytes 14592 | tf_op jit(solution)/shard_map/ppermute | solution.py:10
  78.3 0.0 collective-permute-done.7
  78.3 25.3 %collective-permute-done.2 = f32[1,4,16,455]{3,2,1,0:T(8,128)S(1)} collective-permute-done((f32[1,4,16,455]{3,2,1,0:T(8,128)S(1)}, f32[1,4,16,455]{3,2,1,0:T(8,128)S(1)}, u32[]{:S(2)}, u32[]{:S(2)}) %collective-permute-start.2) | collective-permute-done | bytes 116512 | tf_op jit(solution)/shard_map/ppermute | solution.py:10
  103.6 0.0 collective-permute-done.6
  103.6 5.2 %fusion.32 = f32[2,4,16,455]{3,2,1,0:T(8,128)} fusion(f32[2,4,16,455]{3,2,1,0:T(8,128)S(1)} %get-tuple-element.18, f32[2,4,16,455]{3,2,1,0:T(8,128)S(1)} %get-tuple-element.17, f32[2,4,16,455]{3,2,1,0:T(8,128)S(1)} %get-tuple-element.16, f32[1,4,16,455]{3,2,1,0:T(8,128)S(1)} %get-tuple-element.15, f32[1,4,16,455]{3,2,1,0:T(8,128)S(1)} %collective-permute-done.2, ...), kind=kOutput, calls=%fused_computation.43 | convolution fusion | flops 1529770496 | bytes 11977056 | tf_op jit(solution)/shard_map/dot_general | solution.py:106
  (19 shorter events, 0.1 us)
Async XLA Ops:
  0.8 28.8 %collective-permute-start = (f32[13,1,4,16]{3,2,1,0:T(4,128)S(1)}, f32[13,1,4,16]{3,2,1,0:T(4,128)S(1)}, u32[]{:S(2)}, u32[]{:S(2)}) collective-permute-start(f32[13,1,4,16]{3,2,1,0:T(4,128)S(1)} %get-tuple-element.25), channel_id=1, source_target_pairs={{16,0},{32,16},{48,32},{64,48},{80,64},{96,80},{112,96},{128,112},... | collective-permute-start | bytes 9992 | tf_op jit(solution)/shard_map/ppermute | solution.py:10
  13.2 16.5 %collective-permute-start.3 = (f32[13,2,4,1]{3,2,1,0:T(4,128)S(1)}, f32[13,2,4,1]{3,2,1,0:T(4,128)S(1)}, u32[]{:S(2)}, u32[]{:S(2)}) collective-permute-start(f32[13,2,4,1]{3,2,1,0:T(4,128)S(1)} %fusion.36), channel_id=1, source_target_pairs={{1,0},{2,1},{3,2},{4,3},{5,4},{6,5},{7,6},{8,7},{9,8},{10,9},{11,1... | collective-permute-start | bytes 1256 | tf_op jit(solution)/shard_map/ppermute | solution.py:10
  17.5 29.1 %collective-permute-start.1 = (f32[1,4,16,455]{3,2,1,0:T(8,128)}, f32[1,4,16,455]{3,2,1,0:T(8,128)S(1)}, u32[]{:S(2)}, u32[]{:S(2)}) collective-permute-start(f32[1,4,16,455]{3,2,1,0:T(8,128)} %get-tuple-element.20), channel_id=1, source_target_pairs={{16,0},{32,16},{48,32},{64,48},{80,64},{96,80},{112,96},{128,112},... | collective-permute-start | bytes 349448 | tf_op jit(solution)/shard_map/ppermute | solution.py:10
  21.3 24.5 %collective-permute-start.4 = (f32[2,4,1,455]{3,2,1,0:T(1,128)}, f32[2,4,1,455]{3,2,1,0:T(1,128)}, u32[]{:S(2)}, u32[]{:S(2)}) collective-permute-start(f32[2,4,1,455]{3,2,1,0:T(1,128)} %slice.124), channel_id=1, source_target_pairs={{1,0},{2,1},{3,2},{4,3},{5,4},{6,5},{7,6},{8,7},{9,8},{10,9},{11,1... | collective-permute-start | bytes 43688 | tf_op jit(solution)/shard_map/ppermute | solution.py:10
  26.3 1.7 %copy-start.2 = (f32[12,2,4,16]{3,2,1,0:T(4,128)S(1)}, f32[12,2,4,16]{3,2,1,0:T(4,128)}, u32[]{:S(2)}) copy-start(f32[12,2,4,16]{3,2,1,0:T(4,128)} %param.6) | copy-start | bytes 18436
  26.3 1.7 %copy-start.8 = (f32[2,4,16]{2,1,0:T(4,128)S(1)}, f32[2,4,16]{2,1,0:T(4,128)}, u32[]{:S(2)}) copy-start(f32[2,4,16]{2,1,0:T(4,128)} %param.5) | copy-start | bytes 1540
  26.4 1.7 %copy-start.1 = (f32[2,4,16,455]{3,2,1,0:T(8,128)S(1)}, f32[2,4,16,455]{3,2,1,0:T(8,128)}, u32[]{:S(2)}) copy-start(f32[2,4,16,455]{3,2,1,0:T(8,128)} %param.4) | copy-start | bytes 698884
  46.7 0.6 copy-start.5
  61.8 2.2 %copy-start.3 = (f32[2,4,15,455]{3,2,1,0:T(8,128)S(1)}, f32[2,4,15,455]{3,2,1,0:T(8,128)}, u32[]{:S(2)}) copy-start(f32[2,4,15,455]{3,2,1,0:T(8,128)} %slice.123) | copy-start | bytes 655204
  61.8 2.2 %copy-start.4 = (f32[2,3,16,455]{3,2,1,0:T(8,128)S(1)}, f32[2,3,16,455]{3,2,1,0:T(8,128)}, u32[]{:S(2)}) copy-start(f32[2,3,16,455]{3,2,1,0:T(8,128)} %slice.118) | copy-start | bytes 524164
  61.8 2.2 %copy-start.6 = (f32[1,4,16,455]{3,2,1,0:T(8,128)S(1)}, f32[1,4,16,455]{3,2,1,0:T(8,128)}, u32[]{:S(2)}) copy-start(f32[1,4,16,455]{3,2,1,0:T(8,128)} %copy-done.5) | copy-start | bytes 349444
  61.8 2.2 %copy-start.7 = (f32[1,4,16,455]{3,2,1,0:T(8,128)S(1)}, f32[1,4,16,455]{3,2,1,0:T(8,128)}, u32[]{:S(2)}) copy-start(f32[1,4,16,455]{3,2,1,0:T(8,128)} %get-tuple-element.19) | copy-start | bytes 349444
  61.8 2.2 %copy-start.9 = (f32[2,4,16]{2,1,0:T(4,128)S(1)}, f32[2,4,16]{2,1,0:T(4,128)}, u32[]{:S(2)}) copy-start(f32[2,4,16]{2,1,0:T(4,128)} %get-tuple-element.32) | copy-start | bytes 1540
  61.9 41.7 %collective-permute-start.6 = (f32[1,4,16,2184]{3,2,1,0:T(8,128)S(1)}, f32[1,4,16,2184]{3,2,1,0:T(8,128)S(1)}, u32[]{:S(2)}, u32[]{:S(2)}) collective-permute-start(f32[1,4,16,2184]{3,2,1,0:T(8,128)S(1)} %get-tuple-element.9), channel_id=1, source_target_pairs={{0,16},{16,32},{32,48},{48,64},{64,80},{80,96},{96,112},{112,128},... | collective-permute-start | bytes 1677320 | tf_op jit(solution)/shard_map/ppermute | solution.py:10
  64.9 38.7 %copy-start = (f32[455,1092]{1,0:T(8,128)S(1)}, f32[455,1092]{1,0:T(8,128)}, u32[]{:S(2)}) copy-start(f32[455,1092]{1,0:T(8,128)} %get-tuple-element.34) | copy-start | bytes 5962324
  64.9 38.7 %collective-permute-start.2 = (f32[1,4,16,455]{3,2,1,0:T(8,128)S(1)}, f32[1,4,16,455]{3,2,1,0:T(8,128)S(1)}, u32[]{:S(2)}, u32[]{:S(2)}) collective-permute-start(f32[1,4,16,455]{3,2,1,0:T(8,128)S(1)} %get-tuple-element.14), channel_id=1, source_target_pairs={{0,16},{16,32},{32,48},{48,64},{64,80},{80,96},{96,112},{112,128},... | collective-permute-start | bytes 349448 | tf_op jit(solution)/shard_map/ppermute | solution.py:10
  67.1 11.3 %collective-permute-start.7 = (f32[2,4,1,2184]{3,2,1,0:T(1,128)S(1)}, f32[2,4,1,2184]{3,2,1,0:T(1,128)S(1)}, u32[]{:S(2)}, u32[]{:S(2)}) collective-permute-start(f32[2,4,1,2184]{3,2,1,0:T(1,128)S(1)} %slice.175), channel_id=1, source_target_pairs={{0,1},{1,2},{2,3},{3,4},{4,5},{5,6},{6,7},{7,8},{8,9},{9,10},{10,1... | collective-permute-start | bytes 209672 | tf_op jit(solution)/shard_map/ppermute | solution.py:10
  72.7 5.6 %collective-permute-start.5 = (f32[2,4,1,455]{3,2,1,0:T(1,128)S(1)}, f32[2,4,1,455]{3,2,1,0:T(1,128)S(1)}, u32[]{:S(2)}, u32[]{:S(2)}) collective-permute-start(f32[2,4,1,455]{3,2,1,0:T(1,128)S(1)} %slice.161), channel_id=1, source_target_pairs={{0,1},{1,2},{2,3},{3,4},{4,5},{5,6},{6,7},{7,8},{8,9},{9,10},{10,1... | collective-permute-start | bytes 43688 | tf_op jit(solution)/shard_map/ppermute | solution.py:10
where the time goes:
time: 110 us; the launch traced here: 109 us
  starting transfers between devices  31.9 us (29%)
  waiting for transfers between devices  27.5 us (25%)
  local copies, waits for them, and re-layouts  25 us (23%)
  other arithmetic  13.7 us (12%)
  matrix products  10.3 us (9%)
    ppermute x8, starting transfers between devices, from_behind(): return lax.ppermute(block, axis, route)  31.9 us
    ppermute x8, waiting for transfers between devices, from_behind(): return lax.ppermute(block, axis, route)  27.5 us
    slice x6, local copies, waits for them, and re-layouts, ahead(): kept = lax.slice_in_dim(values, 1, size, axis=direction)  6.34 us
    dot_general x1, matrix products, per_device(): jnp.dot(coupled_sum.reshape(-1, pick.shape[1]), place, precision=lax.Prec...  5.23 us
    dot_general x1, matrix products, gather_pairs(): jnp.dot(flat, pick, precision=lax.Precision.HIGHEST, preferred_element_ty...  5.12 us
    transpose x5, local copies, waits for them, and re-layouts, couple_weights(): kl_last = jnp.moveaxis(kl_face, 0, -1)  4.45 us
    mul x1, other arithmetic, per_device(): coupled = coupled_diffs[direction] * couple_weights(face_coef[1:], scaling)  3.79 us
    reshape x3, local copies, waits for them, and re-layouts, couple_weights(): jnp.repeat(kl_last, scaling.shape[0] // variables, axis=-1) * scaling  3.6 us
  transfers between devices with their start and end apart: 8, of which 2 were waited for; matrix products, arithmetic and copies ran while one was open for 26% of the time, Pallas kernels for 0%

commit v1 on v0

v1 whole, which is shorter than its diff:
```python
import functools

import jax
import jax.numpy as jnp
from jax import lax
from jax.experimental import pallas as pl
from jax.experimental.pallas import tpu as pltpu
from jax.sharding import PartitionSpec as P

F32, BF16 = jnp.float32, jnp.bfloat16
LANES = 128
ROWS, DEPTH, COLS = 2, 4, 16
ROW_CELLS = DEPTH * COLS
CELLS = ROWS * ROW_CELLS
GROUPS = ROWS * DEPTH
WIDTH = 512
COEF = 72


def split(x):
    hi = x.astype(BF16)
    lo = (x - hi.astype(F32)).astype(BF16)
    return jnp.concatenate([hi, lo], axis=0)


def dot(a, b):
    return jnp.dot(a, b, preferred_element_type=F32)


def dot_t(a, b):
    return lax.dot_general(a, b, (((1,), (1,)), ((), ())), preferred_element_type=F32)


def pack_kernel(modes, f_ref, mean_ref, kl_ref, wide1_ref, wide2_ref, nar1_ref, nar2_ref, all_ref):
    variables = kl_ref.shape[0]
    w_odd = lax.rem(lax.axis_index("wide"), 2)
    n_odd = lax.rem(lax.axis_index("narrow"), 2)
    slabs = []
    for g in range(GROUPS):
        r, z = divmod(g, DEPTH)
        slabs.append(mean_ref[r, z : z + 1, :])
        slabs.append(kl_ref[:, r, z, :])
        slabs.append(jnp.zeros((COLS - 1 - variables, COLS), F32))
    stacked = jnp.concatenate(slabs, axis=0)
    stacked = jnp.concatenate([stacked, jnp.zeros((CELLS, LANES - COLS), F32)], axis=1)
    turned = stacked.T[:COLS]
    lane = lax.broadcasted_iota(jnp.int32, (COLS, LANES), 1)
    inside = (lane >= COEF) & (lane < COEF + variables + 1)
    last = WIDTH - LANES
    for g in range(GROUPS):
        r, z = divmod(g, DEPTH)
        part = pltpu.roll(turned, (COEF - g * COLS) % LANES, axis=1)
        all_ref[g * COLS : (g + 1) * COLS, last:] = jnp.where(inside, part, 0.0)
    for r in range(ROWS):
        all_ref[r * ROW_CELLS : (r + 1) * ROW_CELLS, :modes] = f_ref[r]
    wide1_ref[...] = all_ref[pl.ds(pl.multiple_of(w_odd * ROW_CELLS, ROW_CELLS), ROW_CELLS), :]
    wide2_ref[...] = all_ref[pl.ds(pl.multiple_of((1 - w_odd) * ROW_CELLS, ROW_CELLS), ROW_CELLS), :]
    for g in range(GROUPS):
        ref = wide1_ref if g < DEPTH else wide2_ref
        at = g % DEPTH * COLS
        first = ref[at : at + 1, :]
        final = ref[at + COLS - 1 : at + COLS, :]
        nar1_ref[g : g + 1, :] = jnp.where(n_odd == 1, final, first)
        nar2_ref[g : g + 1, :] = jnp.where(n_odd == 1, first, final)


def pack(field, mean, kl):
    shape = jax.ShapeDtypeStruct
    vmem = pl.BlockSpec(memory_space=pltpu.VMEM)
    return pl.pallas_call(
        functools.partial(pack_kernel, field.shape[-1]),
        out_shape=(
            shape((ROW_CELLS, WIDTH), F32),
            shape((ROW_CELLS, WIDTH), F32),
            shape((GROUPS, WIDTH), F32),
            shape((GROUPS, WIDTH), F32),
        ),
        in_specs=[vmem] * 3,
        out_specs=[vmem] * 4,
        scratch_shapes=[pltpu.VMEM((CELLS, WIDTH), F32)],
        name="pack",
    )(field, mean, kl)


def modes_of(ref, modes):
    x = ref[...]
    lane = lax.broadcasted_iota(jnp.int32, x.shape, 1)
    return jnp.where(lane < modes, x, 0.0)


def coefs_of(ref):
    return ref[:, WIDTH - LANES :]


def column(coefs, k):
    return jnp.broadcast_to(coefs[:, COEF + k : COEF + k + 1], coefs.shape)


def tables(pairs_ref, pick_ref, place_ref, level_ref):
    variables, _, count = pairs_ref.shape
    mode = lax.broadcasted_iota(jnp.int32, (WIDTH, LANES), 0)
    lane = lax.broadcasted_iota(jnp.int32, (1, LANES), 1)
    used = lane < count

    def row(k, c):
        values = jnp.concatenate(
            [pairs_ref[k, c : c + 1, :], jnp.zeros((1, LANES - count), jnp.int32)], axis=1
        )
        return values

    low = jnp.where(used, row(0, 0), -1)
    low_column = jnp.broadcast_to(low, (LANES, LANES)).T
    eye = jnp.where(used & (low_column == low), 1.0, 0.0).astype(BF16)
    hot = jnp.where(mode == low, 1.0, 0.0).astype(BF16)
    pick_ref[:, :LANES] = hot
    place_ref[:LANES, :] = dot_t(eye, hot).astype(BF16)
    for k in range(variables):
        same = jnp.where(used & (low_column == row(k, 0)), 1.0, 0.0).astype(BF16)
        raised = jnp.where(mode == jnp.where(used, row(k, 1), -1), 1.0, 0.0).astype(BF16)
        levels = jnp.broadcast_to(jnp.where(used, row(k, 2), 0).astype(F32), (16, LANES)).astype(BF16)
        at = (k + 1) * LANES
        pick_ref[:, at : at + LANES] = dot_t(raised, same).astype(BF16)
        place_ref[at : at + LANES, :] = dot_t(same, raised).astype(BF16)
        level_ref[k * 8 : (k + 1) * 8, :] = jnp.sqrt(dot_t(levels, same)[:8])


def inner_kernel(modes, a_ref, b_ref, nar1_ref, nar2_ref, pairs_ref, pick_ref, place_ref, level_ref, side_ref,
                 low_ref, center_ref, picked_ref):
    variables = pairs_ref.shape[0]
    n_index = lax.axis_index("narrow")
    n_odd = lax.rem(n_index, 2)
    tables(pairs_ref, pick_ref, place_ref, level_ref)

    u = jnp.concatenate([modes_of(a_ref, modes), modes_of(b_ref, modes)], axis=0)
    c = jnp.concatenate([coefs_of(a_ref), coefs_of(b_ref)], axis=0)
    n1, n2 = nar1_ref[...], nar2_ref[...]
    before = jnp.where(n_odd == 1, n2, n1)
    behind = jnp.where(n_odd == 1, n1, n2)
    lane8 = lax.broadcasted_iota(jnp.int32, before.shape, 1)
    edge = jnp.concatenate([before, behind], axis=0)
    edge_u = jnp.concatenate(
        [jnp.where(lane8 < modes, before, 0.0), jnp.where(lane8 < modes, behind, 0.0)], axis=0
    )
    edge_c = edge[:, WIDTH - LANES :]
    rows = CELLS + 2 * GROUPS
    both = dot(split(jnp.concatenate([u, edge_u], axis=0)), pick_ref[...])
    picked_ref[...] = both[:rows] + both[rows:]

    face_y = 0.5 * (c[:ROW_CELLS] + c[ROW_CELLS:])
    zero = jnp.zeros((COLS, LANES), F32)

    def up_z(x):
        return jnp.concatenate(
            [x[COLS:ROW_CELLS], zero, x[ROW_CELLS + COLS :], zero], axis=0
        )

    def down_z(x):
        return jnp.concatenate(
            [zero, x[: ROW_CELLS - COLS], zero, x[ROW_CELLS : CELLS - COLS]], axis=0
        )

    face_z = 0.5 * (c + up_z(c))
    cell = lax.broadcasted_iota(jnp.int32, (CELLS, LANES), 0)
    not_last = lax.rem(cell, COLS) < COLS - 1
    face_x = jnp.where(not_last, 0.5 * (c + pltpu.roll(c, CELLS - 1, axis=0)), 0.0)

    def strip(get):
        return jnp.concatenate(
            [get(slice(g * COLS, g * COLS + 1)) for g in range(GROUPS)]
            + [get(slice((g + 1) * COLS - 1, (g + 1) * COLS)) for g in range(GROUPS)],
            axis=0,
        )

    edge_face = 0.5 * (strip(lambda s: c[s]) + edge_c)
    row16 = lax.broadcasted_iota(jnp.int32, edge_face.shape, 0)
    edge_face = jnp.where((n_index == 0) & (row16 < GROUPS), 0.0, edge_face)

    def weighted(k, dy, dz, dx):
        fy = column(face_y, k) * dy
        fz = column(face_z, k) * dz
        fx = column(face_x, k) * dx
        net = fz - down_z(fz) + fx - pltpu.roll(fx, 1, axis=0)
        return net + jnp.concatenate([fy, -fy], axis=0)

    def diffs(x):
        return (
            x[:ROW_CELLS] - x[ROW_CELLS:],
            x - up_z(x),
            x - pltpu.roll(x, CELLS - 1, axis=0),
        )

    def edge_diff(x, e):
        return strip(lambda s: x[s]) - e

    def add_edge(ref, lanes, value):
        for g in range(GROUPS):
            ref[g * COLS : g * COLS + 1, lanes] += value[g : g + 1]
            s = (g + 1) * COLS - 1
            ref[s : s + 1, lanes] += value[GROUPS + g : GROUPS + g + 1]

    for t in range(WIDTH // LANES):
        lanes = slice(t * LANES, (t + 1) * LANES)
        x = u[:, lanes]
        center_ref[:, lanes] = weighted(0, *diffs(x))
        add_edge(center_ref, lanes, column(edge_face, 0) * edge_diff(x, edge_u[:, lanes]))

    low = picked_ref[:CELLS, :LANES]
    low_diffs = diffs(low)
    low_edge = edge_diff(low, picked_ref[CELLS:, :LANES])
    low_sum = jnp.zeros((CELLS, LANES), F32)
    low_edge_sum = jnp.zeros((2 * GROUPS, LANES), F32)
    for k in range(1, variables + 1):
        lanes = slice(k * LANES, (k + 1) * LANES)
        out = slice((k - 1) * LANES, k * LANES)
        level = level_ref[(k - 1) * 8 : (k - 1) * 8 + 1, :]
        side_ref[:, out] = weighted(k, *low_diffs)
        add_edge(side_ref, out, column(edge_face, k) * low_edge)
        x = picked_ref[:CELLS, lanes]
        low_sum = low_sum + level * weighted(k, *diffs(x))
        low_edge_sum = low_edge_sum + level * (
            column(edge_face, k) * edge_diff(x, picked_ref[CELLS:, lanes])
        )
    low_ref[...] = low_sum
    add_edge(low_ref, slice(0, LANES), low_edge_sum)


def inner(modes, a, b, n1, n2, turned_pairs):
    shape = jax.ShapeDtypeStruct
    vmem = pl.BlockSpec(memory_space=pltpu.VMEM)
    variables = turned_pairs.shape[0]
    blocks = (variables + 1) * LANES
    return pl.pallas_call(
        functools.partial(inner_kernel, modes),
        out_shape=(
            shape((WIDTH, blocks), BF16),
            shape((blocks, WIDTH), BF16),
            shape((8 * variables, LANES), F32),
            shape((CELLS, variables * LANES), F32),
            shape((CELLS, LANES), F32),
            shape((CELLS, WIDTH), F32),
        ),
        in_specs=[vmem] * 5,
        out_specs=[vmem] * 6,
        scratch_shapes=[pltpu.VMEM((CELLS + 2 * GROUPS, blocks), F32)],
        compiler_params=pltpu.CompilerParams(vmem_limit_bytes=40 * 1024 * 1024),
        cost_estimate=pl.CostEstimate(flops=2_000_000_000, bytes_accessed=10_000_000, transcendentals=0),
        name="inner",
    )(a, b, n1, n2, turned_pairs)


def outer_kernel(modes, a_ref, b_ref, ha_ref, hb_ref, pick_ref, place_ref, level_ref, side_ref, low_ref,
                 center_ref, out_ref, terms_ref):
    variables = side_ref.shape[1] // LANES
    w_index = lax.axis_index("wide")
    w_odd = lax.rem(w_index, 2)
    d = jnp.concatenate(
        [modes_of(a_ref, modes) - modes_of(ha_ref, modes), modes_of(b_ref, modes) - modes_of(hb_ref, modes)], axis=0
    )
    face_a = 0.5 * (coefs_of(a_ref) + coefs_of(ha_ref))
    face_a = jnp.where(w_index == 0, 0.0, face_a)
    face = jnp.concatenate([face_a, 0.5 * (coefs_of(b_ref) + coefs_of(hb_ref))], axis=0)
    both = dot(split(d), pick_ref[...])
    picked = both[:CELLS] + both[CELLS:]
    low = picked[:, :LANES]
    low_sum = low_ref[...]
    for k in range(1, variables + 1):
        level = level_ref[(k - 1) * 8 : (k - 1) * 8 + 1, :]
        f = column(face, k)
        low_sum = low_sum + level * (f * picked[:, k * LANES : (k + 1) * LANES])
        side = level * (side_ref[:, (k - 1) * LANES : k * LANES] + f * low)
        terms_ref[:, k * LANES : (k + 1) * LANES] = split(side)
    terms_ref[:, :LANES] = split(low_sum)
    spread = dot(terms_ref[...], place_ref[...])
    f = column(face, 0)
    f = jnp.concatenate([f] * (WIDTH // LANES), axis=1)
    total = center_ref[...] + f * d + spread[:CELLS] + spread[CELLS:]
    out_ref[pl.ds(w_odd, 1)] = total[None, :ROW_CELLS, :modes]
    out_ref[pl.ds(1 - w_odd, 1)] = total[None, ROW_CELLS:, :modes]


def outer(modes, a, b, ha, hb, parts):
    vmem = pl.BlockSpec(memory_space=pltpu.VMEM)
    blocks = parts[0].shape[1]
    return pl.pallas_call(
        functools.partial(outer_kernel, modes),
        out_shape=jax.ShapeDtypeStruct((ROWS, ROW_CELLS, modes), F32),
        in_specs=[vmem] * 10,
        out_specs=vmem,
        scratch_shapes=[pltpu.VMEM((2 * CELLS, blocks), BF16)],
        compiler_params=pltpu.CompilerParams(vmem_limit_bytes=40 * 1024 * 1024),
        name="outer",
    )(a, b, ha, hb, *parts)


def exchange(block, axis, first):
    route = []
    for i in range(first, lax.axis_size(axis) - 1, 2):
        route += [(i, i + 1), (i + 1, i)]
    return lax.ppermute(block, axis, route)


def per_device(chaos_field, mean_conductivity, kl_fields, pairs):
    modes = chaos_field.shape[-1]
    field = chaos_field.reshape(ROWS, ROW_CELLS, modes)
    a, b, n1, n2 = pack(field, mean_conductivity, kl_fields)
    halo_a = exchange(a, "wide", 1)
    edge_1 = exchange(n1, "narrow", 1)
    edge_2 = exchange(n2, "narrow", 0)
    halo_b = exchange(b, "wide", 0)
    parts = inner(modes, a, b, edge_1, edge_2, pairs.transpose(0, 2, 1))
    out = outer(modes, a, b, halo_a, halo_b, parts)
    return out.reshape(chaos_field.shape)


def solution(mesh):
    placed = (
        P("wide", None, "narrow", None),
        P("wide", None, "narrow"),
        P(None, "wide", None, "narrow"),
        P(),
    )
    return jax.shard_map(
        per_device,
        mesh=mesh,
        in_specs=placed,
        out_specs=P("wide", None, "narrow", None),
        check_vma=False,
    )
```

time: 110 us -> 30.8 us (0.28)
  the two profiles are of different devices: /device:TPU:62 before, /device:TPU:7 now
where the time goes in v1:
time: 30.8 us; the launch traced here: 30.5 us
  starting transfers between devices  21.4 us (69%)
  Pallas kernels  6.47 us (21%)
  local copies, waits for them, and re-layouts  2.54 us (8%)
    ppermute x4, starting transfers between devices, exchange(): return lax.ppermute(block, axis, route)  21.4 us
    pallas_call x1, Pallas kernels, inner(): pl.pallas_call(functools.partial(inner_kernel, modes), out_shape=(shape((...  2.55 us
    unnamed x6, local copies, waits for them, and re-layouts  2.54 us
    pallas_call x1, Pallas kernels, outer(): pl.pallas_call(functools.partial(outer_kernel, modes), out_shape=jax.Shap...  2.05 us
    pallas_call x1, Pallas kernels, pack(): pl.pallas_call(functools.partial(pack_kernel, field.shape[-1]), out_shape...  1.87 us
  transfers between devices with their start and end apart: 4, of which 0 were waited for; matrix products, arithmetic and copies ran while one was open for 0% of the time, Pallas kernels for 8%

profile of v1, /device:TPU:7, one launch (start us, length us, event | category | flops | bytes accessed | tf_op | source)
XLA Modules:
  0.0 30.5 jit_solution(2754241138488075796)
XLA Ops:
  0.0 1.9 %pack.1 = (f32[64,512]{1,0:T(8,128)}, f32[64,512]{1,0:T(8,128)}, f32[8,512]{1,0:T(8,128)}, f32[8,512]{1,0:T(8,128)}) custom-call(f32[2,64,455]{2,1,0:T(8,128)} %bitcast.4, f32[2,4,16]{2,1,0:T(4,128)} %mean_ref.1, f32[12,2,4,16]{3,2,1,0:T(4,128)} %kl_ref.1), custom_call_target="tpu_custom_call" | custom-call | tf_op jit(solution)/shard_map/pack/pallas_call | solution.py:70
  1.9 0.7 %collective-permute-start.2 = (f32[8,512]{1,0:T(8,128)}, f32[8,512]{1,0:T(8,128)S(1)}, u32[]{:S(2)}, u32[]{:S(2)}) collective-permute-start(f32[8,512]{1,0:T(8,128)} %get-tuple-element.17), channel_id=1, source_target_pairs={{1,2},{2,1},{3,4},{4,3},{5,6},{6,5},{7,8},{8,7},{9,10},{10,9},{11,... | collective-permute-start | bytes 49160 | tf_op jit(solution)/shard_map/ppermute | solution.py:299
  2.5 5.7 %collective-permute-start.3 = (f32[8,512]{1,0:T(8,128)}, f32[8,512]{1,0:T(8,128)S(1)}, u32[]{:S(2)}, u32[]{:S(2)}) collective-permute-start(f32[8,512]{1,0:T(8,128)} %get-tuple-element.18), channel_id=1, source_target_pairs={{0,1},{1,0},{2,3},{3,2},{4,5},{5,4},{6,7},{7,6},{8,9},{9,8},{10,11... | collective-permute-start | bytes 49160 | tf_op jit(solution)/shard_map/ppermute | solution.py:299
  8.3 9.9 %collective-permute-start = (f32[64,512]{1,0:T(8,128)}, f32[64,512]{1,0:T(8,128)S(1)}, u32[]{:S(2)}, u32[]{:S(2)}) collective-permute-start(f32[64,512]{1,0:T(8,128)} %get-tuple-element.15.a_ref), channel_id=1, source_target_pairs={{16,32},{32,16},{48,64},{64,48},{80,96},{96,80},{112,128},{128,112... | collective-permute-start | bytes 393224 | tf_op jit(solution)/shard_map/ppermute | solution.py:299
  18.2 5.1 %collective-permute-start.1 = (f32[64,512]{1,0:T(8,128)}, f32[64,512]{1,0:T(8,128)S(1)}, u32[]{:S(2)}, u32[]{:S(2)}) collective-permute-start(f32[64,512]{1,0:T(8,128)} %get-tuple-element.16.b_ref), channel_id=1, source_target_pairs={{0,16},{16,0},{32,48},{48,32},{64,80},{80,64},{96,112},{112,96},{1... | collective-permute-start | bytes 393224 | tf_op jit(solution)/shard_map/ppermute | solution.py:299
  23.3 0.0 collective-permute-done.2.nar1_ref
  23.3 0.0 collective-permute-done.3.nar2_ref
  23.3 0.0 copy-start
  23.4 0.9 %copy-done = f32[64,512]{1,0:T(8,128)S(1)} copy-done((f32[64,512]{1,0:T(8,128)S(1)}, f32[64,512]{1,0:T(8,128)}, u32[]{:S(2)}) %copy-start) | copy-done | bytes 131096
  24.2 0.0 copy-start.1
  24.3 0.9 %copy-done.1 = f32[64,512]{1,0:T(8,128)S(1)} copy-done((f32[64,512]{1,0:T(8,128)S(1)}, f32[64,512]{1,0:T(8,128)}, u32[]{:S(2)}) %copy-start.1) | copy-done | bytes 131096
  25.2 0.0 copy-start.2
  25.2 0.7 %copy-done.2 = s32[12,91,3]{1,2,0:T(4,128)S(1)} copy-done((s32[12,91,3]{1,2,0:T(4,128)S(1)}, s32[12,91,3]{1,2,0:T(4,128)}, u32[]{:S(2)}) %copy-start.2) | copy-done | bytes 13128
  25.9 2.6 %inner.1 = (bf16[512,1664]{1,0:T(8,128)(2,1)S(1)}, bf16[1664,512]{1,0:T(8,128)(2,1)S(1)}, f32[96,128]{1,0:T(8,128)S(1)}, f32[128,1536]{1,0:T(8,128)S(1)}, f32[12...) custom-call(f32[64,512]{1,0:T(8,128)S(1)} %copy-done, f32[64,512]{1,0:T(8,128)S(1)} %copy-done.1, ...), custom_call_target="tpu_custom_call" | custom-call | flops 2000000000 | bytes 10000000 | tf_op jit(solution)/shard_map/inner/pallas_call | solution.py:232
  28.4 0.0 collective-permute-done.ha_ref
  28.5 0.0 collective-permute-done.1.hb_ref
  28.5 2.0 %outer.1 = f32[2,64,455]{2,1,0:T(8,128)} custom-call(f32[64,512]{1,0:T(8,128)S(1)} %copy-done, f32[64,512]{1,0:T(8,128)S(1)} %copy-done.1, f32[64,512]{1,0:T(8,128)S(1)} %collective-permute-done.ha_ref, f32[64,512]{1,0:T(8,128)S(1)} %collective-permute-done.1.hb_ref, bf16[512,1664]{1,0:T(8,128)(2,1)S(1)} %get-tuple-element.19.pick_ref, ...), custom_call_target="tpu_custom_call" | custom-call | tf_op jit(solution)/shard_map/outer/pallas_call | solution.py:284
Async XLA Ops:
  1.9 21.5 %collective-permute-start.2 = (f32[8,512]{1,0:T(8,128)}, f32[8,512]{1,0:T(8,128)S(1)}, u32[]{:S(2)}, u32[]{:S(2)}) collective-permute-start(f32[8,512]{1,0:T(8,128)} %get-tuple-element.17), channel_id=1, source_target_pairs={{1,2},{2,1},{3,4},{4,3},{5,6},{6,5},{7,8},{8,7},{9,10},{10,9},{11,... | collective-permute-start | bytes 49160 | tf_op jit(solution)/shard_map/ppermute | solution.py:299
  2.5 20.8 %collective-permute-start.3 = (f32[8,512]{1,0:T(8,128)}, f32[8,512]{1,0:T(8,128)S(1)}, u32[]{:S(2)}, u32[]{:S(2)}) collective-permute-start(f32[8,512]{1,0:T(8,128)} %get-tuple-element.18), channel_id=1, source_target_pairs={{0,1},{1,0},{2,3},{3,2},{4,5},{5,4},{6,7},{7,6},{8,9},{9,8},{10,11... | collective-permute-start | bytes 49160 | tf_op jit(solution)/shard_map/ppermute | solution.py:299
  8.3 20.2 %collective-permute-start = (f32[64,512]{1,0:T(8,128)}, f32[64,512]{1,0:T(8,128)S(1)}, u32[]{:S(2)}, u32[]{:S(2)}) collective-permute-start(f32[64,512]{1,0:T(8,128)} %get-tuple-element.15.a_ref), channel_id=1, source_target_pairs={{16,32},{32,16},{48,64},{64,48},{80,96},{96,80},{112,128},{128,112... | collective-permute-start | bytes 393224 | tf_op jit(solution)/shard_map/ppermute | solution.py:299
  18.2 10.2 %collective-permute-start.1 = (f32[64,512]{1,0:T(8,128)}, f32[64,512]{1,0:T(8,128)S(1)}, u32[]{:S(2)}, u32[]{:S(2)}) collective-permute-start(f32[64,512]{1,0:T(8,128)} %get-tuple-element.16.b_ref), channel_id=1, source_target_pairs={{0,16},{16,0},{32,48},{48,32},{64,80},{80,64},{96,112},{112,96},{1... | collective-permute-start | bytes 393224 | tf_op jit(solution)/shard_map/ppermute | solution.py:299
  23.3 0.9 %copy-start = (f32[64,512]{1,0:T(8,128)S(1)}, f32[64,512]{1,0:T(8,128)}, u32[]{:S(2)}) copy-start(f32[64,512]{1,0:T(8,128)} %get-tuple-element.15.a_ref) | copy-start | bytes 393220
  24.2 0.9 %copy-start.1 = (f32[64,512]{1,0:T(8,128)S(1)}, f32[64,512]{1,0:T(8,128)}, u32[]{:S(2)}) copy-start(f32[64,512]{1,0:T(8,128)} %get-tuple-element.16.b_ref) | copy-start | bytes 393220
  25.2 0.7 %copy-start.2 = (s32[12,91,3]{1,2,0:T(4,128)S(1)}, s32[12,91,3]{1,2,0:T(4,128)}, u32[]{:S(2)}) copy-start(s32[12,91,3]{1,2,0:T(4,128)} %param.7) | copy-start | bytes 39316

commit v2 on v1

--- a/solution.py
+++ b/solution.py
@@ -14,6 +14,7 @@
 CELLS = ROWS * ROW_CELLS
 GROUPS = ROWS * DEPTH
 WIDTH = 512
+HBM = pl.BlockSpec(memory_space=pltpu.HBM)
 COEF = 72
 
 
@@ -31,7 +32,17 @@
     return lax.dot_general(a, b, (((1,), (1,)), ((), ())), preferred_element_type=F32)
 
 
-def pack_kernel(modes, f_ref, mean_ref, kl_ref, wide1_ref, wide2_ref, nar1_ref, nar2_ref, all_ref):
+def fetch(sources, targets, sems):
+    copies = [pltpu.make_async_copy(s, t, sems.at[i]) for i, (s, t) in enumerate(zip(sources, targets))]
+    for copy in copies:
+        copy.start()
+    for copy in copies:
+        copy.wait()
+
+
+def pack_kernel(modes, f_hbm, mean_hbm, kl_hbm, wide1_ref, wide2_ref, nar1_ref, nar2_ref, all_ref, f_ref, mean_ref,
+                kl_ref, sems):
+    fetch((f_hbm, mean_hbm, kl_hbm), (f_ref, mean_ref, kl_ref), sems)
     variables = kl_ref.shape[0]
     w_odd = lax.rem(lax.axis_index("wide"), 2)
     n_odd = lax.rem(lax.axis_index("narrow"), 2)
@@ -75,9 +86,12 @@
             shape((GROUPS, WIDTH), F32),
             shape((GROUPS, WIDTH), F32),
         ),
-        in_specs=[vmem] * 3,
+        in_specs=[HBM] * 3,
         out_specs=[vmem] * 4,
-        scratch_shapes=[pltpu.VMEM((CELLS, WIDTH), F32)],
+        scratch_shapes=[pltpu.VMEM((CELLS, WIDTH), F32)]
+        + [pltpu.VMEM(x.shape, F32) for x in (field, mean, kl)]
+        + [pltpu.SemaphoreType.DMA((3,))],
+        compiler_params=pltpu.CompilerParams(vmem_limit_bytes=60 * 1024 * 1024),
         name="pack",
     )(field, mean, kl)
 
@@ -96,7 +110,8 @@
     return jnp.broadcast_to(coefs[:, COEF + k : COEF + k + 1], coefs.shape)
 
 
-def tables(pairs_ref, pick_ref, place_ref, level_ref):
+def tables_kernel(pairs_hbm, pick_ref, place_ref, level_ref, pairs_ref, sems):
+    fetch((pairs_hbm,), (pairs_ref,), sems)
     variables, _, count = pairs_ref.shape
     mode = lax.broadcasted_iota(jnp.int32, (WIDTH, LANES), 0)
     lane = lax.broadcasted_iota(jnp.int32, (1, LANES), 1)
@@ -124,18 +139,44 @@
         level_ref[k * 8 : (k + 1) * 8, :] = jnp.sqrt(dot_t(levels, same)[:8])
 
 
-def inner_kernel(modes, a_ref, b_ref, nar1_ref, nar2_ref, pairs_ref, pick_ref, place_ref, level_ref, side_ref,
-                 low_ref, center_ref, picked_ref):
-    variables = pairs_ref.shape[0]
+def tables(turned_pairs):
+    shape = jax.ShapeDtypeStruct
+    vmem = pl.BlockSpec(memory_space=pltpu.VMEM)
+    variables = turned_pairs.shape[0]
+    blocks = (variables + 1) * LANES
+    return pl.pallas_call(
+        tables_kernel,
+        out_shape=(
+            shape((WIDTH, blocks), BF16),
+            shape((blocks, WIDTH), BF16),
+            shape((8 * variables, LANES), F32),
+        ),
+        in_specs=[HBM],
+        out_specs=[vmem] * 3,
+        scratch_shapes=[pltpu.VMEM(turned_pairs.shape, jnp.int32), pltpu.SemaphoreType.DMA((1,))],
+        cost_estimate=pl.CostEstimate(flops=1_000_000_000, bytes_accessed=4_000_000, transcendentals=0),
+        compiler_params=pltpu.CompilerParams(vmem_limit_bytes=40 * 1024 * 1024),
+        name="tables",
+    )(turned_pairs)
+
+
+def inner_kernel(modes, a_hbm, b_hbm, nar1_hbm, nar2_hbm, pick_ref, level_ref, side_ref, low_ref, center_ref,
+                 picked_ref, a_ref, b_ref, nar1_ref, nar2_ref, sems):
+    variables = side_ref.shape[1] // LANES
     n_index = lax.axis_index("narrow")
     n_odd = lax.rem(n_index, 2)
-    tables(pairs_ref, pick_ref, place_ref, level_ref)
+    n_end = lax.axis_size("narrow") - 1
+    fetch(
+        (a_hbm, b_hbm, other(nar1_hbm, "narrow", 1), other(nar2_hbm, "narrow", 0)),
+        (a_ref, b_ref, nar1_ref, nar2_ref),
+        sems,
+    )
 
     u = jnp.concatenate([modes_of(a_ref, modes), modes_of(b_ref, modes)], axis=0)
     c = jnp.concatenate([coefs_of(a_ref), coefs_of(b_ref)], axis=0)
     n1, n2 = nar1_ref[...], nar2_ref[...]
     before = jnp.where(n_odd == 1, n2, n1)
-    behind = jnp.where(n_odd == 1, n1, n2)
+    behind = jnp.where(n_index == n_end, 0.0, jnp.where(n_odd == 1, n1, n2))
     lane8 = lax.broadcasted_iota(jnp.int32, before.shape, 1)
     edge = jnp.concatenate([before, behind], axis=0)
     edge_u = jnp.concatenate(
@@ -224,35 +265,48 @@
     add_edge(low_ref, slice(0, LANES), low_edge_sum)
 
 
-def inner(modes, a, b, n1, n2, turned_pairs):
+def inner(modes, a, b, n1, n2, pick, level):
     shape = jax.ShapeDtypeStruct
     vmem = pl.BlockSpec(memory_space=pltpu.VMEM)
-    variables = turned_pairs.shape[0]
-    blocks = (variables + 1) * LANES
+    blocks = pick.shape[1]
     return pl.pallas_call(
         functools.partial(inner_kernel, modes),
         out_shape=(
-            shape((WIDTH, blocks), BF16),
-            shape((blocks, WIDTH), BF16),
-            shape((8 * variables, LANES), F32),
-            shape((CELLS, variables * LANES), F32),
+            shape((CELLS, blocks - LANES), F32),
             shape((CELLS, LANES), F32),
             shape((CELLS, WIDTH), F32),
         ),
-        in_specs=[vmem] * 5,
-        out_specs=[vmem] * 6,
-        scratch_shapes=[pltpu.VMEM((CELLS + 2 * GROUPS, blocks), F32)],
+        in_specs=[HBM] * 4 + [vmem] * 2,
+        out_specs=[vmem] * 3,
+        scratch_shapes=[
+            pltpu.VMEM((CELLS + 2 * GROUPS, blocks), F32),
+            pltpu.VMEM((ROW_CELLS, WIDTH), F32),
+            pltpu.VMEM((ROW_CELLS, WIDTH), F32),
+            pltpu.VMEM((GROUPS, WIDTH), F32),
+            pltpu.VMEM((GROUPS, WIDTH), F32),
+            pltpu.SemaphoreType.DMA((4,)),
+        ],
         compiler_params=pltpu.CompilerParams(vmem_limit_bytes=40 * 1024 * 1024),
         cost_estimate=pl.CostEstimate(flops=2_000_000_000, bytes_accessed=10_000_000, transcendentals=0),
         name="inner",
-    )(a, b, n1, n2, turned_pairs)
-
-
-def outer_kernel(modes, a_ref, b_ref, ha_ref, hb_ref, pick_ref, place_ref, level_ref, side_ref, low_ref,
-                 center_ref, out_ref, terms_ref):
+    )(a, b, n1, n2, pick, level)
+
+
+def outer_kernel(modes, a_hbm, b_hbm, ha_hbm, hb_hbm, pick_ref, place_ref, level_ref, side_ref, low_ref,
+                 center_ref, out_ref, terms_ref, a_ref, b_ref, ha_ref, hb_ref, sems):
     variables = side_ref.shape[1] // LANES
     w_index = lax.axis_index("wide")
     w_odd = lax.rem(w_index, 2)
+    fetch(
+        (a_hbm, b_hbm, other(ha_hbm, "wide", 1), other(hb_hbm, "wide", 0)),
+        (a_ref, b_ref, ha_ref, hb_ref),
+        sems,
+    )
+
+    @pl.when(w_index == lax.axis_size("wide") - 1)
+    def _():
+        ha_ref[...] = jnp.zeros_like(ha_ref)
+
     d = jnp.concatenate(
         [modes_of(a_ref, modes) - modes_of(ha_ref, modes), modes_of(b_ref, modes) - modes_of(hb_ref, modes)], axis=0
     )
@@ -284,31 +338,44 @@
     return pl.pallas_call(
         functools.partial(outer_kernel, modes),
         out_shape=jax.ShapeDtypeStruct((ROWS, ROW_CELLS, modes), F32),
-        in_specs=[vmem] * 10,
+        in_specs=[HBM] * 4 + [vmem] * 6,
         out_specs=vmem,
-        scratch_shapes=[pltpu.VMEM((2 * CELLS, blocks), BF16)],
+        scratch_shapes=[
+            pltpu.VMEM((2 * CELLS, blocks), BF16),
+            pltpu.VMEM((ROW_CELLS, WIDTH), F32),
+            pltpu.VMEM((ROW_CELLS, WIDTH), F32),
+            pltpu.VMEM((ROW_CELLS, WIDTH), F32),
+            pltpu.VMEM((ROW_CELLS, WIDTH), F32),
+            pltpu.SemaphoreType.DMA((4,)),
+        ],
         compiler_params=pltpu.CompilerParams(vmem_limit_bytes=40 * 1024 * 1024),
         name="outer",
     )(a, b, ha, hb, *parts)
 
 
-def exchange(block, axis, first):
-    route = []
-    for i in range(first, lax.axis_size(axis) - 1, 2):
-        route += [(i, i + 1), (i + 1, i)]
-    return lax.ppermute(block, axis, route)
+def pair_up(block, axis, first):
+    size = lax.axis_size(axis)
+    pairs = [[i, (i + 1) % size] for i in range(first, size, 2)]
+    return lax.all_gather(block, axis, axis_index_groups=pairs)
+
+
+def other(ref, axis, first):
+    if ref.shape[0] == 1:
+        return ref.at[0]
+    return ref.at[lax.rem(lax.axis_index(axis) + first + 1, 2)]
 
 
 def per_device(chaos_field, mean_conductivity, kl_fields, pairs):
     modes = chaos_field.shape[-1]
     field = chaos_field.reshape(ROWS, ROW_CELLS, modes)
     a, b, n1, n2 = pack(field, mean_conductivity, kl_fields)
-    halo_a = exchange(a, "wide", 1)
-    edge_1 = exchange(n1, "narrow", 1)
-    edge_2 = exchange(n2, "narrow", 0)
-    halo_b = exchange(b, "wide", 0)
-    parts = inner(modes, a, b, edge_1, edge_2, pairs.transpose(0, 2, 1))
-    out = outer(modes, a, b, halo_a, halo_b, parts)
+    halo_a = pair_up(a, "wide", 1)
+    edge_1 = pair_up(n1, "narrow", 1)
+    edge_2 = pair_up(n2, "narrow", 0)
+    halo_b = pair_up(b, "wide", 0)
+    pick, place, level = tables(pairs.transpose(0, 2, 1))
+    parts = inner(modes, a, b, edge_1, edge_2, pick, level)
+    out = outer(modes, a, b, halo_a, halo_b, (pick, place, level) + tuple(parts))
     return out.reshape(chaos_field.shape)
 
 

time: 30.8 us -> 41.9 us (1.36)
  the two profiles are of different devices: /device:TPU:7 before, /device:TPU:1 now
where the time goes in v2:
time: 41.9 us; the launch traced here: 41.7 us
  blocking collectives  33.1 us (79%)
  Pallas kernels  7.78 us (19%)
  local copies, waits for them, and re-layouts  0.74 us (2%)
    all_gather x4, blocking collectives, pair_up(): return lax.all_gather(block, axis, axis_index_groups=pairs)  33.1 us
    pallas_call x1, Pallas kernels, outer(): pl.pallas_call(functools.partial(outer_kernel, modes), out_shape=jax.Shap...  2.73 us
    pallas_call x1, Pallas kernels, pack(): pl.pallas_call(functools.partial(pack_kernel, field.shape[-1]), out_shape...  1.88 us
    pallas_call x1, Pallas kernels, inner(): pl.pallas_call(functools.partial(inner_kernel, modes), out_shape=(shape((...  1.85 us
    pallas_call x1, Pallas kernels, tables(): pl.pallas_call(tables_kernel, out_shape=(shape((WIDTH, blocks), BF16), sh...  1.32 us

profile of v2, /device:TPU:1, one launch (start us, length us, event | category | flops | bytes accessed | tf_op | source)
XLA Modules:
  0.0 41.7 jit_solution(17231602499445567696)
XLA Ops:
  0.0 1.9 %pack.1 = (f32[64,512]{1,0:T(8,128)}, f32[64,512]{1,0:T(8,128)}, f32[8,512]{1,0:T(8,128)}, f32[8,512]{1,0:T(8,128)}) custom-call(f32[2,64,455]{2,1,0:T(8,128)} %bitcast.12, f32[2,4,16]{2,1,0:T(4,128)} %mean_hbm.1, f32[12,2,4,16]{3,2,1,0:T(4,128)} %kl_hbm.1), custom_call_target="tpu_custom_call" | custom-call | tf_op jit(solution)/shard_map/pack/pallas_call | solution.py:81
  1.9 9.7 %all-gather.2 = f32[16,512]{1,0:T(8,128)S(1)} all-gather(f32[8,512]{1,0:T(8,128)} %get-tuple-element.20), channel_id=4, replica_groups={{1,2},{3,4},{5,6},{7,8},{9,10},{11,12},{13,14},{15,0},{17,18},{19,20},{..., dimensions={0}, use_global_device_ids=true | all-gather | bytes 49152 | tf_op jit(solution)/shard_map/all_gather | solution.py:359
  11.6 3.8 %all-gather.3 = f32[16,512]{1,0:T(8,128)S(1)} all-gather(f32[8,512]{1,0:T(8,128)} %get-tuple-element.21), channel_id=5, replica_groups={{0,1},{2,3},{4,5},{6,7},{8,9},{10,11},{12,13},{14,15},{16,17},{18,19},{..., dimensions={0}, use_global_device_ids=true | all-gather | bytes 49152 | tf_op jit(solution)/shard_map/all_gather | solution.py:359
  15.3 15.6 %all-gather = f32[128,512]{1,0:T(8,128)S(1)} all-gather(f32[64,512]{1,0:T(8,128)} %get-tuple-element.15.a_hbm), channel_id=2, replica_groups={{16,32},{48,64},{80,96},{112,128},{144,160},{176,192},{208,224},{240,25..., dimensions={0}, use_global_device_ids=true | all-gather | bytes 393216 | tf_op jit(solution)/shard_map/all_gather | solution.py:359
  31.0 4.1 %all-gather.1 = f32[128,512]{1,0:T(8,128)S(1)} all-gather(f32[64,512]{1,0:T(8,128)} %get-tuple-element.16.b_hbm), channel_id=3, replica_groups={{0,16},{32,48},{64,80},{96,112},{128,144},{160,176},{192,208},{224,240}..., dimensions={0}, use_global_device_ids=true | all-gather | bytes 393216 | tf_op jit(solution)/shard_map/all_gather | solution.py:359
  35.0 0.0 copy-start.2
  35.0 0.7 %copy-done.2 = s32[12,91,3]{1,2,0:T(4,128)S(1)} copy-done((s32[12,91,3]{1,2,0:T(4,128)S(1)}, s32[12,91,3]{1,2,0:T(4,128)}, u32[]{:S(2)}) %copy-start.2) | copy-done | bytes 13128
  35.8 0.0 copy-start
  35.8 0.0 copy-start.1
  35.8 1.3 %tables.1 = (bf16[512,1664]{1,0:T(8,128)(2,1)S(1)}, bf16[1664,512]{1,0:T(8,128)(2,1)S(1)}, f32[96,128]{1,0:T(8,128)S(1)}) custom-call(s32[12,3,91]{2,1,0:T(4,128)S(1)} %bitcast.11), custom_call_target="tpu_custom_call" | custom-call | flops 1000000000 | bytes 4000000 | tf_op jit(solution)/shard_map/tables/pallas_call | solution.py:147
  37.1 0.0 copy-done
  37.1 0.0 copy-done.1
  37.1 1.9 %inner.1 = (f32[128,1536]{1,0:T(8,128)S(1)}, f32[128,128]{1,0:T(8,128)S(1)}, f32[128,512]{1,0:T(8,128)S(1)}) custom-call(f32[64,512]{1,0:T(8,128)S(1)} %copy-done, f32[64,512]{1,0:T(8,128)S(1)} %copy-done.1, f32[2,8,512]{2,1,0:T(8,128)S(1)} %bitcast.9, f32[2,8,512]{2,1,0:T(8,128)S(1)} %bitcast.10, bf16[512,1664]{1,0:T(8,128)(2,1)S(1)} %get-tuple-element.17.pick_ref, ...), custom_call_target="tpu_custom_call" | custom-call | flops 2000000000 | bytes 10000000 | tf_op jit(solution)/shard_map/inner/pallas_call | solution.py:272
  39.0 2.7 %outer.1 = f32[2,64,455]{2,1,0:T(8,128)} custom-call(f32[64,512]{1,0:T(8,128)S(1)} %copy-done, f32[64,512]{1,0:T(8,128)S(1)} %copy-done.1, f32[2,64,512]{2,1,0:T(8,128)S(1)} %bitcast.7, f32[2,64,512]{2,1,0:T(8,128)S(1)} %bitcast.8, bf16[512,1664]{1,0:T(8,128)(2,1)S(1)} %get-tuple-element.17.pick_ref, bf16[1664,512]{1,0:T(8,128)(2,1)S(1)} %get-tuple-element.18.place_ref, ...), custom_call_target="tpu_custom_call" | custom-call | tf_op jit(solution)/shard_map/outer/pallas_call | solution.py:338
Async XLA Ops:
  35.0 0.7 %copy-start.2 = (s32[12,91,3]{1,2,0:T(4,128)S(1)}, s32[12,91,3]{1,2,0:T(4,128)}, u32[]{:S(2)}) copy-start(s32[12,91,3]{1,2,0:T(4,128)} %param.7) | copy-start | bytes 39316
  35.8 1.3 %copy-start = (f32[64,512]{1,0:T(8,128)S(1)}, f32[64,512]{1,0:T(8,128)}, u32[]{:S(2)}) copy-start(f32[64,512]{1,0:T(8,128)} %get-tuple-element.15.a_hbm) | copy-start | bytes 393220
  35.8 1.3 %copy-start.1 = (f32[64,512]{1,0:T(8,128)S(1)}, f32[64,512]{1,0:T(8,128)}, u32[]{:S(2)}) copy-start(f32[64,512]{1,0:T(8,128)} %get-tuple-element.16.b_hbm) | copy-start | bytes 393220

commit v3 on v1

v3 whole, which is shorter than its diff:
```python
import functools

import jax
import jax.numpy as jnp
from jax import lax
from jax.experimental import pallas as pl
from jax.experimental.pallas import tpu as pltpu
from jax.sharding import PartitionSpec as P

F32, BF16 = jnp.float32, jnp.bfloat16
LANES = 128
ROWS, DEPTH, COLS = 2, 4, 16
ROW_CELLS = DEPTH * COLS
CELLS = ROWS * ROW_CELLS
GROUPS = ROWS * DEPTH
WIDTH = 512
HBM = pl.BlockSpec(memory_space=pltpu.HBM)
IN_VMEM = pl.BlockSpec(memory_space=pltpu.VMEM)
COEF = 72


def split(x):
    hi = x.astype(BF16)
    lo = (x - hi.astype(F32)).astype(BF16)
    return jnp.concatenate([hi, lo], axis=0)


def dot(a, b):
    return jnp.dot(a, b, preferred_element_type=F32)


def dot_t(a, b):
    return lax.dot_general(a, b, (((1,), (1,)), ((), ())), preferred_element_type=F32)


def fetch(sources, targets, sems):
    copies = [pltpu.make_async_copy(s, t, sems.at[i]) for i, (s, t) in enumerate(zip(sources, targets))]
    for copy in copies:
        copy.start()
    for copy in copies:
        copy.wait()


def pack_rows(modes, f_ref, mean_ref, kl_ref, low_ref, high_ref, first_ref, last_ref):
    variables = kl_ref.shape[0]
    slabs = []
    for g in range(GROUPS):
        r, z = divmod(g, DEPTH)
        slabs.append(mean_ref[r, z : z + 1, :])
        slabs.append(kl_ref[:, r, z, :])
        slabs.append(jnp.zeros((COLS - 1 - variables, COLS), F32))
    stacked = jnp.concatenate(slabs, axis=0)
    stacked = jnp.concatenate([stacked, jnp.zeros((CELLS, LANES - COLS), F32)], axis=1)
    turned = stacked.T[:COLS]
    lane = lax.broadcasted_iota(jnp.int32, (COLS, LANES), 1)
    inside = (lane >= COEF) & (lane < COEF + variables + 1)
    behind = WIDTH - LANES
    for g in range(GROUPS):
        r, z = divmod(g, DEPTH)
        part = pltpu.roll(turned, (COEF - g * COLS) % LANES, axis=1)
        row = (low_ref, high_ref)[r]
        row[z * COLS : (z + 1) * COLS, behind:] = jnp.where(inside, part, 0.0)
    low_ref[:, :modes] = f_ref[0]
    high_ref[:, :modes] = f_ref[1]
    for g in range(GROUPS):
        r, z = divmod(g, DEPTH)
        row, at = (low_ref, high_ref)[r], z * COLS
        first_ref[g : g + 1, :] = row[at : at + 1, :]
        last_ref[g : g + 1, :] = row[at + COLS - 1 : at + COLS, :]


def modes_of(ref, modes):
    x = ref[...]
    lane = lax.broadcasted_iota(jnp.int32, x.shape, 1)
    return jnp.where(lane < modes, x, 0.0)


def coefs_of(ref):
    return ref[:, WIDTH - LANES :]


def column(coefs, k):
    return jnp.broadcast_to(coefs[:, COEF + k : COEF + k + 1], coefs.shape)


def tables(pairs_ref, pick_ref, place_ref, level_ref):
    variables, _, count = pairs_ref.shape
    mode = lax.broadcasted_iota(jnp.int32, (WIDTH, LANES), 0)
    lane = lax.broadcasted_iota(jnp.int32, (1, LANES), 1)
    used = lane < count

    def row(k, c):
        values = jnp.concatenate(
            [pairs_ref[k, c : c + 1, :], jnp.zeros((1, LANES - count), jnp.int32)], axis=1
        )
        return values

    low = jnp.where(used, row(0, 0), -1)
    low_column = jnp.broadcast_to(low, (LANES, LANES)).T
    eye = jnp.where(used & (low_column == low), 1.0, 0.0).astype(BF16)
    hot = jnp.where(mode == low, 1.0, 0.0).astype(BF16)
    pick_ref[:, :LANES] = hot
    place_ref[:LANES, :] = dot_t(eye, hot).astype(BF16)
    for k in range(variables):
        same = jnp.where(used & (low_column == row(k, 0)), 1.0, 0.0).astype(BF16)
        raised = jnp.where(mode == jnp.where(used, row(k, 1), -1), 1.0, 0.0).astype(BF16)
        levels = jnp.broadcast_to(jnp.where(used, row(k, 2), 0).astype(F32), (16, LANES)).astype(BF16)
        at = (k + 1) * LANES
        pick_ref[:, at : at + LANES] = dot_t(raised, same).astype(BF16)
        place_ref[at : at + LANES, :] = dot_t(same, raised).astype(BF16)
        level_ref[k * 8 : (k + 1) * 8, :] = jnp.sqrt(dot_t(levels, same)[:8])


def start_kernel(modes, f_hbm, mean_hbm, kl_hbm, pairs_hbm, low_ref, high_ref, first_ref, last_ref, *refs):
    given, (f_ref, mean_ref, kl_ref, pairs_ref, picked_ref, sems) = refs[:6], refs[6:]
    fetch((f_hbm, mean_hbm, kl_hbm), (f_ref, mean_ref, kl_ref), sems)
    pack_rows(modes, f_ref, mean_ref, kl_ref, low_ref, high_ref, first_ref, last_ref)

    @pl.when(early())
    def _():
        fetch((pairs_hbm,), (pairs_ref,), sems)
        inner(modes, low_ref, high_ref, pairs_ref, *given, picked_ref)


def later_kernel(modes, low_ref, high_ref, pairs_hbm, *refs):
    given, (pairs_ref, picked_ref, sems) = refs[:6], refs[6:]

    @pl.when(jnp.logical_not(early()))
    def _():
        fetch((pairs_hbm,), (pairs_ref,), sems)
        inner(modes, low_ref, high_ref, pairs_ref, *given, picked_ref)


def inner(modes, a_ref, b_ref, pairs_ref, pick_ref, place_ref, level_ref, side_ref, low_ref, center_ref, picked_ref):
    variables = pairs_ref.shape[0]
    tables(pairs_ref, pick_ref, place_ref, level_ref)

    u = jnp.concatenate([modes_of(a_ref, modes), modes_of(b_ref, modes)], axis=0)
    c = jnp.concatenate([coefs_of(a_ref), coefs_of(b_ref)], axis=0)
    both = dot(split(u), pick_ref[...])
    picked_ref[...] = both[:CELLS] + both[CELLS:]

    face_y = 0.5 * (c[:ROW_CELLS] + c[ROW_CELLS:])
    zero = jnp.zeros((COLS, LANES), F32)

    def up_z(x):
        return jnp.concatenate(
            [x[COLS:ROW_CELLS], zero, x[ROW_CELLS + COLS :], zero], axis=0
        )

    def down_z(x):
        return jnp.concatenate(
            [zero, x[: ROW_CELLS - COLS], zero, x[ROW_CELLS : CELLS - COLS]], axis=0
        )

    face_z = 0.5 * (c + up_z(c))
    cell = lax.broadcasted_iota(jnp.int32, (CELLS, LANES), 0)
    not_last = lax.rem(cell, COLS) < COLS - 1
    face_x = jnp.where(not_last, 0.5 * (c + pltpu.roll(c, CELLS - 1, axis=0)), 0.0)

    def weighted(k, dy, dz, dx):
        fy = column(face_y, k) * dy
        fz = column(face_z, k) * dz
        fx = column(face_x, k) * dx
        net = fz - down_z(fz) + fx - pltpu.roll(fx, 1, axis=0)
        return net + jnp.concatenate([fy, -fy], axis=0)

    def diffs(x):
        return (
            x[:ROW_CELLS] - x[ROW_CELLS:],
            x - up_z(x),
            x - pltpu.roll(x, CELLS - 1, axis=0),
        )

    for t in range(WIDTH // LANES):
        lanes = slice(t * LANES, (t + 1) * LANES)
        x = u[:, lanes]
        center_ref[:, lanes] = weighted(0, *diffs(x))

    low_diffs = diffs(picked_ref[:, :LANES])
    low_sum = jnp.zeros((CELLS, LANES), F32)
    for k in range(1, variables + 1):
        out = slice((k - 1) * LANES, k * LANES)
        side_ref[:, out] = weighted(k, *low_diffs)
        level = level_ref[(k - 1) * 8 : (k - 1) * 8 + 1, :]
        low_sum = low_sum + level * weighted(k, *diffs(picked_ref[:, k * LANES : (k + 1) * LANES]))
    low_ref[...] = low_sum


def inner_shapes(turned_pairs):
    shape = jax.ShapeDtypeStruct
    variables = turned_pairs.shape[0]
    blocks = (variables + 1) * LANES
    return (
        shape((WIDTH, blocks), BF16),
        shape((blocks, WIDTH), BF16),
        shape((8 * variables, LANES), F32),
        shape((CELLS, variables * LANES), F32),
        shape((CELLS, LANES), F32),
        shape((CELLS, WIDTH), F32),
    )


def start(field, mean, kl, turned_pairs):
    shape = jax.ShapeDtypeStruct
    made = inner_shapes(turned_pairs)
    return pl.pallas_call(
        functools.partial(start_kernel, field.shape[-1]),
        out_shape=(
            shape((ROW_CELLS, WIDTH), F32),
            shape((ROW_CELLS, WIDTH), F32),
            shape((GROUPS, WIDTH), F32),
            shape((GROUPS, WIDTH), F32),
        )
        + made,
        in_specs=[HBM] * 4,
        out_specs=[IN_VMEM] * 10,
        scratch_shapes=[pltpu.VMEM(x.shape, x.dtype) for x in (field, mean, kl, turned_pairs)]
        + [pltpu.VMEM((CELLS, made[0].shape[1]), F32), pltpu.SemaphoreType.DMA((3,))],
        compiler_params=pltpu.CompilerParams(vmem_limit_bytes=44 * 1024 * 1024),
        name="start",
    )(field, mean, kl, turned_pairs)


def later(modes, low, high, turned_pairs):
    made = inner_shapes(turned_pairs)
    return pl.pallas_call(
        functools.partial(later_kernel, modes),
        out_shape=made,
        in_specs=[IN_VMEM, IN_VMEM, HBM],
        out_specs=[IN_VMEM] * 6,
        scratch_shapes=[
            pltpu.VMEM(turned_pairs.shape, turned_pairs.dtype),
            pltpu.VMEM((CELLS, made[0].shape[1]), F32),
            pltpu.SemaphoreType.DMA((1,)),
        ],
        compiler_params=pltpu.CompilerParams(vmem_limit_bytes=44 * 1024 * 1024),
        name="later",
    )(low, high, turned_pairs)


def outer_kernel(modes, *refs):
    rows, parts, parts_then = refs[:6], refs[6:12], refs[12:18]
    out_ref, terms_ref = refs[18:]
    for mine, given in ((early(), parts), (jnp.logical_not(early()), parts_then)):

        @pl.when(mine)
        def _(given=given):
            outer_body(modes, *rows, *given, out_ref, terms_ref)


def outer_body(modes, low_ref, high_ref, before_ref, behind_ref, left_ref, right_ref, pick_ref, place_ref, level_ref,
               side_ref, low_sum_ref, center_ref, out_ref, terms_ref):
    variables = side_ref.shape[1] // LANES
    own = jnp.concatenate([low_ref[...], high_ref[...]], axis=0)

    def strip(x):
        at = [g * COLS for g in range(GROUPS)] + [(g + 1) * COLS - 1 for g in range(GROUPS)]
        return jnp.concatenate([x[i : i + 1] for i in at], axis=0)

    def coefs(x):
        return x[:, WIDTH - LANES :]

    mine = jnp.concatenate([own, strip(own)], axis=0)
    theirs = jnp.concatenate([before_ref[...], behind_ref[...], left_ref[...], right_ref[...]], axis=0)
    lane = lax.broadcasted_iota(jnp.int32, mine.shape, 1)
    d = jnp.where(lane < modes, mine - theirs, 0.0)
    face = 0.5 * (coefs(mine) + coefs(theirs))
    row = lax.broadcasted_iota(jnp.int32, face.shape, 0)
    end = (lax.axis_index("wide") == 0) & (row < ROW_CELLS)
    end |= (lax.axis_index("narrow") == 0) & (row >= CELLS) & (row < CELLS + GROUPS)
    face = jnp.where(end, 0.0, face)
    count = face.shape[0]

    def with_own(ref, lanes, value):
        return jnp.concatenate([ref[:, lanes] + value[:CELLS], value[CELLS:]], axis=0)

    both = dot(split(d), pick_ref[...])
    picked = both[:count] + both[count:]
    low = picked[:, :LANES]
    low_sum = jnp.zeros_like(low)
    for k in range(1, variables + 1):
        level = level_ref[(k - 1) * 8 : (k - 1) * 8 + 1, :]
        f = column(face, k)
        low_sum = low_sum + level * (f * picked[:, k * LANES : (k + 1) * LANES])
        side = level * with_own(side_ref, slice((k - 1) * LANES, k * LANES), f * low)
        terms_ref[:, k * LANES : (k + 1) * LANES] = split(side)
    terms_ref[:, :LANES] = split(with_own(low_sum_ref, slice(0, LANES), low_sum))
    spread = dot(terms_ref[...], place_ref[...])
    f = column(face, 0)
    f = jnp.concatenate([f] * (WIDTH // LANES), axis=1)
    total = f * d + spread[:count] + spread[count:]
    inner_rows = center_ref[...] + total[:CELLS]
    for r in range(ROWS):
        out_ref[r] = inner_rows[r * ROW_CELLS : (r + 1) * ROW_CELLS, :modes]
    for g in range(GROUPS):
        r, z = divmod(g, DEPTH)
        for x, i in ((0, CELLS + g), (COLS - 1, CELLS + GROUPS + g)):
            out_ref[r, z * COLS + x : z * COLS + x + 1, :] += total[i : i + 1, :modes]


def outer(modes, low, high, before, behind, left, right, parts, parts_then):
    vmem = pl.BlockSpec(memory_space=pltpu.VMEM)
    blocks = parts[0].shape[1]
    edges = (low, high, before, behind, left, right)
    return pl.pallas_call(
        functools.partial(outer_kernel, modes),
        out_shape=jax.ShapeDtypeStruct((ROWS, ROW_CELLS, modes), F32),
        in_specs=[vmem] * 18,
        out_specs=vmem,
        scratch_shapes=[pltpu.VMEM((2 * (CELLS + 2 * GROUPS), blocks), BF16)],
        compiler_params=pltpu.CompilerParams(vmem_limit_bytes=40 * 1024 * 1024),
        name="outer",
    )(*edges, *parts, *parts_then)


def held(x):
    return pltpu.with_memory_space_constraint(x, pltpu.HBM)


def shift(block, axis, by):
    size = lax.axis_size(axis)
    route = [(i, i + by) for i in range(size) if 0 <= i + by < size]
    return lax.ppermute(block, axis, route)


RUNS = 4


def early():
    return lax.rem(lax.div(lax.axis_index("wide"), 2), RUNS) == 0


def per_device(chaos_field, mean_conductivity, kl_fields, pairs):
    modes = chaos_field.shape[-1]
    field = chaos_field.reshape(ROWS, ROW_CELLS, modes)
    turned = held(pairs.transpose(0, 2, 1))
    low, high, first, last, *parts = start(held(field), held(mean_conductivity), held(kl_fields), turned)
    before = shift(high, "wide", 1)
    behind = shift(low, "wide", -1)
    left = shift(last, "narrow", 1)
    right = shift(first, "narrow", -1)
    parts_then = later(modes, low, high, turned)
    out = outer(modes, low, high, before, behind, left, right, parts, parts_then)
    return out.reshape(chaos_field.shape)


def solution(mesh):
    placed = (
        P("wide", None, "narrow", None),
        P("wide", None, "narrow"),
        P(None, "wide", None, "narrow"),
        P(),
    )
    return jax.shard_map(
        per_device,
        mesh=mesh,
        in_specs=placed,
        out_specs=P("wide", None, "narrow", None),
        check_vma=False,
    )
```

time: 30.8 us -> 29.1 us (0.945)
  the two profiles are of different devices: /device:TPU:7 before, /device:TPU:30 now
where the time goes in v3:
time: 29.1 us; the launch traced here: 28.9 us
  starting transfers between devices  17.1 us (59%)
  Pallas kernels  6.39 us (22%)
  waiting for transfers between devices  5.3 us (18%)
    ppermute x4, starting transfers between devices, shift(): return lax.ppermute(block, axis, route)  17.1 us
    ppermute x4, waiting for transfers between devices, shift(): return lax.ppermute(block, axis, route)  5.3 us
    pallas_call x1, Pallas kernels, start(): pl.pallas_call(functools.partial(start_kernel, field.shape[-1]), out_shap...  4.23 us
    pallas_call x1, Pallas kernels, outer(): pl.pallas_call(functools.partial(outer_kernel, modes), out_shape=jax.Shap...  2.13 us
  transfers between devices with their start and end apart: 4, of which 2 were waited for; matrix products, arithmetic and copies ran while one was open for 0% of the time, Pallas kernels for 0%

profile of v3, /device:TPU:30, one launch (start us, length us, event | category | flops | bytes accessed | tf_op | source)
XLA Modules:
  0.0 28.9 jit_solution(13126027115117925260)
XLA Ops:
  0.0 4.2 %start.1 = (f32[64,512]{1,0:T(8,128)S(1)}, f32[64,512]{1,0:T(8,128)S(1)}, f32[8,512]{1,0:T(8,128)S(1)}, f32[8,512]{1,0:T(8,128)S(1)}, bf16[512,1664]{1,0:T(8,128...) custom-call(f32[2,64,455]{2,1,0:T(8,128)} %bitcast.3, ...), custom_call_target="tpu_custom_call" | custom-call | tf_op jit(solution)/shard_map/start/pallas_call | solution.py:207
  4.2 9.4 %collective-permute-start.1 = (f32[64,512]{1,0:T(8,128)S(1)}, f32[64,512]{1,0:T(8,128)S(1)}, u32[]{:S(2)}, u32[]{:S(2)}) collective-permute-start(f32[64,512]{1,0:T(8,128)S(1)} %get-tuple-element.21.low_ref.refs_0_), channel_id=1, source_target_pairs={{16,0},{32,16},{48,32},{64,48},{80,64},{96,80},{112,96},{128,112},... | collective-permute-start | bytes 393224 | tf_op jit(solution)/shard_map/ppermute | solution.py:324
  13.6 1.9 %collective-permute-start = (f32[64,512]{1,0:T(8,128)S(1)}, f32[64,512]{1,0:T(8,128)S(1)}, u32[]{:S(2)}, u32[]{:S(2)}) collective-permute-start(f32[64,512]{1,0:T(8,128)S(1)} %get-tuple-element.22.high_ref.refs_1_), channel_id=1, source_target_pairs={{0,16},{16,32},{32,48},{48,64},{64,80},{80,96},{96,112},{112,128},... | collective-permute-start | bytes 393224 | tf_op jit(solution)/shard_map/ppermute | solution.py:324
  15.6 2.6 %collective-permute-start.2 = (f32[8,512]{1,0:T(8,128)S(1)}, f32[8,512]{1,0:T(8,128)S(1)}, u32[]{:S(2)}, u32[]{:S(2)}) collective-permute-start(f32[8,512]{1,0:T(8,128)S(1)} %get-tuple-element.23), channel_id=1, source_target_pairs={{0,1},{1,2},{2,3},{3,4},{4,5},{5,6},{6,7},{7,8},{8,9},{9,10},{10,1... | collective-permute-start | bytes 49160 | tf_op jit(solution)/shard_map/ppermute | solution.py:324
  18.1 3.3 %collective-permute-start.3 = (f32[8,512]{1,0:T(8,128)S(1)}, f32[8,512]{1,0:T(8,128)S(1)}, u32[]{:S(2)}, u32[]{:S(2)}) collective-permute-start(f32[8,512]{1,0:T(8,128)S(1)} %get-tuple-element.24), channel_id=1, source_target_pairs={{1,0},{2,1},{3,2},{4,3},{5,4},{6,5},{7,6},{8,7},{9,8},{10,9},{11,1... | collective-permute-start | bytes 49160 | tf_op jit(solution)/shard_map/ppermute | solution.py:324
  21.5 0.0 collective-permute-done.2.refs_4_
  21.5 4.4 %collective-permute-done.3.refs_5_ = f32[8,512]{1,0:T(8,128)S(1)} collective-permute-done((f32[8,512]{1,0:T(8,128)S(1)}, f32[8,512]{1,0:T(8,128)S(1)}, u32[]{:S(2)}, u32[]{:S(2)}) %collective-permute-start.3) | collective-permute-done | bytes 16416 | tf_op jit(solution)/shard_map/ppermute | solution.py:324
  25.9 0.0 collective-permute-done.1.refs_3_
  25.9 0.9 %collective-permute-done.refs_2_ = f32[64,512]{1,0:T(8,128)S(1)} collective-permute-done((f32[64,512]{1,0:T(8,128)S(1)}, f32[64,512]{1,0:T(8,128)S(1)}, u32[]{:S(2)}, u32[]{:S(2)}) %collective-permute-start) | collective-permute-done | bytes 131104 | tf_op jit(solution)/shard_map/ppermute | solution.py:324
  26.8 2.1 %outer.1 = f32[2,64,455]{2,1,0:T(8,128)} custom-call(f32[64,512]{1,0:T(8,128)S(1)} %get-tuple-element.21.low_ref.refs_0_, f32[64,512]{1,0:T(8,128)S(1)} %get-tuple-element.22.high_ref.refs_1_, f32[64,512]{1,0:T(8,128)S(1)} %collective-permute-done.refs_2_, f32[64,512]{1,0:T(8,128)S(1)} %collective-permute-done.1.refs_3_, ...), custom_call_target="tpu_custom_call" | custom-call | tf_op jit(solution)/shard_map/outer/pallas_call | solution.py:306
  (1 shorter events, 0.0 us)
Async XLA Ops:
  4.2 21.7 %collective-permute-start.1 = (f32[64,512]{1,0:T(8,128)S(1)}, f32[64,512]{1,0:T(8,128)S(1)}, u32[]{:S(2)}, u32[]{:S(2)}) collective-permute-start(f32[64,512]{1,0:T(8,128)S(1)} %get-tuple-element.21.low_ref.refs_0_), channel_id=1, source_target_pairs={{16,0},{32,16},{48,32},{64,48},{80,64},{96,80},{112,96},{128,112},... | collective-permute-start | bytes 393224 | tf_op jit(solution)/shard_map/ppermute | solution.py:324
  13.6 13.1 %collective-permute-start = (f32[64,512]{1,0:T(8,128)S(1)}, f32[64,512]{1,0:T(8,128)S(1)}, u32[]{:S(2)}, u32[]{:S(2)}) collective-permute-start(f32[64,512]{1,0:T(8,128)S(1)} %get-tuple-element.22.high_ref.refs_1_), channel_id=1, source_target_pairs={{0,16},{16,32},{32,48},{48,64},{64,80},{80,96},{96,112},{112,128},... | collective-permute-start | bytes 393224 | tf_op jit(solution)/shard_map/ppermute | solution.py:324
  15.6 5.9 %collective-permute-start.2 = (f32[8,512]{1,0:T(8,128)S(1)}, f32[8,512]{1,0:T(8,128)S(1)}, u32[]{:S(2)}, u32[]{:S(2)}) collective-permute-start(f32[8,512]{1,0:T(8,128)S(1)} %get-tuple-element.23), channel_id=1, source_target_pairs={{0,1},{1,2},{2,3},{3,4},{4,5},{5,6},{6,7},{7,8},{8,9},{9,10},{10,1... | collective-permute-start | bytes 49160 | tf_op jit(solution)/shard_map/ppermute | solution.py:324
  18.1 7.7 %collective-permute-start.3 = (f32[8,512]{1,0:T(8,128)S(1)}, f32[8,512]{1,0:T(8,128)S(1)}, u32[]{:S(2)}, u32[]{:S(2)}) collective-permute-start(f32[8,512]{1,0:T(8,128)S(1)} %get-tuple-element.24), channel_id=1, source_target_pairs={{1,0},{2,1},{3,2},{4,3},{5,4},{6,5},{7,6},{8,7},{9,8},{10,9},{11,1... | collective-permute-start | bytes 49160 | tf_op jit(solution)/shard_map/ppermute | solution.py:324

commit v4 on v3

--- a/solution.py
+++ b/solution.py
@@ -41,7 +41,7 @@
         copy.wait()
 
 
-def pack_rows(modes, f_ref, mean_ref, kl_ref, low_ref, high_ref, first_ref, last_ref):
+def pack_rows(modes, f_ref, mean_ref, kl_ref, low_ref, high_ref, sends, first_ref, last_ref):
     variables = kl_ref.shape[0]
     slabs = []
     for g in range(GROUPS):
@@ -62,6 +62,8 @@
         row[z * COLS : (z + 1) * COLS, behind:] = jnp.where(inside, part, 0.0)
     low_ref[:, :modes] = f_ref[0]
     high_ref[:, :modes] = f_ref[1]
+    for up, ref in zip(goes_up(), sends):
+        ref[...] = jnp.where(up, high_ref[...], low_ref[...])
     for g in range(GROUPS):
         r, z = divmod(g, DEPTH)
         row, at = (low_ref, high_ref)[r], z * COLS
@@ -111,10 +113,11 @@
         level_ref[k * 8 : (k + 1) * 8, :] = jnp.sqrt(dot_t(levels, same)[:8])
 
 
-def start_kernel(modes, f_hbm, mean_hbm, kl_hbm, pairs_hbm, low_ref, high_ref, first_ref, last_ref, *refs):
-    given, (f_ref, mean_ref, kl_ref, pairs_ref, picked_ref, sems) = refs[:6], refs[6:]
+def start_kernel(modes, f_hbm, mean_hbm, kl_hbm, pairs_hbm, low_ref, high_ref, *refs):
+    sends, (first_ref, last_ref), given = refs[:3], refs[3:5], refs[5:11]
+    f_ref, mean_ref, kl_ref, pairs_ref, picked_ref, sems = refs[11:]
     fetch((f_hbm, mean_hbm, kl_hbm), (f_ref, mean_ref, kl_ref), sems)
-    pack_rows(modes, f_ref, mean_ref, kl_ref, low_ref, high_ref, first_ref, last_ref)
+    pack_rows(modes, f_ref, mean_ref, kl_ref, low_ref, high_ref, sends, first_ref, last_ref)
 
     @pl.when(early())
     def _():
@@ -206,15 +209,9 @@
     made = inner_shapes(turned_pairs)
     return pl.pallas_call(
         functools.partial(start_kernel, field.shape[-1]),
-        out_shape=(
-            shape((ROW_CELLS, WIDTH), F32),
-            shape((ROW_CELLS, WIDTH), F32),
-            shape((GROUPS, WIDTH), F32),
-            shape((GROUPS, WIDTH), F32),
-        )
-        + made,
+        out_shape=(shape((ROW_CELLS, WIDTH), F32),) * 5 + (shape((GROUPS, WIDTH), F32),) * 2 + made,
         in_specs=[HBM] * 4,
-        out_specs=[IN_VMEM] * 10,
+        out_specs=[IN_VMEM] * 13,
         scratch_shapes=[pltpu.VMEM(x.shape, x.dtype) for x in (field, mean, kl, turned_pairs)]
         + [pltpu.VMEM((CELLS, made[0].shape[1]), F32), pltpu.SemaphoreType.DMA((3,))],
         compiler_params=pltpu.CompilerParams(vmem_limit_bytes=44 * 1024 * 1024),
@@ -240,8 +237,8 @@
 
 
 def outer_kernel(modes, *refs):
-    rows, parts, parts_then = refs[:6], refs[6:12], refs[12:18]
-    out_ref, terms_ref = refs[18:]
+    rows, parts, parts_then = refs[:9], refs[9:15], refs[15:21]
+    out_ref, terms_ref = refs[21:]
     for mine, given in ((early(), parts), (jnp.logical_not(early()), parts_then)):
 
         @pl.when(mine)
@@ -249,8 +246,9 @@
             outer_body(modes, *rows, *given, out_ref, terms_ref)
 
 
-def outer_body(modes, low_ref, high_ref, before_ref, behind_ref, left_ref, right_ref, pick_ref, place_ref, level_ref,
-               side_ref, low_sum_ref, center_ref, out_ref, terms_ref):
+def outer_body(modes, low_ref, high_ref, rows1_ref, rows2_ref, rows3_ref, left_ref, right_ref, left_then_ref,
+               right_then_ref, pick_ref, place_ref, level_ref, side_ref, low_sum_ref, center_ref,
+               out_ref, terms_ref):
     variables = side_ref.shape[1] // LANES
     own = jnp.concatenate([low_ref[...], high_ref[...]], axis=0)
 
@@ -262,7 +260,11 @@
         return x[:, WIDTH - LANES :]
 
     mine = jnp.concatenate([own, strip(own)], axis=0)
-    theirs = jnp.concatenate([before_ref[...], behind_ref[...], left_ref[...], right_ref[...]], axis=0)
+    given = (rows1_ref[...], rows2_ref[...], rows3_ref[...])
+    before, behind = (pick_from(given, which) for which in comes_in())
+    left = jnp.where(early(), left_ref[...], left_then_ref[...])
+    right = jnp.where(early(), right_ref[...], right_then_ref[...])
+    theirs = jnp.concatenate([before, behind, left, right], axis=0)
     lane = lax.broadcasted_iota(jnp.int32, mine.shape, 1)
     d = jnp.where(lane < modes, mine - theirs, 0.0)
     face = 0.5 * (coefs(mine) + coefs(theirs))
@@ -299,14 +301,14 @@
             out_ref[r, z * COLS + x : z * COLS + x + 1, :] += total[i : i + 1, :modes]
 
 
-def outer(modes, low, high, before, behind, left, right, parts, parts_then):
+def outer(modes, low, high, rows, columns, parts, parts_then):
     vmem = pl.BlockSpec(memory_space=pltpu.VMEM)
     blocks = parts[0].shape[1]
-    edges = (low, high, before, behind, left, right)
+    edges = (low, high, *rows, *columns)
     return pl.pallas_call(
         functools.partial(outer_kernel, modes),
         out_shape=jax.ShapeDtypeStruct((ROWS, ROW_CELLS, modes), F32),
-        in_specs=[vmem] * 18,
+        in_specs=[vmem] * 21,
         out_specs=vmem,
         scratch_shapes=[pltpu.VMEM((2 * (CELLS + 2 * GROUPS), blocks), BF16)],
         compiler_params=pltpu.CompilerParams(vmem_limit_bytes=40 * 1024 * 1024),
@@ -318,30 +320,73 @@
     return pltpu.with_memory_space_constraint(x, pltpu.HBM)
 
 
-def shift(block, axis, by):
-    size = lax.axis_size(axis)
-    route = [(i, i + by) for i in range(size) if 0 <= i + by < size]
-    return lax.ppermute(block, axis, route)
-
-
-RUNS = 4
+RUN = 8
+LAST = RUN - 1
 
 
 def early():
-    return lax.rem(lax.div(lax.axis_index("wide"), 2), RUNS) == 0
+    return lax.rem(lax.axis_index("wide"), RUN) < 2
+
+
+def goes_up():
+    at = lax.rem(lax.axis_index("wide"), RUN)
+    return at == LAST, (at == 0) | (at == LAST - 1), at > 0
+
+
+def comes_in():
+    at = lax.rem(lax.axis_index("wide"), RUN)
+    before = jnp.where(at == 0, 0, jnp.where((at == 1) | (at == LAST), 1, 2))
+    behind = jnp.where(at == LAST, 2, jnp.where((at == 0) | (at == LAST - 1), 1, 0))
+    return before, behind
+
+
+def pick_from(given, which):
+    return jnp.where(which == 0, given[0], jnp.where(which == 1, given[1], given[2]))
+
+
+def steps(turn, at):
+    if turn == 0:
+        return 1 if at == LAST else -1 if at >= 2 else 0
+    if turn == 1:
+        return {0: 1, 1: -1, LAST - 1: 1, LAST: -1}.get(at, 0)
+    return -1 if at == 0 else 1 if at <= LAST - 2 else 0
+
+
+def send_rows(block, turn):
+    size = lax.axis_size("wide")
+    route = [(i, i + steps(turn, i % RUN)) for i in range(size) if steps(turn, i % RUN)]
+    return lax.ppermute(block, "wide", [(i, j) for i, j in route if 0 <= j < size])
+
+
+def send_columns(block, by, is_early):
+    wide, narrow = lax.axis_size("wide"), lax.axis_size("narrow")
+    route = [
+        (w * narrow + n, w * narrow + n + by)
+        for w in range(wide)
+        for n in range(narrow)
+        if (w % RUN < 2) == is_early and 0 <= n + by < narrow
+    ]
+    return lax.ppermute(block, ("wide", "narrow"), route)
 
 
 def per_device(chaos_field, mean_conductivity, kl_fields, pairs):
     modes = chaos_field.shape[-1]
     field = chaos_field.reshape(ROWS, ROW_CELLS, modes)
     turned = held(pairs.transpose(0, 2, 1))
-    low, high, first, last, *parts = start(held(field), held(mean_conductivity), held(kl_fields), turned)
-    before = shift(high, "wide", 1)
-    behind = shift(low, "wide", -1)
-    left = shift(last, "narrow", 1)
-    right = shift(first, "narrow", -1)
+    low, high, send1, send2, send3, first, last, *parts = start(
+        held(field), held(mean_conductivity), held(kl_fields), turned
+    )
+    rows1 = send_rows(send1, 0)
+    left = send_columns(last, 1, True)
+    right = send_columns(first, -1, True)
+    rows2 = send_rows(send2, 1)
+    send3, left, right = lax.optimization_barrier((send3, left, right))
+    rows3 = send_rows(send3, 2)
+    left_then = send_columns(last, 1, False)
+    right_then = send_columns(first, -1, False)
     parts_then = later(modes, low, high, turned)
-    out = outer(modes, low, high, before, behind, left, right, parts, parts_then)
+    columns = (left, right, left_then, right_then)
+    out = outer(modes, low, high, (rows1, rows2, rows3), columns, parts, parts_then)
     return out.reshape(chaos_field.shape)
 
 

time: 29.1 us -> 32.5 us (1.12)
  the two profiles are of different devices: /device:TPU:30 before, /device:TPU:355 now
where the time goes in v4:
time: 32.5 us; the launch traced here: 32.2 us
  starting transfers between devices  25.6 us (79%)
  Pallas kernels  6.44 us (20%)
    ppermute x3, starting transfers between devices, send_rows(): lax.ppermute(block, 'wide', [(i, j) for i, j in route if 0 <= j < size])  16.9 us
    ppermute x4, starting transfers between devices, send_columns(): return lax.ppermute(block, ('wide', 'narrow'), route)  8.72 us
    pallas_call x1, Pallas kernels, later(): pl.pallas_call(functools.partial(later_kernel, modes), out_shape=made, in...  3.1 us
    pallas_call x1, Pallas kernels, outer(): pl.pallas_call(functools.partial(outer_kernel, modes), out_shape=jax.Shap...  2.16 us
    pallas_call x1, Pallas kernels, start(): pl.pallas_call(functools.partial(start_kernel, field.shape[-1]), out_shap...  1.18 us
  transfers between devices with their start and end apart: 7, of which 0 were waited for; matrix products, arithmetic and copies ran while one was open for 0% of the time, Pallas kernels for 10%

profile of v4, /device:TPU:355, one launch (start us, length us, event | category | flops | bytes accessed | tf_op | source)
XLA Modules:
  0.0 32.2 jit_solution(15174278446420219140)
XLA Ops:
  0.0 1.2 %start.1 = (f32[64,512]{1,0:T(8,128)S(1)}, f32[64,512]{1,0:T(8,128)S(1)}, f32[64,512]{1,0:T(8,128)S(1)}, f32[64,512]{1,0:T(8,128)S(1)}, f32[64,512]{1,0:T(8,128)...) custom-call(f32[2,64,455]{2,1,0:T(8,128)} %bitcast.3, ...), custom_call_target="tpu_custom_call" | custom-call | tf_op jit(solution)/shard_map/start/pallas_call | solution.py:210
  1.2 0.7 %collective-permute-start.2 = (f32[8,512]{1,0:T(8,128)S(1)}, f32[8,512]{1,0:T(8,128)S(1)}, u32[]{:S(2)}, u32[]{:S(2)}) collective-permute-start(f32[8,512]{1,0:T(8,128)S(1)} %get-tuple-element.32), channel_id=1, source_target_pairs={{0,1},{1,2},{2,3},{3,4},{4,5},{5,6},{6,7},{7,8},{8,9},{9,10},{10,1... | collective-permute-start | bytes 49160 | tf_op jit(solution)/shard_map/ppermute | solution.py:369
  1.9 0.7 %collective-permute-start.3 = (f32[8,512]{1,0:T(8,128)S(1)}, f32[8,512]{1,0:T(8,128)S(1)}, u32[]{:S(2)}, u32[]{:S(2)}) collective-permute-start(f32[8,512]{1,0:T(8,128)S(1)} %get-tuple-element.33), channel_id=1, source_target_pairs={{1,0},{2,1},{3,2},{4,3},{5,4},{6,5},{7,6},{8,7},{9,8},{10,9},{11,1... | collective-permute-start | bytes 49160 | tf_op jit(solution)/shard_map/ppermute | solution.py:369
  2.5 2.6 %collective-permute-start = (f32[64,512]{1,0:T(8,128)S(1)}, f32[64,512]{1,0:T(8,128)S(1)}, u32[]{:S(2)}, u32[]{:S(2)}) collective-permute-start(f32[64,512]{1,0:T(8,128)S(1)} %get-tuple-element.29), channel_id=1, source_target_pairs={{32,16},{48,32},{64,48},{80,64},{96,80},{112,128},{160,144},{176,1... | collective-permute-start | bytes 393224 | tf_op jit(solution)/shard_map/ppermute | solution.py:358
  5.1 0.7 %collective-permute-start.1 = (f32[64,512]{1,0:T(8,128)S(1)}, f32[64,512]{1,0:T(8,128)S(1)}, u32[]{:S(2)}, u32[]{:S(2)}) collective-permute-start(f32[64,512]{1,0:T(8,128)S(1)} %get-tuple-element.30), channel_id=1, source_target_pairs={{0,16},{16,0},{96,112},{112,96},{128,144},{144,128},{224,240},{240... | collective-permute-start | bytes 393224 | tf_op jit(solution)/shard_map/ppermute | solution.py:358
  5.8 0.0 collective-permute-done.2.refs_5_
  5.8 0.0 collective-permute-done.3.refs_6_
  5.8 13.7 %collective-permute-start.4 = (f32[64,512]{1,0:T(8,128)S(1)}, f32[64,512]{1,0:T(8,128)S(1)}, u32[]{:S(2)}, u32[]{:S(2)}) collective-permute-start(f32[64,512]{1,0:T(8,128)S(1)} %get-tuple-element.34), channel_id=1, source_target_pairs={{16,32},{32,48},{48,64},{64,80},{80,96},{128,112},{144,160},{160,1... | collective-permute-start | bytes 393224 | tf_op jit(solution)/shard_map/ppermute | solution.py:358
  19.5 1.9 %collective-permute-start.5 = (f32[8,512]{1,0:T(8,128)S(1)}, f32[8,512]{1,0:T(8,128)S(1)}, u32[]{:S(2)}, u32[]{:S(2)}) collective-permute-start(f32[8,512]{1,0:T(8,128)S(1)} %get-tuple-element.32), channel_id=1, source_target_pairs={{32,33},{33,34},{34,35},{35,36},{36,37},{37,38},{38,39},{39,40},{4... | collective-permute-start | bytes 49160 | tf_op jit(solution)/shard_map/ppermute | solution.py:369
  21.4 5.5 %collective-permute-start.6 = (f32[8,512]{1,0:T(8,128)S(1)}, f32[8,512]{1,0:T(8,128)S(1)}, u32[]{:S(2)}, u32[]{:S(2)}) collective-permute-start(f32[8,512]{1,0:T(8,128)S(1)} %get-tuple-element.33), channel_id=1, source_target_pairs={{33,32},{34,33},{35,34},{36,35},{37,36},{38,37},{39,38},{40,39},{4... | collective-permute-start | bytes 49160 | tf_op jit(solution)/shard_map/ppermute | solution.py:369
  26.9 3.1 %later.1 = (bf16[512,1664]{1,0:T(8,128)(2,1)S(1)}, bf16[1664,512]{1,0:T(8,128)(2,1)S(1)}, f32[96,128]{1,0:T(8,128)S(1)}, f32[128,1536]{1,0:T(8,128)S(1)}, f32[12...) custom-call(f32[64,512]{1,0:T(8,128)S(1)} %get-tuple-element.27.low_ref.refs_0_, ...), custom_call_target="tpu_custom_call" | custom-call | tf_op jit(solution)/shard_map/later/pallas_call | solution.py:224
  30.0 0.0 collective-permute-done.5.refs_7_
  30.0 0.0 collective-permute-done.6.refs_8_
  30.0 0.0 collective-permute-done.refs_2_
  30.0 0.0 collective-permute-done.1.refs_3_
  30.1 0.0 collective-permute-done.4.refs_4_
  30.1 2.2 %outer.1 = f32[2,64,455]{2,1,0:T(8,128)} custom-call(f32[64,512]{1,0:T(8,128)S(1)} %get-tuple-element.27.low_ref.refs_0_, f32[64,512]{1,0:T(8,128)S(1)} %get-tuple-element.28.high_ref.refs_1_, f32[64,512]{1,0:T(8,128)S(1)} %collective-permute-done.refs_2_, f32[64,512]{1,0:T(8,128)S(1)} %collective-permute-done.1.refs_3_, ...), custom_call_target="tpu_custom_call" | custom-call | tf_op jit(solution)/shard_map/outer/pallas_call | solution.py:308
Async XLA Ops:
  1.2 4.6 %collective-permute-start.2 = (f32[8,512]{1,0:T(8,128)S(1)}, f32[8,512]{1,0:T(8,128)S(1)}, u32[]{:S(2)}, u32[]{:S(2)}) collective-permute-start(f32[8,512]{1,0:T(8,128)S(1)} %get-tuple-element.32), channel_id=1, source_target_pairs={{0,1},{1,2},{2,3},{3,4},{4,5},{5,6},{6,7},{7,8},{8,9},{9,10},{10,1... | collective-permute-start | bytes 49160 | tf_op jit(solution)/shard_map/ppermute | solution.py:369
  1.9 4.0 %collective-permute-start.3 = (f32[8,512]{1,0:T(8,128)S(1)}, f32[8,512]{1,0:T(8,128)S(1)}, u32[]{:S(2)}, u32[]{:S(2)}) collective-permute-start(f32[8,512]{1,0:T(8,128)S(1)} %get-tuple-element.33), channel_id=1, source_target_pairs={{1,0},{2,1},{3,2},{4,3},{5,4},{6,5},{7,6},{8,7},{9,8},{10,9},{11,1... | collective-permute-start | bytes 49160 | tf_op jit(solution)/shard_map/ppermute | solution.py:369
  2.5 27.5 %collective-permute-start = (f32[64,512]{1,0:T(8,128)S(1)}, f32[64,512]{1,0:T(8,128)S(1)}, u32[]{:S(2)}, u32[]{:S(2)}) collective-permute-start(f32[64,512]{1,0:T(8,128)S(1)} %get-tuple-element.29), channel_id=1, source_target_pairs={{32,16},{48,32},{64,48},{80,64},{96,80},{112,128},{160,144},{176,1... | collective-permute-start | bytes 393224 | tf_op jit(solution)/shard_map/ppermute | solution.py:358
  5.1 24.9 %collective-permute-start.1 = (f32[64,512]{1,0:T(8,128)S(1)}, f32[64,512]{1,0:T(8,128)S(1)}, u32[]{:S(2)}, u32[]{:S(2)}) collective-permute-start(f32[64,512]{1,0:T(8,128)S(1)} %get-tuple-element.30), channel_id=1, source_target_pairs={{0,16},{16,0},{96,112},{112,96},{128,144},{144,128},{224,240},{240... | collective-permute-start | bytes 393224 | tf_op jit(solution)/shard_map/ppermute | solution.py:358
  5.8 24.2 %collective-permute-start.4 = (f32[64,512]{1,0:T(8,128)S(1)}, f32[64,512]{1,0:T(8,128)S(1)}, u32[]{:S(2)}, u32[]{:S(2)}) collective-permute-start(f32[64,512]{1,0:T(8,128)S(1)} %get-tuple-element.34), channel_id=1, source_target_pairs={{16,32},{32,48},{48,64},{64,80},{80,96},{128,112},{144,160},{160,1... | collective-permute-start | bytes 393224 | tf_op jit(solution)/shard_map/ppermute | solution.py:358
  19.5 10.5 %collective-permute-start.5 = (f32[8,512]{1,0:T(8,128)S(1)}, f32[8,512]{1,0:T(8,128)S(1)}, u32[]{:S(2)}, u32[]{:S(2)}) collective-permute-start(f32[8,512]{1,0:T(8,128)S(1)} %get-tuple-element.32), channel_id=1, source_target_pairs={{32,33},{33,34},{34,35},{35,36},{36,37},{37,38},{38,39},{39,40},{4... | collective-permute-start | bytes 49160 | tf_op jit(solution)/shard_map/ppermute | solution.py:369
  21.4 8.6 %collective-permute-start.6 = (f32[8,512]{1,0:T(8,128)S(1)}, f32[8,512]{1,0:T(8,128)S(1)}, u32[]{:S(2)}, u32[]{:S(2)}) collective-permute-start(f32[8,512]{1,0:T(8,128)S(1)} %get-tuple-element.33), channel_id=1, source_target_pairs={{33,32},{34,33},{35,34},{36,35},{37,36},{38,37},{39,38},{40,39},{4... | collective-permute-start | bytes 49160 | tf_op jit(solution)/shard_map/ppermute | solution.py:369

commit v5 on v4

--- a/solution.py
+++ b/solution.py
@@ -113,11 +113,14 @@
         level_ref[k * 8 : (k + 1) * 8, :] = jnp.sqrt(dot_t(levels, same)[:8])
 
 
-def start_kernel(modes, f_hbm, mean_hbm, kl_hbm, pairs_hbm, low_ref, high_ref, *refs):
-    sends, (first_ref, last_ref), given = refs[:3], refs[3:5], refs[5:11]
-    f_ref, mean_ref, kl_ref, pairs_ref, picked_ref, sems = refs[11:]
+def pack_kernel(modes, f_hbm, mean_hbm, kl_hbm, low_ref, high_ref, *refs):
+    sends, (first_ref, last_ref), (f_ref, mean_ref, kl_ref, sems) = refs[:3], refs[3:5], refs[5:]
     fetch((f_hbm, mean_hbm, kl_hbm), (f_ref, mean_ref, kl_ref), sems)
     pack_rows(modes, f_ref, mean_ref, kl_ref, low_ref, high_ref, sends, first_ref, last_ref)
+
+
+def first_kernel(modes, passed, low_ref, high_ref, pairs_hbm, *refs):
+    given, (pairs_ref, picked_ref, sems) = refs[passed : passed + 6], refs[2 * passed + 6 :]
 
     @pl.when(early())
     def _():
@@ -204,19 +207,41 @@
     )
 
 
-def start(field, mean, kl, turned_pairs):
+def pack(field, mean, kl):
     shape = jax.ShapeDtypeStruct
+    return pl.pallas_call(
+        functools.partial(pack_kernel, field.shape[-1]),
+        out_shape=(shape((ROW_CELLS, WIDTH), F32),) * 5 + (shape((GROUPS, WIDTH), F32),) * 2,
+        in_specs=[HBM] * 3,
+        out_specs=[IN_VMEM] * 7,
+        scratch_shapes=[pltpu.VMEM(x.shape, x.dtype) for x in (field, mean, kl)] + [pltpu.SemaphoreType.DMA((3,))],
+        compiler_params=pltpu.CompilerParams(vmem_limit_bytes=44 * 1024 * 1024),
+        name="pack",
+    )(field, mean, kl)
+
+
+def inner_scratch(turned_pairs, made):
+    return [
+        pltpu.VMEM(turned_pairs.shape, turned_pairs.dtype),
+        pltpu.VMEM((CELLS, made[0].shape[1]), F32),
+        pltpu.SemaphoreType.DMA((1,)),
+    ]
+
+
+def first_work(modes, low, high, turned_pairs, sends):
     made = inner_shapes(turned_pairs)
-    return pl.pallas_call(
-        functools.partial(start_kernel, field.shape[-1]),
-        out_shape=(shape((ROW_CELLS, WIDTH), F32),) * 5 + (shape((GROUPS, WIDTH), F32),) * 2 + made,
-        in_specs=[HBM] * 4,
-        out_specs=[IN_VMEM] * 13,
-        scratch_shapes=[pltpu.VMEM(x.shape, x.dtype) for x in (field, mean, kl, turned_pairs)]
-        + [pltpu.VMEM((CELLS, made[0].shape[1]), F32), pltpu.SemaphoreType.DMA((3,))],
+    anywhere = pl.BlockSpec(memory_space=pl.ANY)
+    out = pl.pallas_call(
+        functools.partial(first_kernel, modes, len(sends)),
+        out_shape=made + tuple(jax.ShapeDtypeStruct(x.shape, x.dtype) for x in sends),
+        in_specs=[IN_VMEM, IN_VMEM, HBM] + [anywhere] * len(sends),
+        out_specs=[IN_VMEM] * 6 + [anywhere] * len(sends),
+        scratch_shapes=inner_scratch(turned_pairs, made),
+        input_output_aliases={3 + i: 6 + i for i in range(len(sends))},
         compiler_params=pltpu.CompilerParams(vmem_limit_bytes=44 * 1024 * 1024),
-        name="start",
-    )(field, mean, kl, turned_pairs)
+        name="first_work",
+    )(low, high, turned_pairs, *sends)
+    return out[:6], out[6:]
 
 
 def later(modes, low, high, turned_pairs):
@@ -226,11 +251,7 @@
         out_shape=made,
         in_specs=[IN_VMEM, IN_VMEM, HBM],
         out_specs=[IN_VMEM] * 6,
-        scratch_shapes=[
-            pltpu.VMEM(turned_pairs.shape, turned_pairs.dtype),
-            pltpu.VMEM((CELLS, made[0].shape[1]), F32),
-            pltpu.SemaphoreType.DMA((1,)),
-        ],
+        scratch_shapes=inner_scratch(turned_pairs, made),
         compiler_params=pltpu.CompilerParams(vmem_limit_bytes=44 * 1024 * 1024),
         name="later",
     )(low, high, turned_pairs)
@@ -330,13 +351,13 @@
 
 def goes_up():
     at = lax.rem(lax.axis_index("wide"), RUN)
-    return at == LAST, (at == 0) | (at == LAST - 1), at > 0
+    return at == LAST, at != 1, (at > 0) & (at < LAST)
 
 
 def comes_in():
     at = lax.rem(lax.axis_index("wide"), RUN)
-    before = jnp.where(at == 0, 0, jnp.where((at == 1) | (at == LAST), 1, 2))
-    behind = jnp.where(at == LAST, 2, jnp.where((at == 0) | (at == LAST - 1), 1, 0))
+    before = jnp.where(at == 0, 0, jnp.where((at == 1) | (at >= LAST - 1), 1, 2))
+    behind = jnp.where(at >= LAST - 1, 2, jnp.where(at == 0, 1, 0))
     return before, behind
 
 
@@ -348,8 +369,8 @@
     if turn == 0:
         return 1 if at == LAST else -1 if at >= 2 else 0
     if turn == 1:
-        return {0: 1, 1: -1, LAST - 1: 1, LAST: -1}.get(at, 0)
-    return -1 if at == 0 else 1 if at <= LAST - 2 else 0
+        return {0: 1, 1: -1, LAST - 2: 1, LAST - 1: 1}.get(at, 0)
+    return -1 if at in (0, LAST) else 1 if at < LAST - 2 else 0
 
 
 def send_rows(block, turn):
@@ -373,14 +394,13 @@
     modes = chaos_field.shape[-1]
     field = chaos_field.reshape(ROWS, ROW_CELLS, modes)
     turned = held(pairs.transpose(0, 2, 1))
-    low, high, send1, send2, send3, first, last, *parts = start(
-        held(field), held(mean_conductivity), held(kl_fields), turned
-    )
+    low, high, send1, send2, send3, first, last = pack(held(field), held(mean_conductivity), held(kl_fields))
     rows1 = send_rows(send1, 0)
+    parts, (send2, send3, first, last) = first_work(modes, low, high, turned, (send2, send3, first, last))
     left = send_columns(last, 1, True)
     right = send_columns(first, -1, True)
     rows2 = send_rows(send2, 1)
-    send3, left, right = lax.optimization_barrier((send3, left, right))
+    send3, left, right, rows1 = lax.optimization_barrier((send3, left, right, rows1))
     rows3 = send_rows(send3, 2)
     left_then = send_columns(last, 1, False)
     right_then = send_columns(first, -1, False)

time: 32.5 us -> 31.5 us (0.969)
  the two profiles are of different devices: /device:TPU:355 before, /device:TPU:154 now
where the time goes in v5:
time: 31.5 us; the launch traced here: 31.3 us
  starting transfers between devices  23.6 us (75%)
  Pallas kernels  6.43 us (20%)
  waiting for transfers between devices  1.13 us (4%)
    ppermute x3, starting transfers between devices, send_rows(): lax.ppermute(block, 'wide', [(i, j) for i, j in route if 0 <= j < size])  16.4 us
    ppermute x4, starting transfers between devices, send_columns(): return lax.ppermute(block, ('wide', 'narrow'), route)  7.17 us
    pallas_call x1, Pallas kernels, later(): pl.pallas_call(functools.partial(later_kernel, modes), out_shape=made, in...  3.1 us
    pallas_call x1, Pallas kernels, outer(): pl.pallas_call(functools.partial(outer_kernel, modes), out_shape=jax.Shap...  2.13 us
    pallas_call x1, Pallas kernels, pack(): pl.pallas_call(functools.partial(pack_kernel, field.shape[-1]), out_shape...  1.18 us
    ppermute x4, waiting for transfers between devices, send_columns(): return lax.ppermute(block, ('wide', 'narrow'), route)  0.7 us
  transfers between devices with their start and end apart: 7, of which 2 were waited for; matrix products, arithmetic and copies ran while one was open for 0% of the time, Pallas kernels for 10%

profile of v5, /device:TPU:154, one launch (start us, length us, event | category | flops | bytes accessed | tf_op | source)
XLA Modules:
  0.0 31.3 jit_solution(7434560628628786403)
XLA Ops:
  0.0 1.2 %pack.1 = (f32[64,512]{1,0:T(8,128)S(1)}, f32[64,512]{1,0:T(8,128)S(1)}, f32[64,512]{1,0:T(8,128)S(1)}, f32[64,512]{1,0:T(8,128)S(1)}, f32[64,512]{1,0:T(8,128)S...) custom-call(f32[2,64,455]{2,1,0:T(8,128)} %bitcast.3, f32[2,4,16]{2,1,0:T(4,128)} %mean_hbm.1, f32[12,2,4,16]{3,2,1,0:T(4,128)} %kl_hbm.1), custom_call_target="tpu_custom_call" | custom-call | tf_op jit(solution)/shard_map/pack/pallas_call | solution.py:212
  1.2 1.9 %collective-permute-start.2 = (f32[64,512]{1,0:T(8,128)S(1)}, f32[64,512]{1,0:T(8,128)S(1)}, u32[]{:S(2)}, u32[]{:S(2)}) collective-permute-start(f32[64,512]{1,0:T(8,128)S(1)} %get-tuple-element.41), channel_id=1, source_target_pairs={{32,16},{48,32},{64,48},{80,64},{96,80},{112,128},{160,144},{176,1... | collective-permute-start | bytes 393224 | tf_op jit(solution)/shard_map/ppermute | solution.py:379
  3.2 0.7 %collective-permute-start = (f32[8,512]{1,0:T(8,128)S(1)}, f32[8,512]{1,0:T(8,128)S(1)}, u32[]{:S(2)}, u32[]{:S(2)}) collective-permute-start(f32[8,512]{1,0:T(8,128)S(1)} %get-tuple-element.39), channel_id=1, source_target_pairs={{0,1},{1,2},{2,3},{3,4},{4,5},{5,6},{6,7},{7,8},{8,9},{9,10},{10,1... | collective-permute-start | bytes 49160 | tf_op jit(solution)/shard_map/ppermute | solution.py:390
  3.8 0.7 %collective-permute-start.1 = (f32[8,512]{1,0:T(8,128)S(1)}, f32[8,512]{1,0:T(8,128)S(1)}, u32[]{:S(2)}, u32[]{:S(2)}) collective-permute-start(f32[8,512]{1,0:T(8,128)S(1)} %get-tuple-element.40), channel_id=1, source_target_pairs={{1,0},{2,1},{3,2},{4,3},{5,4},{6,5},{7,6},{8,7},{9,8},{10,9},{11,1... | collective-permute-start | bytes 49160 | tf_op jit(solution)/shard_map/ppermute | solution.py:390
  4.5 0.7 %collective-permute-start.3 = (f32[64,512]{1,0:T(8,128)S(1)}, f32[64,512]{1,0:T(8,128)S(1)}, u32[]{:S(2)}, u32[]{:S(2)}) collective-permute-start(f32[64,512]{1,0:T(8,128)S(1)} %get-tuple-element.43), channel_id=1, source_target_pairs={{0,16},{16,0},{80,96},{96,112},{128,144},{144,128},{208,224},{224,... | collective-permute-start | bytes 393224 | tf_op jit(solution)/shard_map/ppermute | solution.py:379
  5.2 0.0 collective-permute-done.refs_5_
  5.2 0.0 collective-permute-done.1.refs_6_
  5.2 0.4 %collective-permute-done.2.refs_2_ = f32[64,512]{1,0:T(8,128)S(1)} collective-permute-done((f32[64,512]{1,0:T(8,128)S(1)}, f32[64,512]{1,0:T(8,128)S(1)}, u32[]{:S(2)}, u32[]{:S(2)}) %collective-permute-start.2) | collective-permute-done | bytes 131104 | tf_op jit(solution)/shard_map/ppermute | solution.py:379
  5.6 13.8 %collective-permute-start.4 = (f32[64,512]{1,0:T(8,128)S(1)}, f32[64,512]{1,0:T(8,128)S(1)}, u32[]{:S(2)}, u32[]{:S(2)}) collective-permute-start(f32[64,512]{1,0:T(8,128)S(1)} %get-tuple-element.44), channel_id=1, source_target_pairs={{16,32},{32,48},{48,64},{64,80},{112,96},{128,112},{144,160},{160,... | collective-permute-start | bytes 393224 | tf_op jit(solution)/shard_map/ppermute | solution.py:379
  19.5 1.9 %collective-permute-start.5 = (f32[8,512]{1,0:T(8,128)S(1)}, f32[8,512]{1,0:T(8,128)S(1)}, u32[]{:S(2)}, u32[]{:S(2)}) collective-permute-start(f32[8,512]{1,0:T(8,128)S(1)} %get-tuple-element.39), channel_id=1, source_target_pairs={{32,33},{33,34},{34,35},{35,36},{36,37},{37,38},{38,39},{39,40},{4... | collective-permute-start | bytes 49160 | tf_op jit(solution)/shard_map/ppermute | solution.py:390
  21.4 3.9 %collective-permute-start.6 = (f32[8,512]{1,0:T(8,128)S(1)}, f32[8,512]{1,0:T(8,128)S(1)}, u32[]{:S(2)}, u32[]{:S(2)}) collective-permute-start(f32[8,512]{1,0:T(8,128)S(1)} %get-tuple-element.40), channel_id=1, source_target_pairs={{33,32},{34,33},{35,34},{36,35},{37,36},{38,37},{39,38},{40,39},{4... | collective-permute-start | bytes 49160 | tf_op jit(solution)/shard_map/ppermute | solution.py:390
  25.3 3.1 %later.1 = (bf16[512,1664]{1,0:T(8,128)(2,1)S(1)}, bf16[1664,512]{1,0:T(8,128)(2,1)S(1)}, f32[96,128]{1,0:T(8,128)S(1)}, f32[128,1536]{1,0:T(8,128)S(1)}, f32[12...) custom-call(f32[64,512]{1,0:T(8,128)S(1)} %get-tuple-element.32.low_ref.refs_0_, ...), custom_call_target="tpu_custom_call" | custom-call | tf_op jit(solution)/shard_map/later/pallas_call | solution.py:249
  28.4 0.0 collective-permute-done.5.refs_7_
  28.4 0.7 %collective-permute-done.6.refs_8_ = f32[8,512]{1,0:T(8,128)S(1)} collective-permute-done((f32[8,512]{1,0:T(8,128)S(1)}, f32[8,512]{1,0:T(8,128)S(1)}, u32[]{:S(2)}, u32[]{:S(2)}) %collective-permute-start.6) | collective-permute-done | bytes 16416 | tf_op jit(solution)/shard_map/ppermute | solution.py:390
  29.1 0.0 collective-permute-done.3.refs_3_
  29.1 0.0 collective-permute-done.4.refs_4_
  29.1 2.1 %outer.1 = f32[2,64,455]{2,1,0:T(8,128)} custom-call(f32[64,512]{1,0:T(8,128)S(1)} %get-tuple-element.32.low_ref.refs_0_, f32[64,512]{1,0:T(8,128)S(1)} %get-tuple-element.33.high_ref.refs_1_, f32[64,512]{1,0:T(8,128)S(1)} %collective-permute-done.2.refs_2_, f32[64,512]{1,0:T(8,128)S(1)} %collective-permute-done.3.refs_3_, ...), custom_call_target="tpu_custom_call" | custom-call | tf_op jit(solution)/shard_map/outer/pallas_call | solution.py:329
  (1 shorter events, 0.0 us)
Async XLA Ops:
  1.2 4.4 %collective-permute-start.2 = (f32[64,512]{1,0:T(8,128)S(1)}, f32[64,512]{1,0:T(8,128)S(1)}, u32[]{:S(2)}, u32[]{:S(2)}) collective-permute-start(f32[64,512]{1,0:T(8,128)S(1)} %get-tuple-element.41), channel_id=1, source_target_pairs={{32,16},{48,32},{64,48},{80,64},{96,80},{112,128},{160,144},{176,1... | collective-permute-start | bytes 393224 | tf_op jit(solution)/shard_map/ppermute | solution.py:379
  3.2 2.0 %collective-permute-start = (f32[8,512]{1,0:T(8,128)S(1)}, f32[8,512]{1,0:T(8,128)S(1)}, u32[]{:S(2)}, u32[]{:S(2)}) collective-permute-start(f32[8,512]{1,0:T(8,128)S(1)} %get-tuple-element.39), channel_id=1, source_target_pairs={{0,1},{1,2},{2,3},{3,4},{4,5},{5,6},{6,7},{7,8},{8,9},{9,10},{10,1... | collective-permute-start | bytes 49160 | tf_op jit(solution)/shard_map/ppermute | solution.py:390
  3.8 1.4 %collective-permute-start.1 = (f32[8,512]{1,0:T(8,128)S(1)}, f32[8,512]{1,0:T(8,128)S(1)}, u32[]{:S(2)}, u32[]{:S(2)}) collective-permute-start(f32[8,512]{1,0:T(8,128)S(1)} %get-tuple-element.40), channel_id=1, source_target_pairs={{1,0},{2,1},{3,2},{4,3},{5,4},{6,5},{7,6},{8,7},{9,8},{10,9},{11,1... | collective-permute-start | bytes 49160 | tf_op jit(solution)/shard_map/ppermute | solution.py:390
  4.5 24.6 %collective-permute-start.3 = (f32[64,512]{1,0:T(8,128)S(1)}, f32[64,512]{1,0:T(8,128)S(1)}, u32[]{:S(2)}, u32[]{:S(2)}) collective-permute-start(f32[64,512]{1,0:T(8,128)S(1)} %get-tuple-element.43), channel_id=1, source_target_pairs={{0,16},{16,0},{80,96},{96,112},{128,144},{144,128},{208,224},{224,... | collective-permute-start | bytes 393224 | tf_op jit(solution)/shard_map/ppermute | solution.py:379
  5.6 23.5 %collective-permute-start.4 = (f32[64,512]{1,0:T(8,128)S(1)}, f32[64,512]{1,0:T(8,128)S(1)}, u32[]{:S(2)}, u32[]{:S(2)}) collective-permute-start(f32[64,512]{1,0:T(8,128)S(1)} %get-tuple-element.44), channel_id=1, source_target_pairs={{16,32},{32,48},{48,64},{64,80},{112,96},{128,112},{144,160},{160,... | collective-permute-start | bytes 393224 | tf_op jit(solution)/shard_map/ppermute | solution.py:379
  19.5 9.0 %collective-permute-start.5 = (f32[8,512]{1,0:T(8,128)S(1)}, f32[8,512]{1,0:T(8,128)S(1)}, u32[]{:S(2)}, u32[]{:S(2)}) collective-permute-start(f32[8,512]{1,0:T(8,128)S(1)} %get-tuple-element.39), channel_id=1, source_target_pairs={{32,33},{33,34},{34,35},{35,36},{36,37},{37,38},{38,39},{39,40},{4... | collective-permute-start | bytes 49160 | tf_op jit(solution)/shard_map/ppermute | solution.py:390
  21.4 7.7 %collective-permute-start.6 = (f32[8,512]{1,0:T(8,128)S(1)}, f32[8,512]{1,0:T(8,128)S(1)}, u32[]{:S(2)}, u32[]{:S(2)}) collective-permute-start(f32[8,512]{1,0:T(8,128)S(1)} %get-tuple-element.40), channel_id=1, source_target_pairs={{33,32},{34,33},{35,34},{36,35},{37,36},{38,37},{39,38},{40,39},{4... | collective-permute-start | bytes 49160 | tf_op jit(solution)/shard_map/ppermute | solution.py:390

commit v6 on v5

--- a/solution.py
+++ b/solution.py
@@ -283,8 +283,8 @@
     mine = jnp.concatenate([own, strip(own)], axis=0)
     given = (rows1_ref[...], rows2_ref[...], rows3_ref[...])
     before, behind = (pick_from(given, which) for which in comes_in())
-    left = jnp.where(early(), left_ref[...], left_then_ref[...])
-    right = jnp.where(early(), right_ref[...], right_then_ref[...])
+    left = jnp.where(columns_late(), left_then_ref[...], left_ref[...])
+    right = jnp.where(columns_late(), right_then_ref[...], right_ref[...])
     theirs = jnp.concatenate([before, behind, left, right], axis=0)
     lane = lax.broadcasted_iota(jnp.int32, mine.shape, 1)
     d = jnp.where(lane < modes, mine - theirs, 0.0)
@@ -349,14 +349,19 @@
     return lax.rem(lax.axis_index("wide"), RUN) < 2
 
 
+def columns_late():
+    at = lax.rem(lax.axis_index("wide"), RUN)
+    return (at == 2) | (at == LAST)
+
+
 def goes_up():
     at = lax.rem(lax.axis_index("wide"), RUN)
-    return at == LAST, at != 1, (at > 0) & (at < LAST)
+    return at == LAST, at != 1, at == 1
 
 
 def comes_in():
     at = lax.rem(lax.axis_index("wide"), RUN)
-    before = jnp.where(at == 0, 0, jnp.where((at == 1) | (at >= LAST - 1), 1, 2))
+    before = jnp.where(at == 0, 0, jnp.where(at == 2, 2, 1))
     behind = jnp.where(at >= LAST - 1, 2, jnp.where(at == 0, 1, 0))
     return before, behind
 
@@ -369,8 +374,8 @@
     if turn == 0:
         return 1 if at == LAST else -1 if at >= 2 else 0
     if turn == 1:
-        return {0: 1, 1: -1, LAST - 2: 1, LAST - 1: 1}.get(at, 0)
-    return -1 if at in (0, LAST) else 1 if at < LAST - 2 else 0
+        return -1 if at == 1 else 1 if at < LAST else 0
+    return {0: -1, 1: 1, LAST: -1}.get(at, 0)
 
 
 def send_rows(block, turn):
@@ -379,13 +384,13 @@
     return lax.ppermute(block, "wide", [(i, j) for i, j in route if 0 <= j < size])
 
 
-def send_columns(block, by, is_early):
+def send_columns(block, by, is_late):
     wide, narrow = lax.axis_size("wide"), lax.axis_size("narrow")
     route = [
         (w * narrow + n, w * narrow + n + by)
         for w in range(wide)
         for n in range(narrow)
-        if (w % RUN < 2) == is_early and 0 <= n + by < narrow
+        if (w % RUN in (2, LAST)) == is_late and 0 <= n + by < narrow
     ]
     return lax.ppermute(block, ("wide", "narrow"), route)
 
@@ -397,13 +402,13 @@
     low, high, send1, send2, send3, first, last = pack(held(field), held(mean_conductivity), held(kl_fields))
     rows1 = send_rows(send1, 0)
     parts, (send2, send3, first, last) = first_work(modes, low, high, turned, (send2, send3, first, last))
-    left = send_columns(last, 1, True)
-    right = send_columns(first, -1, True)
+    left = send_columns(last, 1, False)
+    right = send_columns(first, -1, False)
     rows2 = send_rows(send2, 1)
     send3, left, right, rows1 = lax.optimization_barrier((send3, left, right, rows1))
     rows3 = send_rows(send3, 2)
-    left_then = send_columns(last, 1, False)
-    right_then = send_columns(first, -1, False)
+    left_then = send_columns(last, 1, True)
+    right_then = send_columns(first, -1, True)
     parts_then = later(modes, low, high, turned)
     columns = (left, right, left_then, right_then)
     out = outer(modes, low, high, (rows1, rows2, rows3), columns, parts, parts_then)

time: 31.5 us -> 32.9 us (1.044)
  the two profiles are of different devices: /device:TPU:154 before, /device:TPU:487 now
where the time goes in v6:
time: 32.9 us; the launch traced here: 32.6 us
  starting transfers between devices  26 us (79%)
  Pallas kernels  6.46 us (20%)
    ppermute x3, starting transfers between devices, send_rows(): lax.ppermute(block, 'wide', [(i, j) for i, j in route if 0 <= j < size])  16 us
    ppermute x4, starting transfers between devices, send_columns(): return lax.ppermute(block, ('wide', 'narrow'), route)  9.97 us
    pallas_call x1, Pallas kernels, later(): pl.pallas_call(functools.partial(later_kernel, modes), out_shape=made, in...  3.1 us
    pallas_call x1, Pallas kernels, outer(): pl.pallas_call(functools.partial(outer_kernel, modes), out_shape=jax.Shap...  2.16 us
    pallas_call x1, Pallas kernels, pack(): pl.pallas_call(functools.partial(pack_kernel, field.shape[-1]), out_shape...  1.18 us
  transfers between devices with their start and end apart: 7, of which 0 were waited for; matrix products, arithmetic and copies ran while one was open for 0% of the time, Pallas kernels for 10%

profile of v6, /device:TPU:487, one launch (start us, length us, event | category | flops | bytes accessed | tf_op | source)
XLA Modules:
  0.0 32.6 jit_solution(13630853889687898109)
XLA Ops:
  0.0 1.2 %pack.1 = (f32[64,512]{1,0:T(8,128)S(1)}, f32[64,512]{1,0:T(8,128)S(1)}, f32[64,512]{1,0:T(8,128)S(1)}, f32[64,512]{1,0:T(8,128)S(1)}, f32[64,512]{1,0:T(8,128)S...) custom-call(f32[2,64,455]{2,1,0:T(8,128)} %bitcast.3, f32[2,4,16]{2,1,0:T(4,128)} %mean_hbm.1, f32[12,2,4,16]{3,2,1,0:T(4,128)} %kl_hbm.1), custom_call_target="tpu_custom_call" | custom-call | tf_op jit(solution)/shard_map/pack/pallas_call | solution.py:212
  1.2 0.7 %collective-permute-start.2 = (f32[64,512]{1,0:T(8,128)S(1)}, f32[64,512]{1,0:T(8,128)S(1)}, u32[]{:S(2)}, u32[]{:S(2)}) collective-permute-start(f32[64,512]{1,0:T(8,128)S(1)} %get-tuple-element.41), channel_id=1, source_target_pairs={{32,16},{48,32},{64,48},{80,64},{96,80},{112,128},{160,144},{176,1... | collective-permute-start | bytes 393224 | tf_op jit(solution)/shard_map/ppermute | solution.py:384
  1.9 0.7 %collective-permute-start = (f32[8,512]{1,0:T(8,128)S(1)}, f32[8,512]{1,0:T(8,128)S(1)}, u32[]{:S(2)}, u32[]{:S(2)}) collective-permute-start(f32[8,512]{1,0:T(8,128)S(1)} %get-tuple-element.39), channel_id=1, source_target_pairs={{0,1},{1,2},{2,3},{3,4},{4,5},{5,6},{6,7},{7,8},{8,9},{9,10},{10,1... | collective-permute-start | bytes 49160 | tf_op jit(solution)/shard_map/ppermute | solution.py:395
  2.6 0.7 %collective-permute-start.1 = (f32[8,512]{1,0:T(8,128)S(1)}, f32[8,512]{1,0:T(8,128)S(1)}, u32[]{:S(2)}, u32[]{:S(2)}) collective-permute-start(f32[8,512]{1,0:T(8,128)S(1)} %get-tuple-element.40), channel_id=1, source_target_pairs={{1,0},{2,1},{3,2},{4,3},{5,4},{6,5},{7,6},{8,7},{9,8},{10,9},{11,1... | collective-permute-start | bytes 49160 | tf_op jit(solution)/shard_map/ppermute | solution.py:395
  3.2 1.3 %collective-permute-start.3 = (f32[64,512]{1,0:T(8,128)S(1)}, f32[64,512]{1,0:T(8,128)S(1)}, u32[]{:S(2)}, u32[]{:S(2)}) collective-permute-start(f32[64,512]{1,0:T(8,128)S(1)} %get-tuple-element.43), channel_id=1, source_target_pairs={{0,16},{16,0},{32,48},{48,64},{64,80},{80,96},{96,112},{128,144},{... | collective-permute-start | bytes 393224 | tf_op jit(solution)/shard_map/ppermute | solution.py:384
  4.5 0.0 collective-permute-done.refs_5_
  4.6 0.0 collective-permute-done.1.refs_6_
  4.6 0.0 collective-permute-done.2.refs_2_
  4.6 14.1 %collective-permute-start.4 = (f32[64,512]{1,0:T(8,128)S(1)}, f32[64,512]{1,0:T(8,128)S(1)}, u32[]{:S(2)}, u32[]{:S(2)}) collective-permute-start(f32[64,512]{1,0:T(8,128)S(1)} %get-tuple-element.44), channel_id=1, source_target_pairs={{16,32},{112,96},{128,112},{144,160},{240,224},{256,240},{272,288}... | collective-permute-start | bytes 393224 | tf_op jit(solution)/shard_map/ppermute | solution.py:384
  18.7 2.4 %collective-permute-start.5 = (f32[8,512]{1,0:T(8,128)S(1)}, f32[8,512]{1,0:T(8,128)S(1)}, u32[]{:S(2)}, u32[]{:S(2)}) collective-permute-start(f32[8,512]{1,0:T(8,128)S(1)} %get-tuple-element.39), channel_id=1, source_target_pairs={{32,33},{33,34},{34,35},{35,36},{36,37},{37,38},{38,39},{39,40},{4... | collective-permute-start | bytes 49160 | tf_op jit(solution)/shard_map/ppermute | solution.py:395
  21.1 6.2 %collective-permute-start.6 = (f32[8,512]{1,0:T(8,128)S(1)}, f32[8,512]{1,0:T(8,128)S(1)}, u32[]{:S(2)}, u32[]{:S(2)}) collective-permute-start(f32[8,512]{1,0:T(8,128)S(1)} %get-tuple-element.40), channel_id=1, source_target_pairs={{33,32},{34,33},{35,34},{36,35},{37,36},{38,37},{39,38},{40,39},{4... | collective-permute-start | bytes 49160 | tf_op jit(solution)/shard_map/ppermute | solution.py:395
  27.3 3.1 %later.1 = (bf16[512,1664]{1,0:T(8,128)(2,1)S(1)}, bf16[1664,512]{1,0:T(8,128)(2,1)S(1)}, f32[96,128]{1,0:T(8,128)S(1)}, f32[128,1536]{1,0:T(8,128)S(1)}, f32[12...) custom-call(f32[64,512]{1,0:T(8,128)S(1)} %get-tuple-element.32.low_ref.refs_0_, ...), custom_call_target="tpu_custom_call" | custom-call | tf_op jit(solution)/shard_map/later/pallas_call | solution.py:249
  30.4 0.0 collective-permute-done.5.refs_7_
  30.4 0.0 collective-permute-done.6.refs_8_
  30.4 0.0 collective-permute-done.3.refs_3_
  30.5 0.0 collective-permute-done.4.refs_4_
  30.5 2.2 %outer.1 = f32[2,64,455]{2,1,0:T(8,128)} custom-call(f32[64,512]{1,0:T(8,128)S(1)} %get-tuple-element.32.low_ref.refs_0_, f32[64,512]{1,0:T(8,128)S(1)} %get-tuple-element.33.high_ref.refs_1_, f32[64,512]{1,0:T(8,128)S(1)} %collective-permute-done.2.refs_2_, f32[64,512]{1,0:T(8,128)S(1)} %collective-permute-done.3.refs_3_, ...), custom_call_target="tpu_custom_call" | custom-call | tf_op jit(solution)/shard_map/outer/pallas_call | solution.py:329
  (1 shorter events, 0.0 us)
Async XLA Ops:
  1.2 3.4 %collective-permute-start.2 = (f32[64,512]{1,0:T(8,128)S(1)}, f32[64,512]{1,0:T(8,128)S(1)}, u32[]{:S(2)}, u32[]{:S(2)}) collective-permute-start(f32[64,512]{1,0:T(8,128)S(1)} %get-tuple-element.41), channel_id=1, source_target_pairs={{32,16},{48,32},{64,48},{80,64},{96,80},{112,128},{160,144},{176,1... | collective-permute-start | bytes 393224 | tf_op jit(solution)/shard_map/ppermute | solution.py:384
  1.9 2.6 %collective-permute-start = (f32[8,512]{1,0:T(8,128)S(1)}, f32[8,512]{1,0:T(8,128)S(1)}, u32[]{:S(2)}, u32[]{:S(2)}) collective-permute-start(f32[8,512]{1,0:T(8,128)S(1)} %get-tuple-element.39), channel_id=1, source_target_pairs={{0,1},{1,2},{2,3},{3,4},{4,5},{5,6},{6,7},{7,8},{8,9},{9,10},{10,1... | collective-permute-start | bytes 49160 | tf_op jit(solution)/shard_map/ppermute | solution.py:395
  2.6 2.0 %collective-permute-start.1 = (f32[8,512]{1,0:T(8,128)S(1)}, f32[8,512]{1,0:T(8,128)S(1)}, u32[]{:S(2)}, u32[]{:S(2)}) collective-permute-start(f32[8,512]{1,0:T(8,128)S(1)} %get-tuple-element.40), channel_id=1, source_target_pairs={{1,0},{2,1},{3,2},{4,3},{5,4},{6,5},{7,6},{8,7},{9,8},{10,9},{11,1... | collective-permute-start | bytes 49160 | tf_op jit(solution)/shard_map/ppermute | solution.py:395
  3.2 27.2 %collective-permute-start.3 = (f32[64,512]{1,0:T(8,128)S(1)}, f32[64,512]{1,0:T(8,128)S(1)}, u32[]{:S(2)}, u32[]{:S(2)}) collective-permute-start(f32[64,512]{1,0:T(8,128)S(1)} %get-tuple-element.43), channel_id=1, source_target_pairs={{0,16},{16,0},{32,48},{48,64},{64,80},{80,96},{96,112},{128,144},{... | collective-permute-start | bytes 393224 | tf_op jit(solution)/shard_map/ppermute | solution.py:384
  4.6 25.9 %collective-permute-start.4 = (f32[64,512]{1,0:T(8,128)S(1)}, f32[64,512]{1,0:T(8,128)S(1)}, u32[]{:S(2)}, u32[]{:S(2)}) collective-permute-start(f32[64,512]{1,0:T(8,128)S(1)} %get-tuple-element.44), channel_id=1, source_target_pairs={{16,32},{112,96},{128,112},{144,160},{240,224},{256,240},{272,288}... | collective-permute-start | bytes 393224 | tf_op jit(solution)/shard_map/ppermute | solution.py:384
  18.7 11.8 %collective-permute-start.5 = (f32[8,512]{1,0:T(8,128)S(1)}, f32[8,512]{1,0:T(8,128)S(1)}, u32[]{:S(2)}, u32[]{:S(2)}) collective-permute-start(f32[8,512]{1,0:T(8,128)S(1)} %get-tuple-element.39), channel_id=1, source_target_pairs={{32,33},{33,34},{34,35},{35,36},{36,37},{37,38},{38,39},{39,40},{4... | collective-permute-start | bytes 49160 | tf_op jit(solution)/shard_map/ppermute | solution.py:395
  21.1 9.4 %collective-permute-start.6 = (f32[8,512]{1,0:T(8,128)S(1)}, f32[8,512]{1,0:T(8,128)S(1)}, u32[]{:S(2)}, u32[]{:S(2)}) collective-permute-start(f32[8,512]{1,0:T(8,128)S(1)} %get-tuple-element.40), channel_id=1, source_target_pairs={{33,32},{34,33},{35,34},{36,35},{37,36},{38,37},{39,38},{40,39},{4... | collective-permute-start | bytes 49160 | tf_op jit(solution)/shard_map/ppermute | solution.py:395

commit v7 on v3

--- a/solution.py
+++ b/solution.py
@@ -111,10 +111,12 @@
         level_ref[k * 8 : (k + 1) * 8, :] = jnp.sqrt(dot_t(levels, same)[:8])
 
 
-def start_kernel(modes, f_hbm, mean_hbm, kl_hbm, pairs_hbm, low_ref, high_ref, first_ref, last_ref, *refs):
+def start_kernel(modes, f_hbm, mean_hbm, kl_hbm, pairs_hbm, low_ref, high_ref, again_ref, first_ref, last_ref, *refs):
     given, (f_ref, mean_ref, kl_ref, pairs_ref, picked_ref, sems) = refs[:6], refs[6:]
     fetch((f_hbm, mean_hbm, kl_hbm), (f_ref, mean_ref, kl_ref), sems)
     pack_rows(modes, f_ref, mean_ref, kl_ref, low_ref, high_ref, first_ref, last_ref)
+
+    again_ref[...] = high_ref[...]
 
     @pl.when(early())
     def _():
@@ -209,12 +211,13 @@
         out_shape=(
             shape((ROW_CELLS, WIDTH), F32),
             shape((ROW_CELLS, WIDTH), F32),
+            shape((ROW_CELLS, WIDTH), F32),
             shape((GROUPS, WIDTH), F32),
             shape((GROUPS, WIDTH), F32),
         )
         + made,
         in_specs=[HBM] * 4,
-        out_specs=[IN_VMEM] * 10,
+        out_specs=[IN_VMEM] * 11,
         scratch_shapes=[pltpu.VMEM(x.shape, x.dtype) for x in (field, mean, kl, turned_pairs)]
         + [pltpu.VMEM((CELLS, made[0].shape[1]), F32), pltpu.SemaphoreType.DMA((3,))],
         compiler_params=pltpu.CompilerParams(vmem_limit_bytes=44 * 1024 * 1024),
@@ -240,8 +243,8 @@
 
 
 def outer_kernel(modes, *refs):
-    rows, parts, parts_then = refs[:6], refs[6:12], refs[12:18]
-    out_ref, terms_ref = refs[18:]
+    rows, parts, parts_then = refs[:7], refs[7:13], refs[13:19]
+    out_ref, terms_ref = refs[19:]
     for mine, given in ((early(), parts), (jnp.logical_not(early()), parts_then)):
 
         @pl.when(mine)
@@ -249,8 +252,8 @@
             outer_body(modes, *rows, *given, out_ref, terms_ref)
 
 
-def outer_body(modes, low_ref, high_ref, before_ref, behind_ref, left_ref, right_ref, pick_ref, place_ref, level_ref,
-               side_ref, low_sum_ref, center_ref, out_ref, terms_ref):
+def outer_body(modes, low_ref, high_ref, run_ref, before_ref, behind_ref, left_ref, right_ref, pick_ref, place_ref,
+               level_ref, side_ref, low_sum_ref, center_ref, out_ref, terms_ref):
     variables = side_ref.shape[1] // LANES
     own = jnp.concatenate([low_ref[...], high_ref[...]], axis=0)
 
@@ -262,7 +265,8 @@
         return x[:, WIDTH - LANES :]
 
     mine = jnp.concatenate([own, strip(own)], axis=0)
-    theirs = jnp.concatenate([before_ref[...], behind_ref[...], left_ref[...], right_ref[...]], axis=0)
+    before = jnp.where(lax.rem(lax.axis_index("wide"), RUN) == 0, run_ref[...], before_ref[...])
+    theirs = jnp.concatenate([before, behind_ref[...], left_ref[...], right_ref[...]], axis=0)
     lane = lax.broadcasted_iota(jnp.int32, mine.shape, 1)
     d = jnp.where(lane < modes, mine - theirs, 0.0)
     face = 0.5 * (coefs(mine) + coefs(theirs))
@@ -299,14 +303,14 @@
             out_ref[r, z * COLS + x : z * COLS + x + 1, :] += total[i : i + 1, :modes]
 
 
-def outer(modes, low, high, before, behind, left, right, parts, parts_then):
+def outer(modes, low, high, before_run, before, behind, left, right, parts, parts_then):
     vmem = pl.BlockSpec(memory_space=pltpu.VMEM)
     blocks = parts[0].shape[1]
-    edges = (low, high, before, behind, left, right)
+    edges = (low, high, before_run, before, behind, left, right)
     return pl.pallas_call(
         functools.partial(outer_kernel, modes),
         out_shape=jax.ShapeDtypeStruct((ROWS, ROW_CELLS, modes), F32),
-        in_specs=[vmem] * 18,
+        in_specs=[vmem] * 19,
         out_specs=vmem,
         scratch_shapes=[pltpu.VMEM((2 * (CELLS + 2 * GROUPS), blocks), BF16)],
         compiler_params=pltpu.CompilerParams(vmem_limit_bytes=40 * 1024 * 1024),
@@ -318,30 +322,33 @@
     return pltpu.with_memory_space_constraint(x, pltpu.HBM)
 
 
-def shift(block, axis, by):
+def shift(block, axis, by, ends=None):
     size = lax.axis_size(axis)
     route = [(i, i + by) for i in range(size) if 0 <= i + by < size]
+    if ends is not None:
+        route = [(i, j) for i, j in route if (i % RUN == RUN - 1) == ends]
     return lax.ppermute(block, axis, route)
 
 
-RUNS = 4
+RUN = 8
 
 
 def early():
-    return lax.rem(lax.div(lax.axis_index("wide"), 2), RUNS) == 0
+    return lax.rem(lax.axis_index("wide"), RUN) < 2
 
 
 def per_device(chaos_field, mean_conductivity, kl_fields, pairs):
     modes = chaos_field.shape[-1]
     field = chaos_field.reshape(ROWS, ROW_CELLS, modes)
     turned = held(pairs.transpose(0, 2, 1))
-    low, high, first, last, *parts = start(held(field), held(mean_conductivity), held(kl_fields), turned)
-    before = shift(high, "wide", 1)
+    low, high, again, first, last, *parts = start(held(field), held(mean_conductivity), held(kl_fields), turned)
+    before_run = shift(again, "wide", 1, ends=True)
+    before = shift(high, "wide", 1, ends=False)
     behind = shift(low, "wide", -1)
     left = shift(last, "narrow", 1)
     right = shift(first, "narrow", -1)
     parts_then = later(modes, low, high, turned)
-    out = outer(modes, low, high, before, behind, left, right, parts, parts_then)
+    out = outer(modes, low, high, before_run, before, behind, left, right, parts, parts_then)
     return out.reshape(chaos_field.shape)
 
 

time: 29.1 us -> 29.6 us (1.017)
  the two profiles are of different devices: /device:TPU:30 before, /device:TPU:92 now
where the time goes in v7:
time: 29.6 us; the launch traced here: 29.3 us
  starting transfers between devices  17.5 us (59%)
  Pallas kernels  6.39 us (22%)
  waiting for transfers between devices  5.34 us (18%)
    ppermute x5, starting transfers between devices, shift(): return lax.ppermute(block, axis, route)  17.5 us
    ppermute x5, waiting for transfers between devices, shift(): return lax.ppermute(block, axis, route)  5.34 us
    pallas_call x1, Pallas kernels, start(): pl.pallas_call(functools.partial(start_kernel, field.shape[-1]), out_shap...  4.23 us
    pallas_call x1, Pallas kernels, outer(): pl.pallas_call(functools.partial(outer_kernel, modes), out_shape=jax.Shap...  2.14 us
  transfers between devices with their start and end apart: 5, of which 1 were waited for; matrix products, arithmetic and copies ran while one was open for 0% of the time, Pallas kernels for 0%

profile of v7, /device:TPU:92, one launch (start us, length us, event | category | flops | bytes accessed | tf_op | source)
XLA Modules:
  0.0 29.3 jit_solution(1649843532245002638)
XLA Ops:
  0.0 4.2 %start.1 = (f32[64,512]{1,0:T(8,128)S(1)}, f32[64,512]{1,0:T(8,128)S(1)}, f32[64,512]{1,0:T(8,128)S(1)}, f32[8,512]{1,0:T(8,128)S(1)}, f32[8,512]{1,0:T(8,128)S(...) custom-call(f32[2,64,455]{2,1,0:T(8,128)} %bitcast.3, ...), custom_call_target="tpu_custom_call" | custom-call | tf_op jit(solution)/shard_map/start/pallas_call | solution.py:209
  4.2 1.3 %collective-permute-start = (f32[64,512]{1,0:T(8,128)S(1)}, f32[64,512]{1,0:T(8,128)S(1)}, u32[]{:S(2)}, u32[]{:S(2)}) collective-permute-start(f32[64,512]{1,0:T(8,128)S(1)} %get-tuple-element.24), channel_id=1, source_target_pairs={{112,128},{240,256},{368,384},{113,129},{241,257},{369,385},{114,1... | collective-permute-start | bytes 393224 | tf_op jit(solution)/shard_map/ppermute | solution.py:330
  5.5 9.1 %collective-permute-start.2 = (f32[64,512]{1,0:T(8,128)S(1)}, f32[64,512]{1,0:T(8,128)S(1)}, u32[]{:S(2)}, u32[]{:S(2)}) collective-permute-start(f32[64,512]{1,0:T(8,128)S(1)} %get-tuple-element.22.low_ref.refs_0_), channel_id=1, source_target_pairs={{16,0},{32,16},{48,32},{64,48},{80,64},{96,80},{112,96},{128,112},... | collective-permute-start | bytes 393224 | tf_op jit(solution)/shard_map/ppermute | solution.py:330
  14.6 1.3 %collective-permute-start.1 = (f32[64,512]{1,0:T(8,128)S(1)}, f32[64,512]{1,0:T(8,128)S(1)}, u32[]{:S(2)}, u32[]{:S(2)}) collective-permute-start(f32[64,512]{1,0:T(8,128)S(1)} %get-tuple-element.23.high_ref.refs_1_), channel_id=1, source_target_pairs={{0,16},{16,32},{32,48},{48,64},{64,80},{80,96},{96,112},{128,144},... | collective-permute-start | bytes 393224 | tf_op jit(solution)/shard_map/ppermute | solution.py:330
  15.9 3.5 %collective-permute-start.3 = (f32[8,512]{1,0:T(8,128)S(1)}, f32[8,512]{1,0:T(8,128)S(1)}, u32[]{:S(2)}, u32[]{:S(2)}) collective-permute-start(f32[8,512]{1,0:T(8,128)S(1)} %get-tuple-element.25), channel_id=1, source_target_pairs={{0,1},{1,2},{2,3},{3,4},{4,5},{5,6},{6,7},{7,8},{8,9},{9,10},{10,1... | collective-permute-start | bytes 49160 | tf_op jit(solution)/shard_map/ppermute | solution.py:330
  19.4 2.4 %collective-permute-start.4 = (f32[8,512]{1,0:T(8,128)S(1)}, f32[8,512]{1,0:T(8,128)S(1)}, u32[]{:S(2)}, u32[]{:S(2)}) collective-permute-start(f32[8,512]{1,0:T(8,128)S(1)} %get-tuple-element.26), channel_id=1, source_target_pairs={{1,0},{2,1},{3,2},{4,3},{5,4},{6,5},{7,6},{8,7},{9,8},{10,9},{11,1... | collective-permute-start | bytes 49160 | tf_op jit(solution)/shard_map/ppermute | solution.py:330
  21.8 0.0 collective-permute-done.3.refs_5_
  21.8 5.3 %collective-permute-done.4.refs_6_ = f32[8,512]{1,0:T(8,128)S(1)} collective-permute-done((f32[8,512]{1,0:T(8,128)S(1)}, f32[8,512]{1,0:T(8,128)S(1)}, u32[]{:S(2)}, u32[]{:S(2)}) %collective-permute-start.4) | collective-permute-done | bytes 16416 | tf_op jit(solution)/shard_map/ppermute | solution.py:330
  27.2 0.0 collective-permute-done.refs_2_
  27.2 0.0 collective-permute-done.2.refs_4_
  27.2 0.0 collective-permute-done.1.refs_3_
  27.2 2.1 %outer.1 = f32[2,64,455]{2,1,0:T(8,128)} custom-call(f32[64,512]{1,0:T(8,128)S(1)} %get-tuple-element.22.low_ref.refs_0_, f32[64,512]{1,0:T(8,128)S(1)} %get-tuple-element.23.high_ref.refs_1_, f32[64,512]{1,0:T(8,128)S(1)} %collective-permute-done.refs_2_, f32[64,512]{1,0:T(8,128)S(1)} %collective-permute-done.1.refs_3_, ...), custom_call_target="tpu_custom_call" | custom-call | tf_op jit(solution)/shard_map/outer/pallas_call | solution.py:310
  (1 shorter events, 0.0 us)
Async XLA Ops:
  4.2 22.9 %collective-permute-start = (f32[64,512]{1,0:T(8,128)S(1)}, f32[64,512]{1,0:T(8,128)S(1)}, u32[]{:S(2)}, u32[]{:S(2)}) collective-permute-start(f32[64,512]{1,0:T(8,128)S(1)} %get-tuple-element.24), channel_id=1, source_target_pairs={{112,128},{240,256},{368,384},{113,129},{241,257},{369,385},{114,1... | collective-permute-start | bytes 393224 | tf_op jit(solution)/shard_map/ppermute | solution.py:330
  5.5 21.6 %collective-permute-start.2 = (f32[64,512]{1,0:T(8,128)S(1)}, f32[64,512]{1,0:T(8,128)S(1)}, u32[]{:S(2)}, u32[]{:S(2)}) collective-permute-start(f32[64,512]{1,0:T(8,128)S(1)} %get-tuple-element.22.low_ref.refs_0_), channel_id=1, source_target_pairs={{16,0},{32,16},{48,32},{64,48},{80,64},{96,80},{112,96},{128,112},... | collective-permute-start | bytes 393224 | tf_op jit(solution)/shard_map/ppermute | solution.py:330
  14.6 12.6 %collective-permute-start.1 = (f32[64,512]{1,0:T(8,128)S(1)}, f32[64,512]{1,0:T(8,128)S(1)}, u32[]{:S(2)}, u32[]{:S(2)}) collective-permute-start(f32[64,512]{1,0:T(8,128)S(1)} %get-tuple-element.23.high_ref.refs_1_), channel_id=1, source_target_pairs={{0,16},{16,32},{32,48},{48,64},{64,80},{80,96},{96,112},{128,144},... | collective-permute-start | bytes 393224 | tf_op jit(solution)/shard_map/ppermute | solution.py:330
  15.9 5.9 %collective-permute-start.3 = (f32[8,512]{1,0:T(8,128)S(1)}, f32[8,512]{1,0:T(8,128)S(1)}, u32[]{:S(2)}, u32[]{:S(2)}) collective-permute-start(f32[8,512]{1,0:T(8,128)S(1)} %get-tuple-element.25), channel_id=1, source_target_pairs={{0,1},{1,2},{2,3},{3,4},{4,5},{5,6},{6,7},{7,8},{8,9},{9,10},{10,1... | collective-permute-start | bytes 49160 | tf_op jit(solution)/shard_map/ppermute | solution.py:330
  19.4 7.7 %collective-permute-start.4 = (f32[8,512]{1,0:T(8,128)S(1)}, f32[8,512]{1,0:T(8,128)S(1)}, u32[]{:S(2)}, u32[]{:S(2)}) collective-permute-start(f32[8,512]{1,0:T(8,128)S(1)} %get-tuple-element.26), channel_id=1, source_target_pairs={{1,0},{2,1},{3,2},{4,3},{5,4},{6,5},{7,6},{8,7},{9,8},{10,9},{11,1... | collective-permute-start | bytes 49160 | tf_op jit(solution)/shard_map/ppermute | solution.py:330

commit v8 on v3

--- a/solution.py
+++ b/solution.py
@@ -111,10 +111,15 @@
         level_ref[k * 8 : (k + 1) * 8, :] = jnp.sqrt(dot_t(levels, same)[:8])
 
 
-def start_kernel(modes, f_hbm, mean_hbm, kl_hbm, pairs_hbm, low_ref, high_ref, first_ref, last_ref, *refs):
-    given, (f_ref, mean_ref, kl_ref, pairs_ref, picked_ref, sems) = refs[:6], refs[6:]
+def start_kernel(modes, f_hbm, mean_hbm, kl_hbm, pairs_hbm, low_ref, high_ref, rows1_ref, rows2_ref, columns1_ref, columns2_ref, *refs):
+    given, (f_ref, mean_ref, kl_ref, pairs_ref, picked_ref, first_ref, last_ref, sems) = refs[:6], refs[6:]
     fetch((f_hbm, mean_hbm, kl_hbm), (f_ref, mean_ref, kl_ref), sems)
     pack_rows(modes, f_ref, mean_ref, kl_ref, low_ref, high_ref, first_ref, last_ref)
+    low, high, first, last = low_ref[...], high_ref[...], first_ref[...], last_ref[...]
+    rows1_ref[...] = jnp.where(odd("wide"), high, low)
+    rows2_ref[...] = jnp.where(odd("wide"), low, high)
+    columns1_ref[...] = jnp.where(odd("narrow"), last, first)
+    columns2_ref[...] = jnp.where(odd("narrow"), first, last)
 
     @pl.when(early())
     def _():
@@ -206,17 +211,14 @@
     made = inner_shapes(turned_pairs)
     return pl.pallas_call(
         functools.partial(start_kernel, field.shape[-1]),
-        out_shape=(
-            shape((ROW_CELLS, WIDTH), F32),
-            shape((ROW_CELLS, WIDTH), F32),
-            shape((GROUPS, WIDTH), F32),
-            shape((GROUPS, WIDTH), F32),
-        )
+        out_shape=(shape((ROW_CELLS, WIDTH), F32),) * 4 + (shape((GROUPS, WIDTH), F32),) * 2
         + made,
         in_specs=[HBM] * 4,
-        out_specs=[IN_VMEM] * 10,
+        out_specs=[IN_VMEM] * 12,
         scratch_shapes=[pltpu.VMEM(x.shape, x.dtype) for x in (field, mean, kl, turned_pairs)]
-        + [pltpu.VMEM((CELLS, made[0].shape[1]), F32), pltpu.SemaphoreType.DMA((3,))],
+        + [pltpu.VMEM((CELLS, made[0].shape[1]), F32)]
+        + [pltpu.VMEM((GROUPS, WIDTH), F32)] * 2
+        + [pltpu.SemaphoreType.DMA((3,))],
         compiler_params=pltpu.CompilerParams(vmem_limit_bytes=44 * 1024 * 1024),
         name="start",
     )(field, mean, kl, turned_pairs)
@@ -235,6 +237,7 @@
             pltpu.SemaphoreType.DMA((1,)),
         ],
         compiler_params=pltpu.CompilerParams(vmem_limit_bytes=44 * 1024 * 1024),
+        cost_estimate=pl.CostEstimate(flops=2_000_000_000, bytes_accessed=10_000_000, transcendentals=0),
         name="later",
     )(low, high, turned_pairs)
 
@@ -249,7 +252,7 @@
             outer_body(modes, *rows, *given, out_ref, terms_ref)
 
 
-def outer_body(modes, low_ref, high_ref, before_ref, behind_ref, left_ref, right_ref, pick_ref, place_ref, level_ref,
+def outer_body(modes, low_ref, high_ref, rows1_ref, rows2_ref, columns1_ref, columns2_ref, pick_ref, place_ref, level_ref,
                side_ref, low_sum_ref, center_ref, out_ref, terms_ref):
     variables = side_ref.shape[1] // LANES
     own = jnp.concatenate([low_ref[...], high_ref[...]], axis=0)
@@ -262,7 +265,11 @@
         return x[:, WIDTH - LANES :]
 
     mine = jnp.concatenate([own, strip(own)], axis=0)
-    theirs = jnp.concatenate([before_ref[...], behind_ref[...], left_ref[...], right_ref[...]], axis=0)
+    before = jnp.where(odd("wide"), rows2_ref[...], rows1_ref[...])
+    behind = jnp.where(odd("wide"), rows1_ref[...], rows2_ref[...])
+    left = jnp.where(odd("narrow"), columns2_ref[...], columns1_ref[...])
+    right = jnp.where(odd("narrow"), columns1_ref[...], columns2_ref[...])
+    theirs = jnp.concatenate([before, behind, left, right], axis=0)
     lane = lax.broadcasted_iota(jnp.int32, mine.shape, 1)
     d = jnp.where(lane < modes, mine - theirs, 0.0)
     face = 0.5 * (coefs(mine) + coefs(theirs))
@@ -299,10 +306,10 @@
             out_ref[r, z * COLS + x : z * COLS + x + 1, :] += total[i : i + 1, :modes]
 
 
-def outer(modes, low, high, before, behind, left, right, parts, parts_then):
+def outer(modes, low, high, rows1, rows2, columns1, columns2, parts, parts_then):
     vmem = pl.BlockSpec(memory_space=pltpu.VMEM)
     blocks = parts[0].shape[1]
-    edges = (low, high, before, behind, left, right)
+    edges = (low, high, rows1, rows2, columns1, columns2)
     return pl.pallas_call(
         functools.partial(outer_kernel, modes),
         out_shape=jax.ShapeDtypeStruct((ROWS, ROW_CELLS, modes), F32),
@@ -318,9 +325,14 @@
     return pltpu.with_memory_space_constraint(x, pltpu.HBM)
 
 
-def shift(block, axis, by):
-    size = lax.axis_size(axis)
-    route = [(i, i + by) for i in range(size) if 0 <= i + by < size]
+def odd(axis):
+    return lax.rem(lax.axis_index(axis), 2) == 1
+
+
+def swap(block, axis, first):
+    route = []
+    for i in range(first, lax.axis_size(axis) - 1, 2):
+        route += [(i, i + 1), (i + 1, i)]
     return lax.ppermute(block, axis, route)
 
 
@@ -335,13 +347,15 @@
     modes = chaos_field.shape[-1]
     field = chaos_field.reshape(ROWS, ROW_CELLS, modes)
     turned = held(pairs.transpose(0, 2, 1))
-    low, high, first, last, *parts = start(held(field), held(mean_conductivity), held(kl_fields), turned)
-    before = shift(high, "wide", 1)
-    behind = shift(low, "wide", -1)
-    left = shift(last, "narrow", 1)
-    right = shift(first, "narrow", -1)
+    low, high, rows1, rows2, columns1, columns2, *parts = start(
+        held(field), held(mean_conductivity), held(kl_fields), turned
+    )
+    rows1 = swap(rows1, "wide", 1)
+    columns1 = swap(columns1, "narrow", 1)
+    columns2 = swap(columns2, "narrow", 0)
+    rows2 = swap(rows2, "wide", 0)
     parts_then = later(modes, low, high, turned)
-    out = outer(modes, low, high, before, behind, left, right, parts, parts_then)
+    out = outer(modes, low, high, rows1, rows2, columns1, columns2, parts, parts_then)
     return out.reshape(chaos_field.shape)
 
 

time: 29.1 us -> 29.2 us (level)
  the two profiles are of different devices: /device:TPU:30 before, /device:TPU:6 now
where the time goes in v8:
time: 29.2 us; the launch traced here: 29 us
  starting transfers between devices  17.7 us (61%)
  Pallas kernels  6.43 us (22%)
  waiting for transfers between devices  4.76 us (16%)
    ppermute x4, starting transfers between devices, swap(): return lax.ppermute(block, axis, route)  17.7 us
    ppermute x4, waiting for transfers between devices, swap(): return lax.ppermute(block, axis, route)  4.76 us
    pallas_call x1, Pallas kernels, start(): pl.pallas_call(functools.partial(start_kernel, field.shape[-1]), out_shap...  4.24 us
    pallas_call x1, Pallas kernels, outer(): pl.pallas_call(functools.partial(outer_kernel, modes), out_shape=jax.Shap...  2.16 us
  transfers between devices with their start and end apart: 4, of which 1 were waited for; matrix products, arithmetic and copies ran while one was open for 0% of the time, Pallas kernels for 0%

profile of v8, /device:TPU:6, one launch (start us, length us, event | category | flops | bytes accessed | tf_op | source)
XLA Modules:
  0.0 29.0 jit_solution(16920368676949750694)
XLA Ops:
  0.0 4.2 %start.1 = (f32[64,512]{1,0:T(8,128)S(1)}, f32[64,512]{1,0:T(8,128)S(1)}, f32[64,512]{1,0:T(8,128)S(1)}, f32[64,512]{1,0:T(8,128)S(1)}, f32[8,512]{1,0:T(8,128)S...) custom-call(f32[2,64,455]{2,1,0:T(8,128)} %bitcast.3, ...), custom_call_target="tpu_custom_call" | custom-call | tf_op jit(solution)/shard_map/start/pallas_call | solution.py:212
  4.2 0.7 %collective-permute-start.2 = (f32[8,512]{1,0:T(8,128)S(1)}, f32[8,512]{1,0:T(8,128)S(1)}, u32[]{:S(2)}, u32[]{:S(2)}) collective-permute-start(f32[8,512]{1,0:T(8,128)S(1)} %get-tuple-element.27), channel_id=1, source_target_pairs={{1,2},{2,1},{3,4},{4,3},{5,6},{6,5},{7,8},{8,7},{9,10},{10,9},{11,... | collective-permute-start | bytes 49160 | tf_op jit(solution)/shard_map/ppermute | solution.py:336
  4.9 6.3 %collective-permute-start.3 = (f32[8,512]{1,0:T(8,128)S(1)}, f32[8,512]{1,0:T(8,128)S(1)}, u32[]{:S(2)}, u32[]{:S(2)}) collective-permute-start(f32[8,512]{1,0:T(8,128)S(1)} %get-tuple-element.28), channel_id=1, source_target_pairs={{0,1},{1,0},{2,3},{3,2},{4,5},{5,4},{6,7},{7,6},{8,9},{9,8},{10,11... | collective-permute-start | bytes 49160 | tf_op jit(solution)/shard_map/ppermute | solution.py:336
  11.2 8.8 %collective-permute-start = (f32[64,512]{1,0:T(8,128)S(1)}, f32[64,512]{1,0:T(8,128)S(1)}, u32[]{:S(2)}, u32[]{:S(2)}) collective-permute-start(f32[64,512]{1,0:T(8,128)S(1)} %get-tuple-element.25), channel_id=1, source_target_pairs={{16,32},{32,16},{48,64},{64,48},{80,96},{96,80},{112,128},{128,112... | collective-permute-start | bytes 393224 | tf_op jit(solution)/shard_map/ppermute | solution.py:336
  20.1 1.9 %collective-permute-start.1 = (f32[64,512]{1,0:T(8,128)S(1)}, f32[64,512]{1,0:T(8,128)S(1)}, u32[]{:S(2)}, u32[]{:S(2)}) collective-permute-start(f32[64,512]{1,0:T(8,128)S(1)} %get-tuple-element.26), channel_id=1, source_target_pairs={{0,16},{16,0},{32,48},{48,32},{64,80},{80,64},{96,112},{112,96},{1... | collective-permute-start | bytes 393224 | tf_op jit(solution)/shard_map/ppermute | solution.py:336
  22.0 0.0 collective-permute-done.2.refs_4_
  22.0 0.0 collective-permute-done.3.refs_5_
  22.1 4.8 %collective-permute-done.refs_2_ = f32[64,512]{1,0:T(8,128)S(1)} collective-permute-done((f32[64,512]{1,0:T(8,128)S(1)}, f32[64,512]{1,0:T(8,128)S(1)}, u32[]{:S(2)}, u32[]{:S(2)}) %collective-permute-start) | collective-permute-done | bytes 131104 | tf_op jit(solution)/shard_map/ppermute | solution.py:336
  26.8 0.0 collective-permute-done.1.refs_3_
  26.8 2.2 %outer.1 = f32[2,64,455]{2,1,0:T(8,128)} custom-call(f32[64,512]{1,0:T(8,128)S(1)} %get-tuple-element.23.low_ref.refs_0_, f32[64,512]{1,0:T(8,128)S(1)} %get-tuple-element.24.high_ref.refs_1_, f32[64,512]{1,0:T(8,128)S(1)} %collective-permute-done.refs_2_, f32[64,512]{1,0:T(8,128)S(1)} %collective-permute-done.1.refs_3_, ...), custom_call_target="tpu_custom_call" | custom-call | tf_op jit(solution)/shard_map/outer/pallas_call | solution.py:313
  (1 shorter events, 0.0 us)
Async XLA Ops:
  4.2 17.8 %collective-permute-start.2 = (f32[8,512]{1,0:T(8,128)S(1)}, f32[8,512]{1,0:T(8,128)S(1)}, u32[]{:S(2)}, u32[]{:S(2)}) collective-permute-start(f32[8,512]{1,0:T(8,128)S(1)} %get-tuple-element.27), channel_id=1, source_target_pairs={{1,2},{2,1},{3,4},{4,3},{5,6},{6,5},{7,8},{8,7},{9,10},{10,9},{11,... | collective-permute-start | bytes 49160 | tf_op jit(solution)/shard_map/ppermute | solution.py:336
  4.9 17.1 %collective-permute-start.3 = (f32[8,512]{1,0:T(8,128)S(1)}, f32[8,512]{1,0:T(8,128)S(1)}, u32[]{:S(2)}, u32[]{:S(2)}) collective-permute-start(f32[8,512]{1,0:T(8,128)S(1)} %get-tuple-element.28), channel_id=1, source_target_pairs={{0,1},{1,0},{2,3},{3,2},{4,5},{5,4},{6,7},{7,6},{8,9},{9,8},{10,11... | collective-permute-start | bytes 49160 | tf_op jit(solution)/shard_map/ppermute | solution.py:336
  11.2 15.6 %collective-permute-start = (f32[64,512]{1,0:T(8,128)S(1)}, f32[64,512]{1,0:T(8,128)S(1)}, u32[]{:S(2)}, u32[]{:S(2)}) collective-permute-start(f32[64,512]{1,0:T(8,128)S(1)} %get-tuple-element.25), channel_id=1, source_target_pairs={{16,32},{32,16},{48,64},{64,48},{80,96},{96,80},{112,128},{128,112... | collective-permute-start | bytes 393224 | tf_op jit(solution)/shard_map/ppermute | solution.py:336
  20.1 6.7 %collective-permute-start.1 = (f32[64,512]{1,0:T(8,128)S(1)}, f32[64,512]{1,0:T(8,128)S(1)}, u32[]{:S(2)}, u32[]{:S(2)}) collective-permute-start(f32[64,512]{1,0:T(8,128)S(1)} %get-tuple-element.26), channel_id=1, source_target_pairs={{0,16},{16,0},{32,48},{48,32},{64,80},{80,64},{96,112},{112,96},{1... | collective-permute-start | bytes 393224 | tf_op jit(solution)/shard_map/ppermute | solution.py:336

commit v9 on v8

--- a/solution.py
+++ b/solution.py
@@ -237,7 +237,6 @@
             pltpu.SemaphoreType.DMA((1,)),
         ],
         compiler_params=pltpu.CompilerParams(vmem_limit_bytes=44 * 1024 * 1024),
-        cost_estimate=pl.CostEstimate(flops=2_000_000_000, bytes_accessed=10_000_000, transcendentals=0),
         name="later",
     )(low, high, turned_pairs)
 

time: 29.2 us -> 28.1 us (0.962)
  the two profiles are of different devices: /device:TPU:6 before, /device:TPU:38 now
where the time goes in v9:
time: 28.1 us; the launch traced here: 27.8 us
  starting transfers between devices  17.7 us (63%)
  Pallas kernels  6.42 us (23%)
  waiting for transfers between devices  3.67 us (13%)
    ppermute x4, starting transfers between devices, swap(): return lax.ppermute(block, axis, route)  17.7 us
    pallas_call x1, Pallas kernels, start(): pl.pallas_call(functools.partial(start_kernel, field.shape[-1]), out_shap...  4.24 us
    ppermute x4, waiting for transfers between devices, swap(): return lax.ppermute(block, axis, route)  3.67 us
    pallas_call x1, Pallas kernels, outer(): pl.pallas_call(functools.partial(outer_kernel, modes), out_shape=jax.Shap...  2.15 us
  transfers between devices with their start and end apart: 4, of which 2 were waited for; matrix products, arithmetic and copies ran while one was open for 0% of the time, Pallas kernels for 0%

profile of v9, /device:TPU:38, one launch (start us, length us, event | category | flops | bytes accessed | tf_op | source)
XLA Modules:
  0.0 27.8 jit_solution(13994530597881095085)
XLA Ops:
  0.0 4.2 %start.1 = (f32[64,512]{1,0:T(8,128)S(1)}, f32[64,512]{1,0:T(8,128)S(1)}, f32[64,512]{1,0:T(8,128)S(1)}, f32[64,512]{1,0:T(8,128)S(1)}, f32[8,512]{1,0:T(8,128)S...) custom-call(f32[2,64,455]{2,1,0:T(8,128)} %bitcast.3, ...), custom_call_target="tpu_custom_call" | custom-call | tf_op jit(solution)/shard_map/start/pallas_call | solution.py:212
  4.2 8.5 %collective-permute-start = (f32[64,512]{1,0:T(8,128)S(1)}, f32[64,512]{1,0:T(8,128)S(1)}, u32[]{:S(2)}, u32[]{:S(2)}) collective-permute-start(f32[64,512]{1,0:T(8,128)S(1)} %get-tuple-element.25), channel_id=1, source_target_pairs={{16,32},{32,16},{48,64},{64,48},{80,96},{96,80},{112,128},{128,112... | collective-permute-start | bytes 393224 | tf_op jit(solution)/shard_map/ppermute | solution.py:335
  12.7 1.9 %collective-permute-start.1 = (f32[64,512]{1,0:T(8,128)S(1)}, f32[64,512]{1,0:T(8,128)S(1)}, u32[]{:S(2)}, u32[]{:S(2)}) collective-permute-start(f32[64,512]{1,0:T(8,128)S(1)} %get-tuple-element.26), channel_id=1, source_target_pairs={{0,16},{16,0},{32,48},{48,32},{64,80},{80,64},{96,112},{112,96},{1... | collective-permute-start | bytes 393224 | tf_op jit(solution)/shard_map/ppermute | solution.py:335
  14.7 5.4 %collective-permute-start.2 = (f32[8,512]{1,0:T(8,128)S(1)}, f32[8,512]{1,0:T(8,128)S(1)}, u32[]{:S(2)}, u32[]{:S(2)}) collective-permute-start(f32[8,512]{1,0:T(8,128)S(1)} %get-tuple-element.27), channel_id=1, source_target_pairs={{1,2},{2,1},{3,4},{4,3},{5,6},{6,5},{7,8},{8,7},{9,10},{10,9},{11,... | collective-permute-start | bytes 49160 | tf_op jit(solution)/shard_map/ppermute | solution.py:335
  20.0 1.9 %collective-permute-start.3 = (f32[8,512]{1,0:T(8,128)S(1)}, f32[8,512]{1,0:T(8,128)S(1)}, u32[]{:S(2)}, u32[]{:S(2)}) collective-permute-start(f32[8,512]{1,0:T(8,128)S(1)} %get-tuple-element.28), channel_id=1, source_target_pairs={{0,1},{1,0},{2,3},{3,2},{4,5},{5,4},{6,7},{7,6},{8,9},{9,8},{10,11... | collective-permute-start | bytes 49160 | tf_op jit(solution)/shard_map/ppermute | solution.py:335
  22.0 0.4 %collective-permute-done.2.refs_4_ = f32[8,512]{1,0:T(8,128)S(1)} collective-permute-done((f32[8,512]{1,0:T(8,128)S(1)}, f32[8,512]{1,0:T(8,128)S(1)}, u32[]{:S(2)}, u32[]{:S(2)}) %collective-permute-start.2) | collective-permute-done | bytes 16416 | tf_op jit(solution)/shard_map/ppermute | solution.py:335
  22.4 3.3 %collective-permute-done.3.refs_5_ = f32[8,512]{1,0:T(8,128)S(1)} collective-permute-done((f32[8,512]{1,0:T(8,128)S(1)}, f32[8,512]{1,0:T(8,128)S(1)}, u32[]{:S(2)}, u32[]{:S(2)}) %collective-permute-start.3) | collective-permute-done | bytes 16416 | tf_op jit(solution)/shard_map/ppermute | solution.py:335
  25.7 0.0 collective-permute-done.refs_2_
  25.7 0.0 collective-permute-done.1.refs_3_
  25.7 2.1 %outer.1 = f32[2,64,455]{2,1,0:T(8,128)} custom-call(f32[64,512]{1,0:T(8,128)S(1)} %get-tuple-element.23.low_ref.refs_0_, f32[64,512]{1,0:T(8,128)S(1)} %get-tuple-element.24.high_ref.refs_1_, f32[64,512]{1,0:T(8,128)S(1)} %collective-permute-done.refs_2_, f32[64,512]{1,0:T(8,128)S(1)} %collective-permute-done.1.refs_3_, ...), custom_call_target="tpu_custom_call" | custom-call | tf_op jit(solution)/shard_map/outer/pallas_call | solution.py:312
  (1 shorter events, 0.0 us)
Async XLA Ops:
  4.2 21.4 %collective-permute-start = (f32[64,512]{1,0:T(8,128)S(1)}, f32[64,512]{1,0:T(8,128)S(1)}, u32[]{:S(2)}, u32[]{:S(2)}) collective-permute-start(f32[64,512]{1,0:T(8,128)S(1)} %get-tuple-element.25), channel_id=1, source_target_pairs={{16,32},{32,16},{48,64},{64,48},{80,96},{96,80},{112,128},{128,112... | collective-permute-start | bytes 393224 | tf_op jit(solution)/shard_map/ppermute | solution.py:335
  12.7 12.9 %collective-permute-start.1 = (f32[64,512]{1,0:T(8,128)S(1)}, f32[64,512]{1,0:T(8,128)S(1)}, u32[]{:S(2)}, u32[]{:S(2)}) collective-permute-start(f32[64,512]{1,0:T(8,128)S(1)} %get-tuple-element.26), channel_id=1, source_target_pairs={{0,16},{16,0},{32,48},{48,32},{64,80},{80,64},{96,112},{112,96},{1... | collective-permute-start | bytes 393224 | tf_op jit(solution)/shard_map/ppermute | solution.py:335
  14.7 7.7 %collective-permute-start.2 = (f32[8,512]{1,0:T(8,128)S(1)}, f32[8,512]{1,0:T(8,128)S(1)}, u32[]{:S(2)}, u32[]{:S(2)}) collective-permute-start(f32[8,512]{1,0:T(8,128)S(1)} %get-tuple-element.27), channel_id=1, source_target_pairs={{1,2},{2,1},{3,4},{4,3},{5,6},{6,5},{7,8},{8,7},{9,10},{10,9},{11,... | collective-permute-start | bytes 49160 | tf_op jit(solution)/shard_map/ppermute | solution.py:335
  20.0 5.6 %collective-permute-start.3 = (f32[8,512]{1,0:T(8,128)S(1)}, f32[8,512]{1,0:T(8,128)S(1)}, u32[]{:S(2)}, u32[]{:S(2)}) collective-permute-start(f32[8,512]{1,0:T(8,128)S(1)} %get-tuple-element.28), channel_id=1, source_target_pairs={{0,1},{1,0},{2,3},{3,2},{4,5},{5,4},{6,7},{7,6},{8,9},{9,8},{10,11... | collective-permute-start | bytes 49160 | tf_op jit(solution)/shard_map/ppermute | solution.py:335

commit v10 on v9

--- a/solution.py
+++ b/solution.py
@@ -118,8 +118,8 @@
     low, high, first, last = low_ref[...], high_ref[...], first_ref[...], last_ref[...]
     rows1_ref[...] = jnp.where(odd("wide"), high, low)
     rows2_ref[...] = jnp.where(odd("wide"), low, high)
-    columns1_ref[...] = jnp.where(odd("narrow"), last, first)
-    columns2_ref[...] = jnp.where(odd("narrow"), first, last)
+    columns1_ref[...] = jnp.where(odd("narrow"), first, last)
+    columns2_ref[...] = jnp.where(odd("narrow"), last, first)
 
     @pl.when(early())
     def _():
@@ -266,8 +266,8 @@
     mine = jnp.concatenate([own, strip(own)], axis=0)
     before = jnp.where(odd("wide"), rows2_ref[...], rows1_ref[...])
     behind = jnp.where(odd("wide"), rows1_ref[...], rows2_ref[...])
-    left = jnp.where(odd("narrow"), columns2_ref[...], columns1_ref[...])
-    right = jnp.where(odd("narrow"), columns1_ref[...], columns2_ref[...])
+    left = jnp.where(odd("narrow"), columns1_ref[...], columns2_ref[...])
+    right = jnp.where(odd("narrow"), columns2_ref[...], columns1_ref[...])
     theirs = jnp.concatenate([before, behind, left, right], axis=0)
     lane = lax.broadcasted_iota(jnp.int32, mine.shape, 1)
     d = jnp.where(lane < modes, mine - theirs, 0.0)
@@ -350,8 +350,8 @@
         held(field), held(mean_conductivity), held(kl_fields), turned
     )
     rows1 = swap(rows1, "wide", 1)
-    columns1 = swap(columns1, "narrow", 1)
-    columns2 = swap(columns2, "narrow", 0)
+    columns1 = swap(columns1, "narrow", 0)
+    columns2 = swap(columns2, "narrow", 1)
     rows2 = swap(rows2, "wide", 0)
     parts_then = later(modes, low, high, turned)
     out = outer(modes, low, high, rows1, rows2, columns1, columns2, parts, parts_then)

time: 28.1 us -> 28.4 us (1.011)
  the two profiles are of different devices: /device:TPU:38 before, /device:TPU:30 now
where the time goes in v10:
time: 28.4 us; the launch traced here: 28.1 us
  starting transfers between devices  17.4 us (61%)
  Pallas kernels  6.42 us (23%)
  waiting for transfers between devices  4.27 us (15%)
    ppermute x4, starting transfers between devices, swap(): return lax.ppermute(block, axis, route)  17.4 us
    ppermute x4, waiting for transfers between devices, swap(): return lax.ppermute(block, axis, route)  4.27 us
    pallas_call x1, Pallas kernels, start(): pl.pallas_call(functools.partial(start_kernel, field.shape[-1]), out_shap...  4.24 us
    pallas_call x1, Pallas kernels, outer(): pl.pallas_call(functools.partial(outer_kernel, modes), out_shape=jax.Shap...  2.15 us
  transfers between devices with their start and end apart: 4, of which 1 were waited for; matrix products, arithmetic and copies ran while one was open for 0% of the time, Pallas kernels for 0%

profile of v10, /device:TPU:30, one launch (start us, length us, event | category | flops | bytes accessed | tf_op | source)
XLA Modules:
  0.0 28.1 jit_solution(1654719742482627775)
XLA Ops:
  0.0 4.2 %start.1 = (f32[64,512]{1,0:T(8,128)S(1)}, f32[64,512]{1,0:T(8,128)S(1)}, f32[64,512]{1,0:T(8,128)S(1)}, f32[64,512]{1,0:T(8,128)S(1)}, f32[8,512]{1,0:T(8,128)S...) custom-call(f32[2,64,455]{2,1,0:T(8,128)} %bitcast.3, ...), custom_call_target="tpu_custom_call" | custom-call | tf_op jit(solution)/shard_map/start/pallas_call | solution.py:212
  4.2 9.4 %collective-permute-start = (f32[64,512]{1,0:T(8,128)S(1)}, f32[64,512]{1,0:T(8,128)S(1)}, u32[]{:S(2)}, u32[]{:S(2)}) collective-permute-start(f32[64,512]{1,0:T(8,128)S(1)} %get-tuple-element.25), channel_id=1, source_target_pairs={{16,32},{32,16},{48,64},{64,48},{80,96},{96,80},{112,128},{128,112... | collective-permute-start | bytes 393224 | tf_op jit(solution)/shard_map/ppermute | solution.py:335
  13.6 1.9 %collective-permute-start.1 = (f32[64,512]{1,0:T(8,128)S(1)}, f32[64,512]{1,0:T(8,128)S(1)}, u32[]{:S(2)}, u32[]{:S(2)}) collective-permute-start(f32[64,512]{1,0:T(8,128)S(1)} %get-tuple-element.26), channel_id=1, source_target_pairs={{0,16},{16,0},{32,48},{48,32},{64,80},{80,64},{96,112},{112,96},{1... | collective-permute-start | bytes 393224 | tf_op jit(solution)/shard_map/ppermute | solution.py:335
  15.6 2.7 %collective-permute-start.2 = (f32[8,512]{1,0:T(8,128)S(1)}, f32[8,512]{1,0:T(8,128)S(1)}, u32[]{:S(2)}, u32[]{:S(2)}) collective-permute-start(f32[8,512]{1,0:T(8,128)S(1)} %get-tuple-element.27), channel_id=1, source_target_pairs={{0,1},{1,0},{2,3},{3,2},{4,5},{5,4},{6,7},{7,6},{8,9},{9,8},{10,11... | collective-permute-start | bytes 49160 | tf_op jit(solution)/shard_map/ppermute | solution.py:335
  18.2 3.4 %collective-permute-start.3 = (f32[8,512]{1,0:T(8,128)S(1)}, f32[8,512]{1,0:T(8,128)S(1)}, u32[]{:S(2)}, u32[]{:S(2)}) collective-permute-start(f32[8,512]{1,0:T(8,128)S(1)} %get-tuple-element.28), channel_id=1, source_target_pairs={{1,2},{2,1},{3,4},{4,3},{5,6},{6,5},{7,8},{8,7},{9,10},{10,9},{11,... | collective-permute-start | bytes 49160 | tf_op jit(solution)/shard_map/ppermute | solution.py:335
  21.7 0.0 collective-permute-done.2.refs_4_
  21.7 4.3 %collective-permute-done.3.refs_5_ = f32[8,512]{1,0:T(8,128)S(1)} collective-permute-done((f32[8,512]{1,0:T(8,128)S(1)}, f32[8,512]{1,0:T(8,128)S(1)}, u32[]{:S(2)}, u32[]{:S(2)}) %collective-permute-start.3) | collective-permute-done | bytes 16416 | tf_op jit(solution)/shard_map/ppermute | solution.py:335
  26.0 0.0 collective-permute-done.refs_2_
  26.0 0.0 collective-permute-done.1.refs_3_
  26.0 2.1 %outer.1 = f32[2,64,455]{2,1,0:T(8,128)} custom-call(f32[64,512]{1,0:T(8,128)S(1)} %get-tuple-element.23.low_ref.refs_0_, f32[64,512]{1,0:T(8,128)S(1)} %get-tuple-element.24.high_ref.refs_1_, f32[64,512]{1,0:T(8,128)S(1)} %collective-permute-done.refs_2_, f32[64,512]{1,0:T(8,128)S(1)} %collective-permute-done.1.refs_3_, ...), custom_call_target="tpu_custom_call" | custom-call | tf_op jit(solution)/shard_map/outer/pallas_call | solution.py:312
  (1 shorter events, 0.0 us)
Async XLA Ops:
  4.2 21.7 %collective-permute-start = (f32[64,512]{1,0:T(8,128)S(1)}, f32[64,512]{1,0:T(8,128)S(1)}, u32[]{:S(2)}, u32[]{:S(2)}) collective-permute-start(f32[64,512]{1,0:T(8,128)S(1)} %get-tuple-element.25), channel_id=1, source_target_pairs={{16,32},{32,16},{48,64},{64,48},{80,96},{96,80},{112,128},{128,112... | collective-permute-start | bytes 393224 | tf_op jit(solution)/shard_map/ppermute | solution.py:335
  13.6 12.3 %collective-permute-start.1 = (f32[64,512]{1,0:T(8,128)S(1)}, f32[64,512]{1,0:T(8,128)S(1)}, u32[]{:S(2)}, u32[]{:S(2)}) collective-permute-start(f32[64,512]{1,0:T(8,128)S(1)} %get-tuple-element.26), channel_id=1, source_target_pairs={{0,16},{16,0},{32,48},{48,32},{64,80},{80,64},{96,112},{112,96},{1... | collective-permute-start | bytes 393224 | tf_op jit(solution)/shard_map/ppermute | solution.py:335
  15.6 6.1 %collective-permute-start.2 = (f32[8,512]{1,0:T(8,128)S(1)}, f32[8,512]{1,0:T(8,128)S(1)}, u32[]{:S(2)}, u32[]{:S(2)}) collective-permute-start(f32[8,512]{1,0:T(8,128)S(1)} %get-tuple-element.27), channel_id=1, source_target_pairs={{0,1},{1,0},{2,3},{3,2},{4,5},{5,4},{6,7},{7,6},{8,9},{9,8},{10,11... | collective-permute-start | bytes 49160 | tf_op jit(solution)/shard_map/ppermute | solution.py:335
  18.2 7.7 %collective-permute-start.3 = (f32[8,512]{1,0:T(8,128)S(1)}, f32[8,512]{1,0:T(8,128)S(1)}, u32[]{:S(2)}, u32[]{:S(2)}) collective-permute-start(f32[8,512]{1,0:T(8,128)S(1)} %get-tuple-element.28), channel_id=1, source_target_pairs={{1,2},{2,1},{3,4},{4,3},{5,6},{6,5},{7,8},{8,7},{9,10},{10,9},{11,... | collective-permute-start | bytes 49160 | tf_op jit(solution)/shard_map/ppermute | solution.py:335
